TPU v7x, 128 devices: a whole 4x4x4 slice. The times are simulated.
128 devices in a mesh: dp: 8 (over z_lo, x), tensor: 16 (over z_hi, y, core).
Axes of the slice: x: 4, y: 4, z: 4 (z_hi: 2, z_lo: 2; z = z_hi * 2 + z_lo), core: 2. Of those that a mesh axis runs over, the one named last changes fastest.
Arguments:
- tokens: bfloat16 [2048, 4096], P(('dp', 'tensor')), may hold values from -700 to 700
- gate_up: bfloat16 [4096, 2, 14336], P(None, None, 'tensor'), may hold values from -0.09375 to 0.09375
- down_proj: bfloat16 [14336, 4096], P('tensor'), may hold values from -0.046875 to 0.046875
- norm_gain: float32 [4096], replicated, may hold values from 0.5 to 1.5
- act_history: float32 [1], replicated, may hold values from 3 to 8
- grad_history: float32 [1], replicated, may hold values from 20 to 60
- grad_out: bfloat16 [2048, 4096], P(('dp', 'tensor')), may hold values from -240 to 240
Outputs:
- mlp_out: bfloat16 [2048, 4096], P(('dp', 'tensor'))
- grad_tokens: bfloat16 [2048, 4096], P(('dp', 'tensor'))
- grad_gate_up: bfloat16 [4096, 2, 14336], P('dp', None, 'tensor')
- grad_down: bfloat16 [14336, 4096], P(('tensor', 'dp'))
- grad_gain: float32 [4096], replicated
- peak_act: float32 [1], replicated
- peak_grad: float32 [1], replicated
All inputs are finite; a program needn't handle non-finite values.
Results may differ from a plain program's by a relative error of at most 0.02.
Values may be sent and summed in bfloat16 or wider, within the bound.
No kernel may reach another device: no remote copies, remote signals or barrier semaphores. Data moves between devices by JAX's collectives and lax.ppermute only.
A program may use at most 192 MiB of HBM per device.

v0:
```python
import math

import jax
import jax.numpy as jnp
from jax import lax
from jax.sharding import PartitionSpec as P

PEAK = 448.0
EPSILON = 1e-05
CONTRACT_ROWS = (((0,), (0,)), ((), ()))
CONTRACT_COLS = (((1,), (1,)), ((), ()))


def shards(tokens, gate_up, down_proj, norm_gain, act_history, grad_history, grad_out):
    own_rows = tokens.shape[0]
    features = tokens.shape[1]
    width = down_proj.shape[0]
    groups = lax.axis_size("dp")
    lanes = lax.axis_size("tensor")
    root = 1.0 / math.sqrt(own_rows * groups * lanes)
    act_unit = act_history[0] / PEAK
    grad_unit = grad_history[0] / PEAK
    values = tokens.astype(jnp.float32)
    inverse_rms = lax.rsqrt(jnp.mean(values * values, axis=-1, keepdims=True) + EPSILON)
    unit_rows = values * inverse_rms
    normed = unit_rows * norm_gain
    local_act = jnp.max(jnp.abs(normed))
    local_grad = jnp.max(jnp.abs(grad_out.astype(jnp.float32)))
    quantized = jnp.clip(normed * (PEAK / act_history[0]), -PEAK, PEAK).astype(jnp.bfloat16)
    paired = gate_up.reshape(features, 2 * width)
    peak_act = lax.pmax(local_act, ("dp", "tensor"))
    projected = (
        jnp.dot(
            lax.all_gather(quantized, "tensor", axis=0, tiled=True),
            paired,
            preferred_element_type=jnp.float32,
        )
        * act_unit
    )
    pre_gate = projected[:, :width]
    pre_up = projected[:, width:]
    sigmoid_gate = jax.nn.sigmoid(pre_gate)
    silu_gate = pre_gate * sigmoid_gate
    hidden = (silu_gate * pre_up).astype(jnp.bfloat16)
    block = hidden
    mlp_out = lax.psum_scatter(
        jnp.dot(block, down_proj, preferred_element_type=jnp.float32).astype(jnp.bfloat16),
        "tensor",
        scatter_dimension=0,
        tiled=True,
    )
    grad_quant = jnp.clip(
        grad_out.astype(jnp.float32) * (PEAK / grad_history[0]), -PEAK, PEAK
    ).astype(jnp.bfloat16)
    peak_grad = lax.pmax(local_grad, ("dp", "tensor"))
    grad_rows = lax.all_gather(grad_quant, "tensor", axis=0, tiled=True)
    d_hidden = (
        lax.dot_general(grad_rows, down_proj, CONTRACT_COLS, preferred_element_type=jnp.float32)
        * grad_unit
    )
    d_gate = (d_hidden * pre_up * sigmoid_gate * (1.0 + pre_gate * (1.0 - sigmoid_gate))).astype(
        jnp.bfloat16
    )
    d_up = (d_hidden * silu_gate).astype(jnp.bfloat16)
    d_pair = jnp.concatenate([d_gate, d_up], axis=1)
    block = d_pair
    d_normed = lax.psum_scatter(
        lax.dot_general(block, paired, CONTRACT_COLS, preferred_element_type=jnp.float32).astype(
            jnp.bfloat16
        ),
        "tensor",
        scatter_dimension=0,
        tiled=True,
    ).astype(jnp.float32)
    grad_gain = lax.psum(jnp.sum(d_normed * unit_rows, axis=0), ("dp", "tensor")) * root
    scaled = d_normed * norm_gain
    grad_tokens = (
        inverse_rms * (scaled - unit_rows * jnp.mean(scaled * unit_rows, axis=-1, keepdims=True))
    ).astype(jnp.bfloat16)
    gathered = lax.all_gather(quantized, "tensor", axis=0, tiled=True)
    pair_scale = act_unit * root
    down_scale = grad_unit * root
    block = gathered
    product = lax.dot_general(block, d_pair, CONTRACT_ROWS, preferred_element_type=jnp.float32)
    grad_gate_up = lax.psum_scatter(
        (product * pair_scale)
        .reshape(features // groups * lax.axis_size("dp"), 2, width)
        .astype(jnp.bfloat16),
        "dp",
        scatter_dimension=0,
        tiled=True,
    )
    block = hidden
    grad_down = lax.psum_scatter(
        (
            lax.dot_general(block, grad_rows, CONTRACT_ROWS, preferred_element_type=jnp.float32)
            * down_scale
        ).astype(jnp.bfloat16),
        "dp",
        scatter_dimension=0,
        tiled=True,
    )
    return (
        mlp_out,
        grad_tokens,
        grad_gate_up,
        grad_down,
        grad_gain,
        peak_act.reshape(1),
        peak_grad.reshape(1),
    )


def solution(mesh):
    placed = (
        P(("dp", "tensor"), None),
        P(None, None, "tensor"),
        P("tensor", None),
        P(),
        P(),
        P(),
        P(("dp", "tensor"), None),
    )
    return jax.shard_map(
        shards,
        mesh=mesh,
        in_specs=placed,
        out_specs=(
            P(("dp", "tensor"), None),
            P(("dp", "tensor"), None),
            P("dp", None, "tensor"),
            P(("tensor", "dp"), None),
            P(),
            P(),
            P(),
        ),
        check_vma=False,
    )
```

profile of v0, /device:TPU:0, one launch (start us, length us, event | category | flops | bytes accessed | tf_op | source)
XLA Modules:
  0.0 676.1 jit_solution(15344182487565273550)
XLA Ops:
  7.2 0.0 all-gather.3.cloned.1.call-start
  7.9 1.1 fusion.13
  9.0 1.7 fusion.8
  10.7 0.0 all-gather.3.cloned.1.call-update
  10.7 0.0 all-gather.5.cloned.1.call-start
  11.4 2.2 fusion.16
  13.6 0.0 all-gather.5.cloned.1.call-update
  13.6 0.0 reduce-scatter.6.cloned.1.call-start
  13.7 16.0 %copy.16 = bf16[512,8,2,896]{3,1,2,0:T(8,128)(2,1)} copy(bf16[512,8,2,896]{3,2,1,0:T(2,128)(2,1)} %bitcast.22) | data formatting | bytes 29360128
  29.7 32.3 %all-gather.3.cloned.1.call-done = bf16[256,4096]{1,0:T(8,128)(2,1)} async-done(((bf16[16,4096]{1,0:T(8,128)(2,1)}), bf16[256,4096]{1,0:T(8,128)(2,1)}) %all-gather.3.cloned.1.call-update) | async-done | bytes 2097168 | tf_op jit(solution)/shard_map/all_gather | solution.py:34
  62.0 11.0 %convolution_multiply_fusion = f32[256,1792]{1,0:T(8,128)} fusion(bf16[256,4096]{1,0:T(8,128)(2,1)} %all-gather.3.cloned.1.call-done, bf16[4096,1792]{1,0:T(8,128)(2,1)} %bitcast.23, f32[]{:T(128)} %bitcast.1), kind=kOutput, calls=%fused_computation.4 | convolution fusion | flops 3758555136 | bytes 18612228 | tf_op jit(solution)/shard_map/dot_general | solution.py:33
  73.0 39.2 %all-gather.5.cloned.1.call-done = bf16[256,4096]{1,0:T(8,128)(2,1)} async-done(((bf16[16,4096]{1,0:T(8,128)(2,1)}), bf16[256,4096]{1,0:T(8,128)(2,1)}) %all-gather.5.cloned.1.call-update) | async-done | bytes 2097168 | tf_op jit(solution)/shard_map/all_gather | solution.py:56
  112.1 6.8 %multiply_convert_fusion.3 = (bf16[256,896]{1,0:T(8,128)(2,1)S(1)}, bf16[256,896]{1,0:T(8,128)(2,1)S(1)}, bf16[256,896]{1,0:T(8,128)(2,1)S(1)}) fusion(f32[256,1792]{1,0:T(8,128)} %convolution_multiply_fusion, f32[]{:T(128)} %bitcast.3, bf16[256,4096]{1,0:T(8,128)(2,1)} %all-gather.5.cloned.1.call-done, bf16[896,4096]{1,0:T(8,128)(2,1)} %param.9), kind=kOutput, calls=%fused_computation.8 | convolution fusion | flops 1882718208 | bytes 12648452 | tf_op jit(solution)/shard_map/dot_general | solution.py:58
  119.0 0.0 copy-start.5
  119.0 0.8 copy-done.5
  119.8 15.8 %convolution_convert_fusion = bf16[256,4096]{1,0:T(8,128)(2,1)} fusion(bf16[4096,1792]{1,0:T(8,128)(2,1)} %bitcast.24, bf16[256,896]{1,0:T(8,128)(2,1)S(1)} %get-tuple-element.13, bf16[256,896]{1,0:T(8,128)(2,1)S(1)} %get-tuple-element.12), kind=kOutput, calls=%fused_computation.2 | convolution fusion | flops 3760979968 | bytes 17694720 | tf_op jit(solution)/shard_map/dot_general | solution.py:68
  135.6 0.0 copy-start.3
  135.6 0.0 reduce-scatter.6.cloned.1.call-update
  135.6 0.0 all-reduce.4.cloned.1.call-start
  135.6 1.5 copy-done.3
  137.1 8.5 %multiply_convert_fusion = bf16[4096,1792]{0,1:T(8,128)(2,1)} fusion(bf16[256,4096]{1,0:T(8,128)(2,1)S(1)} %copy-done.3, f32[]{:T(128)} %bitcast.4, bf16[256,896]{1,0:T(8,128)(2,1)} %copy-done.5, bf16[256,896]{1,0:T(8,128)(2,1)S(1)} %get-tuple-element.12), kind=kOutput, calls=%fused_computation | convolution fusion | flops 3774611456 | bytes 17694724 | tf_op jit(solution)/shard_map/dot_general | solution.py:84
  145.7 36.7 %copy.15 = bf16[4096,2,896]{2,1,0:T(2,128)(2,1)} copy(bf16[4096,2,896]{0,2,1:T(8,128)(2,1)} %bitcast.25) | data formatting | bytes 29360128 | tf_op jit(solution)/shard_map/convert_element_type | solution.py:88
  182.4 0.0 all-reduce.4.cloned.1.call-update
  182.4 0.2 reduce-scatter.4.cloned.1.call-start
  182.6 6.9 %convolution_convert_fusion.1 = bf16[256,4096]{1,0:T(8,128)(2,1)} fusion(bf16[256,896]{1,0:T(8,128)(2,1)S(1)} %get-tuple-element.14, bf16[896,4096]{1,0:T(8,128)(2,1)} %param.9), kind=kOutput, calls=%fused_computation.3 | convolution fusion | flops 1880096768 | bytes 9895936 | tf_op jit(solution)/shard_map/dot_general | solution.py:47
  189.5 0.0 copy-start.2
  189.5 0.0 reduce-scatter.4.cloned.1.call-update
  189.5 0.0 reduce-scatter.8.cloned.1.call-start
  189.6 1.5 copy-done.2
  191.1 5.1 multiply_convert_fusion.1
  196.2 0.0 copy-start.4
  196.2 0.0 copy-start
  196.2 0.0 copy-start.1
  196.2 0.0 reduce-scatter.8.cloned.1.call-update
  196.2 0.6 copy-done.4
  196.8 0.6 dynamic-slice
  198.1 7.2 %reduce-scatter.6.cloned.1.call-done = bf16[16,4096]{1,0:T(8,128)(2,1)} async-done(((bf16[256,4096]{1,0:T(8,128)(2,1)}), bf16[16,4096]{1,0:T(8,128)(2,1)}) %reduce-scatter.6.cloned.1.call-update) | async-done | bytes 131088 | tf_op jit(solution)/shard_map/reduce_scatter | solution.py:67
  205.3 0.0 copy-done
  205.3 0.0 copy-done.1
  205.3 1.7 fusion.17
  206.9 325.9 %all-reduce.1 = (f32[1]{0:T(128)}, f32[1]{0:T(128)}) all-reduce(f32[1]{0:T(128)} %bitcast.7, f32[1]{0:T(128)} %bitcast.8), channel_id=1, replica_groups=mesh['dp'=8,'tensor'=16] {'dp','tensor'}, use_global_device_ids=true, to_apply=%region_9.10 | all-reduce | flops 2 | bytes 16 | tf_op jit(solution)/shard_map/pmax | solution.py:31
  532.9 69.1 %psum.7 = f32[4096]{0:T(1024)S(1)} all-reduce(f32[4096]{0:T(1024)S(1)} %get-tuple-element.7), channel_id=1, replica_groups=mesh['dp'=8,'tensor'=16] {'dp','tensor'}, use_global_device_ids=true, to_apply=%region_7.8 | all-reduce | flops 4096 | bytes 32768 | tf_op jit(solution)/shard_map/psum | solution.py:75
  602.0 0.6 broadcast_multiply_fusion
  602.6 1.7 fusion.11
  604.3 0.0 all-reduce.4.cloned.1.call-done
  604.3 4.0 constant_dynamic-slice_fusion
  608.3 0.0 reduce-scatter.4.cloned.1.call-done
  608.3 60.9 %reduce-scatter.8.cloned.1.call-done = bf16[112,4096]{1,0:T(8,128)(2,1)} async-done(((bf16[896,4096]{1,0:T(8,128)(2,1)}), bf16[112,4096]{1,0:T(8,128)(2,1)}) %reduce-scatter.8.cloned.1.call-update) | async-done | bytes 917520 | tf_op jit(solution)/shard_map/reduce_scatter | solution.py:94
  (2 shorter events, 0.0 us)
Async XLA Ops:
  7.2 54.8 %all-gather.3.cloned.1.call-start = ((), (), s32[]{:S(2)}) async-start(), calls=%async_computation.3 | async-start | bytes 2228224 | tf_op jit(solution)/shard_map/all_gather | solution.py:34
  10.7 101.5 %all-gather.5.cloned.1.call-start = ((), (), s32[]{:S(2)}) async-start(), calls=%async_computation.5 | async-start | bytes 2228224 | tf_op jit(solution)/shard_map/all_gather | solution.py:56
  13.6 191.6 %reduce-scatter.6.cloned.1.call-start = ((), (), s32[]{:S(2)}) async-start(), calls=%async_computation.6 | async-start | bytes 2228224 | tf_op jit(solution)/shard_map/reduce_scatter | solution.py:67
  119.0 0.8 copy-start.5
  135.6 1.6 copy-start.3
  135.6 468.7 %all-reduce.4.cloned.1.call-start = ((), (), s32[]{:S(2)}) async-start(), calls=%async_computation.8 | async-start | bytes 29360128
  182.4 425.9 %reduce-scatter.4.cloned.1.call-start = ((), (), s32[]{:S(2)}) async-start(), calls=%async_computation.4 | async-start | bytes 2228224 | tf_op jit(solution)/shard_map/reduce_scatter | solution.py:46
  189.5 1.6 copy-start.2
  189.5 479.7 %reduce-scatter.8.cloned.1.call-start = ((), (), s32[]{:S(2)}) async-start(), calls=%async_computation.7 | async-start | bytes 8257536 | tf_op jit(solution)/shard_map/reduce_scatter | solution.py:94
  196.2 0.7 copy-start.4
  196.2 9.1 %copy-start = (bf16[16,4096]{1,0:T(8,128)(2,1)S(1)}, bf16[16,4096]{1,0:T(8,128)(2,1)}, u32[]{:S(2)}) copy-start(bf16[16,4096]{1,0:T(8,128)(2,1)} %param.7) | copy-start | bytes 393220
  196.2 9.1 %copy-start.1 = (f32[4096]{0:T(1024)S(1)}, f32[4096]{0:T(1024)}, u32[]{:S(2)}) copy-start(f32[4096]{0:T(1024)} %param.10) | copy-start | bytes 49156
Sparse Core Ops, SparseCore 0:
  11.0 50.9 all-gather.2
  65.0 47.0 all-gather.4
  135.7 69.5 reduce-scatter.5
  207.6 302.4 all-reduce.3
  514.5 69.8 reduce-scatter.3
  587.2 81.9 reduce-scatter.7
where the time goes:
time: 681 us; the launch traced here: 676 us
  blocking collectives  395 us (58%)
  waiting for transfers between devices  140 us (21%)
  local copies, waits for them, and re-layouts  61.7 us (9%)
  matrix products  54.1 us (8%)
  between operations  16.2 us (2%)
  other arithmetic  8.9 us (1%)
    pmax x1, blocking collectives, shards(): peak_act = lax.pmax(local_act, ('dp', 'tensor'))  326 us
    psum x1, blocking collectives, shards(): lax.psum(jnp.sum(d_normed * unit_rows, axis=0), ('dp', 'tensor')) * root  69.1 us
    reduce_scatter x1, waiting for transfers between devices, shards(): lax.psum_scatter((lax.dot_general(block, grad_rows, CONTRACT_ROWS, prefer...  60.9 us
    all_gather x1, waiting for transfers between devices, shards(): grad_rows = lax.all_gather(grad_quant, 'tensor', axis=0, tiled=True)  39.2 us
    convert_element_type x1, local copies, waits for them, and re-layouts, shards(): grad_gate_up = lax.psum_scatter((product * pair_scale).reshape(features /...  36.7 us
    all_gather x1, waiting for transfers between devices, shards(): lax.all_gather(quantized, 'tensor', axis=0, tiled=True)  32.3 us
    unnamed x15, local copies, waits for them, and re-layouts  25 us
    dot_general x1, matrix products, shards(): lax.dot_general(block, paired, CONTRACT_COLS, preferred_element_type=jnp....  15.8 us
  transfers between devices with their start and end apart: 6, of which 4 were waited for; matrix products, arithmetic and copies ran while one was open for 14% of the time, Pallas kernels for 0%

commit v1 on v0

v1 whole, which is shorter than its diff:
```python
import math

import jax
import jax.numpy as jnp
from jax import lax
from jax.sharding import PartitionSpec as P

PEAK = 448.0
EPSILON = 1e-05
ROWS = (((0,), (0,)), ((), ()))
COLS = (((1,), (1,)), ((), ()))
F32 = jnp.float32
BF16 = jnp.bfloat16

RINGS = [[2 * k + core for k in range(8)] for core in range(2)]
CORE = [(i, i ^ 1) for i in range(16)]
ZPAIR = [(i, i ^ 4) for i in range(8)]


def along_x(step):
    return [(z * 4 + x, z * 4 + (x + step) % 4) for z in range(2) for x in range(4)]


def send_x(block, step):
    return lax.ppermute(block, "dp", along_x(step))


def exchange(parts):
    return lax.all_to_all(parts, "tensor", 0, 0, tiled=True, axis_index_groups=RINGS)


def gather_tensor(block):
    own = exchange(jnp.broadcast_to(block[None], (8,) + block.shape))
    other = lax.ppermute(own, "tensor", CORE)
    return own, other


def gather_x(piece):
    left = send_x(piece, 1)
    right = send_x(piece, -1)
    half = piece.shape[0] // 2
    far_top = send_x(left[:half], 1)
    far_low = send_x(right[half:], -1)
    return jnp.concatenate([piece, left, right, far_top, far_low], axis=0)


def quantize(values, unit):
    return jnp.clip(values * unit, -PEAK, PEAK).astype(BF16)


def shards(tokens, gate_up, down_proj, norm_gain, act_history, grad_history, grad_out):
    own_rows, features = tokens.shape
    width = down_proj.shape[0]
    groups = lax.axis_size("dp")
    lanes = lax.axis_size("tensor")
    root = 1.0 / math.sqrt(own_rows * groups * lanes)
    act_unit = act_history[0] / PEAK
    grad_unit = grad_history[0] / PEAK
    dp = lax.axis_index("dp")
    z_lo = dp // 4
    x = dp % 4
    span = features // 8
    half_rows = own_rows * 8

    tokens_own, tokens_other = gather_tensor(tokens)
    grads_own, grads_other = gather_tensor(grad_out)

    values = tokens.astype(F32)
    inverse_rms = lax.rsqrt(jnp.mean(values * values, axis=-1, keepdims=True) + EPSILON)
    unit_rows = values * inverse_rms
    q_mine = quantize(unit_rows * norm_gain, PEAK / act_history[0])
    g_mine = quantize(grad_out.astype(F32), PEAK / grad_history[0])

    def slices(step):
        to = (x + step) % 4

        def cut(rows, z):
            return lax.dynamic_slice(rows, (0, (z * 4 + to) * span), (own_rows, span))

        q_part = jnp.concatenate([cut(q_mine, z_lo), cut(q_mine, 1 - z_lo)], axis=1)
        g_part = jnp.concatenate([cut(g_mine, 0), cut(g_mine, 1)], axis=1)
        return jnp.stack([q_part, g_part])

    sliced = jnp.stack(
        [slices(0), send_x(slices(1), 1), send_x(slices(-1), -1), send_x(slices(2), 2)]
    )
    slices_own, slices_other = gather_tensor(sliced.reshape(4 * 2 * own_rows, 2 * span))

    def lay(k):
        both = jnp.stack([slices_own, slices_other]).reshape(2, 8, 4, 2, own_rows, 2 * span)
        return both[:, :, :, k].transpose(2, 0, 1, 3, 4).reshape(4 * 2 * half_rows, 2 * span)

    q_slice = lay(0)
    g_slice = lay(1)

    rows = jnp.concatenate(
        [tokens_own.reshape(half_rows, features), tokens_other.reshape(half_rows, features)]
    ).astype(F32)
    unit_all = rows * lax.rsqrt(jnp.mean(rows * rows, axis=-1, keepdims=True) + EPSILON)
    normed = unit_all * norm_gain
    local_act = jnp.max(jnp.abs(normed))
    quantized = quantize(normed, PEAK / act_history[0])
    paired = gate_up.reshape(features, 2 * width)
    projected = jnp.dot(quantized, paired, preferred_element_type=F32) * act_unit
    pre_gate = projected[:, :width]
    pre_up = projected[:, width:]
    sigmoid_gate = jax.nn.sigmoid(pre_gate)
    silu_gate = pre_gate * sigmoid_gate
    hidden = (silu_gate * pre_up).astype(BF16)
    hidden_all = gather_x(hidden)

    out_rows = jnp.concatenate(
        [grads_own.reshape(half_rows, features), grads_other.reshape(half_rows, features)]
    ).astype(F32)
    local_grad = jnp.max(jnp.abs(out_rows))
    grad_rows = quantize(out_rows, PEAK / grad_history[0])
    d_hidden = lax.dot_general(grad_rows, down_proj, COLS, preferred_element_type=F32) * grad_unit
    d_gate = (d_hidden * pre_up * sigmoid_gate * (1.0 + pre_gate * (1.0 - sigmoid_gate))).astype(
        BF16
    )
    d_up = (d_hidden * silu_gate).astype(BF16)
    d_pair = jnp.concatenate([d_gate, d_up], axis=1)
    pair_all = gather_x(d_pair)

    share_out = jnp.dot(hidden, down_proj, preferred_element_type=F32).astype(BF16)
    share_normed = lax.dot_general(d_pair, paired, COLS, preferred_element_type=F32)
    gain_share = jnp.sum(share_normed * unit_all, axis=0).reshape(1, features)
    share_normed = share_normed.astype(BF16)

    def pair_sum(share):
        got = lax.ppermute(share[half_rows:], "tensor", CORE)
        total = share[:half_rows].astype(F32) + got.astype(F32)
        return total.astype(BF16).reshape(8, own_rows, features)

    gain_share = gain_share + lax.ppermute(gain_share, "tensor", CORE)
    gain_high = lax.reduce_precision(gain_share, 8, 7)
    gain_rows = jnp.concatenate([gain_high, gain_share - gain_high]).astype(BF16)
    parts = jnp.concatenate(
        [
            pair_sum(share_out),
            pair_sum(share_normed),
            jnp.broadcast_to(gain_rows[None], (8, 2, features)),
        ],
        axis=1,
    )
    totals = jnp.sum(exchange(parts).astype(F32), axis=0)
    mlp_out = totals[:own_rows].astype(BF16)
    d_normed = totals[own_rows : 2 * own_rows]
    gain_sum = totals[2 * own_rows] + totals[2 * own_rows + 1]

    peaks = jnp.concatenate([jnp.full((64,), local_act), jnp.full((64,), local_grad)])
    small = jnp.concatenate([gain_sum.reshape(-1, 128), peaks.reshape(1, 128)])
    small = lax.all_to_all(
        jnp.broadcast_to(small[None], (groups,) + small.shape), "dp", 0, 0, tiled=True
    )
    grad_gain = jnp.sum(small[:, :-1], axis=0).reshape(features) * root
    peak = jnp.max(small[:, -1], axis=0)

    scaled = d_normed * norm_gain
    grad_tokens = (
        inverse_rms * (scaled - unit_rows * jnp.mean(scaled * unit_rows, axis=-1, keepdims=True))
    ).astype(BF16)

    pair_scale = act_unit * root
    down_scale = grad_unit * root
    down_part = (
        lax.dot_general(hidden_all, g_slice, ROWS, preferred_element_type=F32) * down_scale
    ).astype(BF16)
    hand = width // 2
    sent_down = lax.dynamic_slice(down_part, ((1 - z_lo) * hand, 0), (hand, 2 * span))
    kept_down = lax.dynamic_slice(down_part, (z_lo * hand, 0), (hand, 2 * span))
    got_down = lax.ppermute(sent_down, "dp", ZPAIR)
    sum_down = (kept_down.astype(F32) + got_down.astype(F32)).astype(BF16)
    turned = lax.all_to_all(
        sum_down.reshape(4, hand // 4, 2 * span),
        "dp",
        0,
        0,
        tiled=True,
        axis_index_groups=[[0, 1, 2, 3], [4, 5, 6, 7]],
    )
    grad_down = (
        turned.reshape(4, hand // 4, 2, span).transpose(1, 2, 0, 3).reshape(hand // 4, features)
    )

    def pair_grad(part):
        sent = (
            lax.dot_general(q_slice[:, span:], part, ROWS, preferred_element_type=F32) * pair_scale
        ).astype(BF16)
        got = lax.ppermute(sent, "dp", ZPAIR)
        kept = (
            lax.dot_general(q_slice[:, :span], part, ROWS, preferred_element_type=F32) * pair_scale
        )
        return (kept + got.astype(F32)).astype(BF16)

    grad_gate_up = jnp.stack(
        [pair_grad(pair_all[:, :width]), pair_grad(pair_all[:, width:])], axis=1
    )
    return (
        mlp_out,
        grad_tokens,
        grad_gate_up,
        grad_down,
        grad_gain,
        peak[0].reshape(1),
        peak[64].reshape(1),
    )


def solution(mesh):
    placed = (
        P(("dp", "tensor"), None),
        P(None, None, "tensor"),
        P("tensor", None),
        P(),
        P(),
        P(),
        P(("dp", "tensor"), None),
    )
    return jax.shard_map(
        shards,
        mesh=mesh,
        in_specs=placed,
        out_specs=(
            P(("dp", "tensor"), None),
            P(("dp", "tensor"), None),
            P("dp", None, "tensor"),
            P(("tensor", "dp"), None),
            P(),
            P(),
            P(),
        ),
        check_vma=False,
    )
```

time: 681 us -> 292 us (0.43)
  blocking collectives: 395 us -> 24.9 us
  starting transfers between devices: 0.43 us -> 48.5 us
  waiting for transfers between devices: 140 us -> 101 us
  between operations: 16.2 us -> 2.43 us
  local copies, waits for them, and re-layouts: 61.7 us -> 50.3 us
  other arithmetic: 8.9 us -> 18.7 us
  matrix products: 54.1 us -> 44.7 us
    pmax x1 -> x0, blocking collectives: 326 us -> none  [shards(): peak_act = lax.pmax(local_act, ('dp', 'tensor'))]
    all_gather x2 -> x0, waiting for transfers between devices: 71.5 us -> none  [the longest x1 39.2 us: shards(): grad_rows = lax.all_gather(grad_quant, 'tensor', axis=0, tiled=True)]
    psum x1 -> x0, blocking collectives: 69.1 us -> none  [shards(): lax.psum(jnp.sum(d_normed * unit_rows, axis=0), ('dp', 'tensor')) * root]
    reduce_scatter x3 -> x0, waiting for transfers between devices: 68.1 us -> none  [the longest x1 60.9 us: shards(): lax.psum_scatter((lax.dot_general(block, grad_rows, CONTRACT_ROWS, prefer...]
    ppermute x0 -> x20, waiting for transfers between devices: none -> 62.4 us  [the longest x2 31.1 us: pair_grad(): got = lax.ppermute(sent, 'dp', ZPAIR)]
    all_to_all x0 -> x5, waiting for transfers between devices: none -> 38.9 us  [the longest x3 34.9 us: exchange(): lax.all_to_all(parts, 'tensor', 0, 0, tiled=True, axis_index_groups=RINGS)]
    convert_element_type x1 -> x0, local copies, waits for them, and re-layouts: 36.7 us -> none  [shards(): grad_gate_up = lax.psum_scatter((product * pair_scale).reshape(features /...]
    all_to_all x0 -> x5, starting transfers between devices: none -> 28.1 us  [the longest x3 20.7 us: exchange(): lax.all_to_all(parts, 'tensor', 0, 0, tiled=True, axis_index_groups=RINGS)]
  transfers between devices with their start and end apart: 6 -> 25, of which waited for: 4 -> 12; matrix products, arithmetic and copies ran while one was open for 14% -> 29% of each run, Pallas kernels for 0% -> 0%
where the time goes in v1:
time: 292 us; the launch traced here: 291 us
  waiting for transfers between devices  101 us (35%)
  local copies, waits for them, and re-layouts  50.3 us (17%)
  starting transfers between devices  48.5 us (17%)
  matrix products  44.7 us (15%)
  blocking collectives  24.9 us (9%)
  other arithmetic  18.7 us (6%)
    all_to_all x3, waiting for transfers between devices, exchange(): lax.all_to_all(parts, 'tensor', 0, 0, tiled=True, axis_index_groups=RINGS)  34.9 us
    unnamed x32, local copies, waits for them, and re-layouts  31.7 us
    ppermute x2, waiting for transfers between devices, pair_grad(): got = lax.ppermute(sent, 'dp', ZPAIR)  31.1 us
    all_to_all x1, blocking collectives, exchange(): lax.all_to_all(parts, 'tensor', 0, 0, tiled=True, axis_index_groups=RINGS)  24.9 us
    ppermute x11, waiting for transfers between devices, send_x(): return lax.ppermute(block, 'dp', along_x(step))  23 us
    all_to_all x3, starting transfers between devices, exchange(): lax.all_to_all(parts, 'tensor', 0, 0, tiled=True, axis_index_groups=RINGS)  20.7 us
    ppermute x11, starting transfers between devices, send_x(): return lax.ppermute(block, 'dp', along_x(step))  16.8 us
    dot_general x1, matrix products, shards(): lax.dot_general(d_pair, paired, COLS, preferred_element_type=F32)  10.4 us
  transfers between devices with their start and end apart: 25, of which 12 were waited for; matrix products, arithmetic and copies ran while one was open for 29% of the time, Pallas kernels for 0%

profile of v1, /device:TPU:0, one launch (start us, length us, event | category | flops | bytes accessed | tf_op | source)
XLA Modules:
  0.0 290.8 jit_solution(1385129892013082547)
XLA Ops:
  1.7 24.9 %all_to_all.30 = bf16[8,16,4096]{2,1,0:T(8,128)(2,1)S(1)} all-to-all(bf16[8,16,4096]{2,1,0:T(8,128)(2,1)S(1)} %broadcast_in_dim.14), channel_id=1, replica_groups={{0,2,4,6,8,10,12,14},{1,3,5,7,9,11,13,15},{16,18,20,22,24,26,28,30},{17..., dimensions={0} | all-to-all | bytes 2097152 | tf_op jit(solution)/shard_map/all_to_all | solution.py:29
  27.6 3.6 %all-to-all-start.1 = ((bf16[8,16,4096]{2,1,0:T(8,128)(2,1)}), bf16[8,16,4096]{2,1,0:T(8,128)(2,1)S(1)}, u32[]{:S(2)}, u32[]{:S(2)}) async-start(bf16[8,16,4096]{2,1,0:T(8,128)(2,1)} %broadcast_in_dim.15), calls=%async_computation.1 | async-start | bytes 2097152 | tf_op jit(solution)/shard_map/all_to_all | solution.py:29
  32.6 16.0 %copy.32 = bf16[512,8,2,896]{3,1,2,0:T(8,128)(2,1)} copy(bf16[512,8,2,896]{3,2,1,0:T(2,128)(2,1)} %bitcast.70) | data formatting | bytes 29360128
  49.9 9.0 %convolution_multiply_fusion = f32[256,1792]{1,0:T(8,128)S(1)} fusion(bf16[4096,1792]{1,0:T(8,128)(2,1)} %bitcast.71, f32[]{:T(128)} %bitcast.2, f32[4096]{0:T(1024)S(1)} %copy-done.9, f32[256]{0:T(256)S(1)} %add_rsqrt_fusion, f32[]{:T(128)} %bitcast.3, bf16[128,4096]{1,0:T(8,128)(2,1)S(1)} %bitcast.91, bf16[128,4096]{1,0:T(8,128)(2,1)S(1)} %bitcast.79), kind=kOutput, calls=%fused_computation.21 | convolution fusion | flops 3767992320 | bytes 18629640 | tf_op jit(solution)/shard_map/dot_general | solution.py:104
  60.1 3.5 %multiply_convert_fusion.4 = (bf16[256,896]{1,0:T(8,128)(2,1)}, bf16[256,896]{1,0:T(8,128)(2,1)}) fusion(f32[256,1792]{1,0:T(8,128)S(1)} %convolution_multiply_fusion, f32[]{:T(128)} %bitcast.8, bf16[896,4096]{1,0:T(8,128)(2,1)S(1)} %bitcast.101, f32[]{:T(128)} %bitcast.7, bf16[128,4096]{1,0:T(8,128)(2,1)S(1)} %bitcast.87, bf16[128,4096]{1,0:T(8,128)(2,1)S(1)} %bitcast.76), kind=kOutput, calls=%fused_computation.64 | convolution fusion | flops 1889599488 | bytes 12189704 | tf_op jit(solution)/shard_map/dot_general | solution.py:117
  63.6 10.4 %fusion.6 = (f32[]{:T(128)}, f32[4096]{0:T(1024)S(1)}, bf16[256,4096]{1,0:T(8,128)(2,1)S(1)}) fusion(f32[4096]{0:T(1024)S(1)} %copy-done.9, f32[256]{0:T(256)S(1)} %add_rsqrt_fusion, bf16[128,4096]{1,0:T(8,128)(2,1)} %bitcast.92, bf16[128,4096]{1,0:T(8,128)(2,1)S(1)} %bitcast.80, bf16[4096,1792]{1,0:T(8,128)(2,1)} %bitcast.72, ...), kind=kOutput, calls=%fused_computation.12 | convolution fusion | flops 3771461632 | bytes 19825668 | tf_op jit(solution)/shard_map/dot_general | solution.py:126
  75.0 5.4 %convolution_convert_fusion = bf16[256,4096]{1,0:T(8,128)(2,1)S(1)} fusion(bf16[256,896]{1,0:T(8,128)(2,1)S(1)} %copy-done.7, bf16[896,4096]{1,0:T(8,128)(2,1)} %param.9), kind=kOutput, calls=%fused_computation.5 | convolution fusion | flops 1880096768 | bytes 9895936 | tf_op jit(solution)/shard_map/dot_general | solution.py:125
  81.0 2.2 collective-permute-done.1
  83.6 1.8 pad_maximum_fusion
  85.4 6.5 %all-to-all-start.2 = ((bf16[8,34,4096]{2,1,0:T(8,128)(2,1)}), bf16[8,34,4096]{2,1,0:T(8,128)(2,1)S(1)}, u32[]{:S(2)}, u32[]{:S(2)}) async-start(bf16[8,34,4096]{2,1,0:T(8,128)(2,1)} %pad_maximum_fusion), calls=%async_computation.2 | async-start | bytes 5242880 | tf_op jit(solution)/shard_map/all_to_all | solution.py:29
  92.1 34.2 %all-to-all-done.2 = bf16[8,34,4096]{2,1,0:T(8,128)(2,1)S(1)} async-done(((bf16[8,34,4096]{2,1,0:T(8,128)(2,1)}), bf16[8,34,4096]{2,1,0:T(8,128)(2,1)S(1)}, u32[]{:S(2)}, u32[]{:S(2)}) %all-to-all-start.2) | async-done | bytes 2228256 | tf_op jit(solution)/shard_map/all_to_all | solution.py:29
  128.5 1.6 collective-permute-start.5
  130.1 1.8 collective-permute-start.6
  131.9 1.9 collective-permute-start.7
  134.8 3.0 %collective-permute-done.7 = bf16[2,16,1024]{2,1,0:T(8,128)(2,1)S(1)} collective-permute-done((bf16[2,16,1024]{2,1,0:T(8,128)(2,1)S(1)}, bf16[2,16,1024]{2,1,0:T(8,128)(2,1)S(1)}, u32[]{:S(2)}, u32[]{:S(2)}) %collective-permute-start.7) | collective-permute-done | bytes 65568 | tf_op jit(solution)/shard_map/ppermute | solution.py:25
  137.8 1.6 broadcast_in_dim.18
  139.4 10.6 %all-to-all-start.3 = ((bf16[8,128,1024]{2,1,0:T(8,128)(2,1)}), bf16[8,128,1024]{2,1,0:T(8,128)(2,1)S(1)}, u32[]{:S(2)}, u32[]{:S(2)}) async-start(bf16[8,128,1024]{2,1,0:T(8,128)(2,1)} %broadcast_in_dim.18), calls=%async_computation.3 | async-start | bytes 4194304 | tf_op jit(solution)/shard_map/all_to_all | solution.py:29
  150.0 1.6 collective-permute-start.16
  152.1 2.5 pad_maximum_fusion.6
  155.0 2.8 collective-permute-start.10
  157.9 2.1 fusion.11
  161.3 2.6 collective-permute-done.16
  164.8 2.8 collective-permute-start.18
  168.7 1.8 constant_dynamic-update-slice_fusion.8
  170.5 1.8 constant_dynamic-update-slice_fusion.7
  172.3 14.9 %collective-permute-done.17 = bf16[128,896]{1,0:T(8,128)(2,1)S(1)} collective-permute-done((bf16[128,896]{1,0:T(8,128)(2,1)S(1)}, bf16[128,896]{1,0:T(8,128)(2,1)S(1)}, u32[]{:S(2)}, u32[]{:S(2)}) %collective-permute-start.17) | collective-permute-done | bytes 229408 | tf_op jit(solution)/shard_map/ppermute | solution.py:25
  188.6 1.8 slice.110
  191.6 3.3 %collective-permute-start.12 = (bf16[128,1792]{1,0:T(8,128)(2,1)S(1)}, bf16[128,1792]{1,0:T(8,128)(2,1)S(1)}, u32[]{:S(2)}, u32[]{:S(2)}) collective-permute-start(bf16[128,1792]{1,0:T(8,128)(2,1)S(1)} %slice.111), channel_id=1, source_target_pairs={{0,48},{16,0},{32,16},{48,32},{64,112},{80,64},{96,80},{112,96},{1... | collective-permute-start | bytes 1376264 | tf_op jit(solution)/shard_map/ppermute | solution.py:25
  194.9 2.2 constant_dynamic-update-slice_fusion.3
  197.0 2.2 constant_dynamic-update-slice_fusion.2
  199.2 1.6 collective-permute-done.11
  200.8 1.8 constant_dynamic-update-slice_fusion.1
  204.3 3.6 %all-to-all-start.5 = ((f32[8,33,128]{2,1,0:T(8,128)}), f32[8,33,128]{2,1,0:T(8,128)S(1)}, u32[]{:S(2)}, u32[]{:S(2)}) async-start(f32[8,33,128]{2,1,0:T(8,128)} %broadcast_in_dim.20), calls=%async_computation.5 | async-start | bytes 327680 | tf_op jit(solution)/shard_map/all_to_all | solution.py:153
  208.7 1.6 slice.168
  210.4 4.0 %all-to-all-done.5 = f32[8,33,128]{2,1,0:T(8,128)S(1)} async-done(((f32[8,33,128]{2,1,0:T(8,128)}), f32[8,33,128]{2,1,0:T(8,128)S(1)}, u32[]{:S(2)}, u32[]{:S(2)}) %all-to-all-start.5) | async-done | bytes 135200 | tf_op jit(solution)/shard_map/all_to_all | solution.py:153
  215.6 1.7 fusion.17
  218.9 2.1 multiply_convert_fusion
  222.0 3.7 %multiply_convert_fusion.1 = bf16[512,896]{1,0:T(8,128)(2,1)} fusion(bf16[1024,1792]{1,0:T(8,128)(2,1)} %constant_dynamic-update-slice_fusion, bf16[1024,1024]{1,0:T(8,128)(2,1)S(1)} %bitcast.82, f32[]{:T(128)} %bitcast.29), kind=kOutput, calls=%fused_computation.43 | convolution fusion | flops 940441600 | bytes 3801600 | tf_op jit(solution)/shard_map/dot_general | solution.py:188
  225.7 1.5 collective-permute-start.14
  227.2 3.7 %multiply_convert_fusion.2 = bf16[512,896]{1,0:T(8,128)(2,1)} fusion(bf16[1024,1792]{1,0:T(8,128)(2,1)} %constant_dynamic-update-slice_fusion, bf16[1024,1024]{1,0:T(8,128)(2,1)S(1)} %bitcast.83, f32[]{:T(128)} %bitcast.29), kind=kOutput, calls=%fused_computation.45 | convolution fusion | flops 940441600 | bytes 3801600 | tf_op jit(solution)/shard_map/dot_general | solution.py:188
  231.5 2.8 fusion.28
  234.3 4.0 %fusion.32 = f32[512,896]{1,0:T(8,128)} fusion(bf16[1024,1792]{1,0:T(8,128)(2,1)} %constant_dynamic-update-slice_fusion, bf16[1024,1024]{1,0:T(8,128)(2,1)S(1)} %bitcast.85), kind=kOutput, calls=%fused_computation.52 | convolution fusion | flops 939524096 | bytes 4718592 | tf_op jit(solution)/shard_map/dot_general | solution.py:192
  238.3 6.1 %collective-permute-done.19 = bf16[448,1024]{1,0:T(8,128)(2,1)S(1)} collective-permute-done((bf16[448,1024]{1,0:T(8,128)(2,1)S(1)}, bf16[448,1024]{1,0:T(8,128)(2,1)S(1)}, u32[]{:S(2)}, u32[]{:S(2)}) %collective-permute-start.19) | collective-permute-done | bytes 917536 | tf_op jit(solution)/shard_map/ppermute | solution.py:172
  245.7 3.8 %all-to-all-start.4 = ((bf16[4,112,1024]{2,1,0:T(8,128)(2,1)}), bf16[4,112,1024]{2,1,0:T(8,128)(2,1)S(1)}, u32[]{:S(2)}, u32[]{:S(2)}) async-start(bf16[4,112,1024]{2,1,0:T(8,128)(2,1)} %bitcast.36), calls=%async_computation.4 | async-start | bytes 1835008 | tf_op jit(solution)/shard_map/all_to_all | solution.py:174
  249.5 31.1 %collective-permute-done.13 = bf16[512,896]{1,0:T(8,128)(2,1)} collective-permute-done((bf16[512,896]{1,0:T(8,128)(2,1)}, bf16[512,896]{1,0:T(8,128)(2,1)}, u32[]{:S(2)}, u32[]{:S(2)}) %collective-permute-start.13) | collective-permute-done | bytes 917536 | tf_op jit(solution)/shard_map/ppermute | solution.py:190
  280.6 2.0 fusion.45
  284.2 3.1 %copy.31 = bf16[512,2,896]{2,1,0:T(2,128)(2,1)} copy(bf16[512,2,896]{2,0,1:T(8,128)(2,1)S(1)} %pad_maximum_fusion.4) | data formatting | bytes 3670016
  289.2 1.6 reshape.133
  (107 shorter events, 28.0 us)
Async XLA Ops:
  0.6 25.9 %copy-start.6 = (bf16[16,4096]{1,0:T(8,128)(2,1)S(1)}, bf16[16,4096]{1,0:T(8,128)(2,1)}, u32[]{:S(2)}) copy-start(bf16[16,4096]{1,0:T(8,128)(2,1)} %param.13) | copy-start | bytes 393220
  26.6 22.7 %collective-permute-start = (bf16[8,16,4096]{2,1,0:T(8,128)(2,1)S(1)}, bf16[8,16,4096]{2,1,0:T(8,128)(2,1)S(1)}, u32[]{:S(2)}, u32[]{:S(2)}) collective-permute-start(bf16[8,16,4096]{2,1,0:T(8,128)(2,1)S(1)} %all_to_all.30), channel_id=1, source_target_pairs={{0,1},{1,0},{2,3},{3,2},{4,5},{5,4},{6,7},{7,6},{8,9},{9,8},{10,11... | collective-permute-start | bytes 3145736 | tf_op jit(solution)/shard_map/ppermute | solution.py:34
  27.6 21.7 %all-to-all-start.1 = ((bf16[8,16,4096]{2,1,0:T(8,128)(2,1)}), bf16[8,16,4096]{2,1,0:T(8,128)(2,1)S(1)}, u32[]{:S(2)}, u32[]{:S(2)}) async-start(bf16[8,16,4096]{2,1,0:T(8,128)(2,1)} %broadcast_in_dim.15), calls=%async_computation.1 | async-start | bytes 2097152 | tf_op jit(solution)/shard_map/all_to_all | solution.py:29
  48.6 1.2 copy-start.9
  49.3 10.7 %copy-start = (bf16[8,16,4096]{2,1,0:T(8,128)(2,1)}, bf16[8,16,4096]{2,1,0:T(8,128)(2,1)S(1)}, u32[]{:S(2)}) copy-start(bf16[8,16,4096]{2,1,0:T(8,128)(2,1)S(1)} %all-to-all-done.1) | copy-start | bytes 3145732
  49.3 10.7 %collective-permute-start.2 = (bf16[8,16,4096]{2,1,0:T(8,128)(2,1)S(1)}, bf16[8,16,4096]{2,1,0:T(8,128)(2,1)S(1)}, u32[]{:S(2)}, u32[]{:S(2)}) collective-permute-start(bf16[8,16,4096]{2,1,0:T(8,128)(2,1)S(1)} %all-to-all-done.1), channel_id=1, source_target_pairs={{0,1},{1,0},{2,3},{3,2},{4,5},{5,4},{6,7},{7,6},{8,9},{9,8},{10,11... | collective-permute-start | bytes 3145736 | tf_op jit(solution)/shard_map/ppermute | solution.py:34
  49.3 9.5 %copy-start.5 = (bf16[8,16,4096]{2,1,0:T(8,128)(2,1)}, bf16[8,16,4096]{2,1,0:T(8,128)(2,1)S(1)}, u32[]{:S(2)}) copy-start(bf16[8,16,4096]{2,1,0:T(8,128)(2,1)S(1)} %collective-permute-done) | copy-start | bytes 3145732
  49.3 10.7 %slice-start = ((s8[7340032]{0:T(1024)(128)(4,1)}), s8[3145728]{0:T(1024)(128)(4,1)S(1)}, s32[]{:S(2)}) async-start(s8[7340032]{0:T(1024)(128)(4,1)} %bitcast.100), calls=%async_computation.6 | async-start | bytes 6291456
  49.8 10.2 %slice-start.1 = ((s8[7340032]{0:T(1024)(128)(4,1)}), s8[4194304]{0:T(1024)(128)(4,1)S(1)}, s32[]{:S(2)}) async-start(s8[7340032]{0:T(1024)(128)(4,1)} %bitcast.100), calls=%async_computation.7 | async-start | bytes 8388608
  60.0 3.6 %copy-start.4 = (bf16[8,16,4096]{2,1,0:T(8,128)(2,1)}, bf16[8,16,4096]{2,1,0:T(8,128)(2,1)S(1)}, u32[]{:S(2)}) copy-start(bf16[8,16,4096]{2,1,0:T(8,128)(2,1)S(1)} %collective-permute-done.2) | copy-start | bytes 3145732
  74.0 1.0 copy-start.7
  74.0 6.7 %collective-permute-start.4 = (f32[1,4096]{1,0:T(1,128)S(1)}, f32[1,4096]{1,0:T(1,128)S(1)}, u32[]{:S(2)}, u32[]{:S(2)}) collective-permute-start(f32[1,4096]{1,0:T(1,128)S(1)} %bitcast.98), channel_id=1, source_target_pairs={{0,1},{1,0},{2,3},{3,2},{4,5},{5,4},{6,7},{7,6},{8,9},{9,8},{10,11... | collective-permute-start | bytes 49160 | tf_op jit(solution)/shard_map/ppermute | solution.py:135
  74.2 6.6 %collective-permute-start.3 = (bf16[128,4096]{1,0:T(8,128)(2,1)S(1)}, bf16[128,4096]{1,0:T(8,128)(2,1)S(1)}, u32[]{:S(2)}, u32[]{:S(2)}) collective-permute-start(bf16[128,4096]{1,0:T(8,128)(2,1)S(1)} %slice.104), channel_id=1, source_target_pairs={{0,1},{1,0},{2,3},{3,2},{4,5},{5,4},{6,7},{7,6},{8,9},{9,8},{10,11... | collective-permute-start | bytes 3145736 | tf_op jit(solution)/shard_map/ppermute | solution.py:131
  80.5 2.7 collective-permute-start.1
  85.3 6.6 %copy-start.3 = (bf16[16,4096]{1,0:T(8,128)(2,1)S(1)}, bf16[16,4096]{1,0:T(8,128)(2,1)}, u32[]{:S(2)}) copy-start(bf16[16,4096]{1,0:T(8,128)(2,1)} %param.7) | copy-start | bytes 393220
  85.4 41.0 %all-to-all-start.2 = ((bf16[8,34,4096]{2,1,0:T(8,128)(2,1)}), bf16[8,34,4096]{2,1,0:T(8,128)(2,1)S(1)}, u32[]{:S(2)}, u32[]{:S(2)}) async-start(bf16[8,34,4096]{2,1,0:T(8,128)(2,1)} %pad_maximum_fusion), calls=%async_computation.2 | async-start | bytes 5242880 | tf_op jit(solution)/shard_map/all_to_all | solution.py:29
  126.7 0.9 copy-start.2
  128.5 5.5 %collective-permute-start.5 = (bf16[2,16,1024]{2,1,0:T(8,128)(2,1)S(1)}, bf16[2,16,1024]{2,1,0:T(8,128)(2,1)S(1)}, u32[]{:S(2)}, u32[]{:S(2)}) collective-permute-start(bf16[2,16,1024]{2,1,0:T(8,128)(2,1)S(1)} %pad_maximum_fusion.8), channel_id=1, source_target_pairs={{0,16},{16,32},{32,48},{48,0},{64,80},{80,96},{96,112},{112,64},{1... | collective-permute-start | bytes 196616 | tf_op jit(solution)/shard_map/ppermute | solution.py:25
  130.1 4.7 %collective-permute-start.6 = (bf16[2,16,1024]{2,1,0:T(8,128)(2,1)S(1)}, bf16[2,16,1024]{2,1,0:T(8,128)(2,1)S(1)}, u32[]{:S(2)}, u32[]{:S(2)}) collective-permute-start(bf16[2,16,1024]{2,1,0:T(8,128)(2,1)S(1)} %pad_maximum_fusion.9), channel_id=1, source_target_pairs={{0,48},{16,0},{32,16},{48,32},{64,112},{80,64},{96,80},{112,96},{1... | collective-permute-start | bytes 196616 | tf_op jit(solution)/shard_map/ppermute | solution.py:25
  131.9 5.8 %collective-permute-start.7 = (bf16[2,16,1024]{2,1,0:T(8,128)(2,1)S(1)}, bf16[2,16,1024]{2,1,0:T(8,128)(2,1)S(1)}, u32[]{:S(2)}, u32[]{:S(2)}) collective-permute-start(bf16[2,16,1024]{2,1,0:T(8,128)(2,1)S(1)} %pad_maximum_fusion.10), channel_id=1, source_target_pairs={{0,32},{16,48},{32,0},{48,16},{64,96},{80,112},{96,64},{112,80},{1... | collective-permute-start | bytes 196616 | tf_op jit(solution)/shard_map/ppermute | solution.py:25
  139.4 57.6 %all-to-all-start.3 = ((bf16[8,128,1024]{2,1,0:T(8,128)(2,1)}), bf16[8,128,1024]{2,1,0:T(8,128)(2,1)S(1)}, u32[]{:S(2)}, u32[]{:S(2)}) async-start(bf16[8,128,1024]{2,1,0:T(8,128)(2,1)} %broadcast_in_dim.18), calls=%async_computation.3 | async-start | bytes 4194304 | tf_op jit(solution)/shard_map/all_to_all | solution.py:29
  150.0 7.9 %copy-start.1 = (bf16[8,16,4096]{2,1,0:T(8,128)(2,1)S(1)}, bf16[8,16,4096]{2,1,0:T(8,128)(2,1)}, u32[]{:S(2)}) copy-start(bf16[8,16,4096]{2,1,0:T(8,128)(2,1)} %copy-done) | copy-start | bytes 3145732
  150.0 13.8 %collective-permute-start.16 = (bf16[256,896]{1,0:T(8,128)(2,1)}, bf16[256,896]{1,0:T(8,128)(2,1)}, u32[]{:S(2)}, u32[]{:S(2)}) collective-permute-start(bf16[256,896]{1,0:T(8,128)(2,1)} %get-tuple-element.45), channel_id=1, source_target_pairs={{0,48},{16,0},{32,16},{48,32},{64,112},{80,64},{96,80},{112,96},{1... | collective-permute-start | bytes 1376264 | tf_op jit(solution)/shard_map/ppermute | solution.py:25
  151.6 16.0 %collective-permute-start.15 = (bf16[256,896]{1,0:T(8,128)(2,1)}, bf16[256,896]{1,0:T(8,128)(2,1)}, u32[]{:S(2)}, u32[]{:S(2)}) collective-permute-start(bf16[256,896]{1,0:T(8,128)(2,1)} %get-tuple-element.45), channel_id=1, source_target_pairs={{0,16},{16,32},{32,48},{48,0},{64,80},{80,96},{96,112},{112,64},{1... | collective-permute-start | bytes 1376264 | tf_op jit(solution)/shard_map/ppermute | solution.py:25
  154.6 34.0 %collective-permute-start.9 = (bf16[256,1792]{1,0:T(8,128)(2,1)}, bf16[256,1792]{1,0:T(8,128)(2,1)}, u32[]{:S(2)}, u32[]{:S(2)}) collective-permute-start(bf16[256,1792]{1,0:T(8,128)(2,1)} %get-tuple-element.51), channel_id=1, source_target_pairs={{0,16},{16,32},{32,48},{48,0},{64,80},{80,96},{96,112},{112,64},{1... | collective-permute-start | bytes 2752520 | tf_op jit(solution)/shard_map/ppermute | solution.py:25
  155.0 35.5 %collective-permute-start.10 = (bf16[256,1792]{1,0:T(8,128)(2,1)}, bf16[256,1792]{1,0:T(8,128)(2,1)}, u32[]{:S(2)}, u32[]{:S(2)}) collective-permute-start(bf16[256,1792]{1,0:T(8,128)(2,1)} %get-tuple-element.51), channel_id=1, source_target_pairs={{0,48},{16,0},{32,16},{48,32},{64,112},{80,64},{96,80},{112,96},{1... | collective-permute-start | bytes 2752520 | tf_op jit(solution)/shard_map/ppermute | solution.py:25
  164.8 23.1 %collective-permute-start.18 = (bf16[128,896]{1,0:T(8,128)(2,1)S(1)}, bf16[128,896]{1,0:T(8,128)(2,1)S(1)}, u32[]{:S(2)}, u32[]{:S(2)}) collective-permute-start(bf16[128,896]{1,0:T(8,128)(2,1)S(1)} %slice.116), channel_id=1, source_target_pairs={{0,48},{16,0},{32,16},{48,32},{64,112},{80,64},{96,80},{112,96},{1... | collective-permute-start | bytes 688136 | tf_op jit(solution)/shard_map/ppermute | solution.py:25
  168.6 18.6 %collective-permute-start.17 = (bf16[128,896]{1,0:T(8,128)(2,1)S(1)}, bf16[128,896]{1,0:T(8,128)(2,1)S(1)}, u32[]{:S(2)}, u32[]{:S(2)}) collective-permute-start(bf16[128,896]{1,0:T(8,128)(2,1)S(1)} %slice.115), channel_id=1, source_target_pairs={{0,16},{16,32},{32,48},{48,0},{64,80},{80,96},{96,112},{112,64},{1... | collective-permute-start | bytes 688136 | tf_op jit(solution)/shard_map/ppermute | solution.py:25
  190.5 10.3 %collective-permute-start.11 = (bf16[128,1792]{1,0:T(8,128)(2,1)}, bf16[128,1792]{1,0:T(8,128)(2,1)}, u32[]{:S(2)}, u32[]{:S(2)}) collective-permute-start(bf16[128,1792]{1,0:T(8,128)(2,1)} %slice.110), channel_id=1, source_target_pairs={{0,16},{16,32},{32,48},{48,0},{64,80},{80,96},{96,112},{112,64},{1... | collective-permute-start | bytes 1376264 | tf_op jit(solution)/shard_map/ppermute | solution.py:25
  191.6 16.4 %collective-permute-start.12 = (bf16[128,1792]{1,0:T(8,128)(2,1)S(1)}, bf16[128,1792]{1,0:T(8,128)(2,1)S(1)}, u32[]{:S(2)}, u32[]{:S(2)}) collective-permute-start(bf16[128,1792]{1,0:T(8,128)(2,1)S(1)} %slice.111), channel_id=1, source_target_pairs={{0,48},{16,0},{32,16},{48,32},{64,112},{80,64},{96,80},{112,96},{1... | collective-permute-start | bytes 1376264 | tf_op jit(solution)/shard_map/ppermute | solution.py:25
  197.0 18.6 %collective-permute-start.8 = (bf16[8,128,1024]{2,1,0:T(8,128)(2,1)S(1)}, bf16[8,128,1024]{2,1,0:T(8,128)(2,1)}, u32[]{:S(2)}, u32[]{:S(2)}) collective-permute-start(bf16[8,128,1024]{2,1,0:T(8,128)(2,1)S(1)} %all-to-all-done.3), channel_id=1, source_target_pairs={{0,1},{1,0},{2,3},{3,2},{4,5},{5,4},{6,7},{7,6},{8,9},{9,8},{10,11... | collective-permute-start | bytes 6291464 | tf_op jit(solution)/shard_map/ppermute | solution.py:34
  204.3 10.1 %all-to-all-start.5 = ((f32[8,33,128]{2,1,0:T(8,128)}), f32[8,33,128]{2,1,0:T(8,128)S(1)}, u32[]{:S(2)}, u32[]{:S(2)}) async-start(f32[8,33,128]{2,1,0:T(8,128)} %broadcast_in_dim.20), calls=%async_computation.5 | async-start | bytes 327680 | tf_op jit(solution)/shard_map/all_to_all | solution.py:153
  217.4 1.5 copy-start.8
  221.1 23.4 %collective-permute-start.19 = (bf16[448,1024]{1,0:T(8,128)(2,1)S(1)}, bf16[448,1024]{1,0:T(8,128)(2,1)S(1)}, u32[]{:S(2)}, u32[]{:S(2)}) collective-permute-start(bf16[448,1024]{1,0:T(8,128)(2,1)S(1)} %constant_dynamic-slice_fusion), channel_id=1, source_target_pairs={{0,64},{16,80},{32,96},{48,112},{64,0},{80,16},{96,32},{112,48},{1... | collective-permute-start | bytes 2752520 | tf_op jit(solution)/shard_map/ppermute | solution.py:172
  225.7 56.9 %collective-permute-start.14 = (bf16[512,896]{1,0:T(8,128)(2,1)}, bf16[512,896]{1,0:T(8,128)(2,1)}, u32[]{:S(2)}, u32[]{:S(2)}) collective-permute-start(bf16[512,896]{1,0:T(8,128)(2,1)} %multiply_convert_fusion.1), channel_id=1, source_target_pairs={{0,64},{16,80},{32,96},{48,112},{64,0},{80,16},{96,32},{112,48},{1... | collective-permute-start | bytes 2752520 | tf_op jit(solution)/shard_map/ppermute | solution.py:190
  231.0 49.6 %collective-permute-start.13 = (bf16[512,896]{1,0:T(8,128)(2,1)}, bf16[512,896]{1,0:T(8,128)(2,1)}, u32[]{:S(2)}, u32[]{:S(2)}) collective-permute-start(bf16[512,896]{1,0:T(8,128)(2,1)} %multiply_convert_fusion.2), channel_id=1, source_target_pairs={{0,64},{16,80},{32,96},{48,112},{64,0},{80,16},{96,32},{112,48},{1... | collective-permute-start | bytes 2752520 | tf_op jit(solution)/shard_map/ppermute | solution.py:190
  245.7 41.6 %all-to-all-start.4 = ((bf16[4,112,1024]{2,1,0:T(8,128)(2,1)}), bf16[4,112,1024]{2,1,0:T(8,128)(2,1)S(1)}, u32[]{:S(2)}, u32[]{:S(2)}) async-start(bf16[4,112,1024]{2,1,0:T(8,128)(2,1)} %bitcast.36), calls=%async_computation.4 | async-start | bytes 1835008 | tf_op jit(solution)/shard_map/all_to_all | solution.py:174

commit v2 on v0

v2 whole, which is shorter than its diff:
```python
import functools
import math

import jax
import jax.numpy as jnp
from jax import lax
from jax.experimental import pallas as pl
from jax.experimental.pallas import tpu as pltpu
from jax.sharding import PartitionSpec as P

PEAK = 448.0
EPSILON = 1e-05
ROWS = (((0,), (0,)), ((), ()))
COLS = (((1,), (1,)), ((), ()))
F32 = jnp.float32
BF16 = jnp.bfloat16
MIB = 1024 * 1024
SMEM = pltpu.SMEM
VMEM = pltpu.VMEM


def options(mib):
    return pltpu.CompilerParams(
        dimension_semantics=("arbitrary",), vmem_limit_bytes=mib * MIB
    )


def cost(macs, moved):
    return pl.CostEstimate(flops=2 * macs, bytes_accessed=moved, transcendentals=0)


def forward_kernel(
    steps, act_ref, own_ref, other_ref, gain_ref, wg_ref, wu_ref,
    hidden_ref, slope_ref, silu_ref, inverse_ref, peak_ref, q_ref, gate_ref, up_ref,
):
    step = pl.program_id(0)
    group = own_ref.shape[1]
    half = own_ref.shape[0] * group
    depth = wg_ref.shape[0]
    chunk = 2 * group

    def take(source, r, columns):
        block = source[r // group : r // group + 2, :, columns]
        return block.reshape(chunk, block.shape[2])

    def quantized(k, slot):
        scale = PEAK / act_ref[0]
        columns = pl.ds(pl.multiple_of(k * depth, depth), depth)
        gain = gain_ref[:, columns]
        peak = peak_ref[...]
        for source, base in ((own_ref, 0), (other_ref, half)):
            for r in range(0, half, chunk):
                rows = pl.ds(base + r, chunk)
                values = take(source, r, columns).astype(F32)
                normed = (values * inverse_ref[rows, :1]) * gain
                q_ref[slot, rows, :] = jnp.clip(normed * scale, -PEAK, PEAK).astype(BF16)
                size = jnp.abs(normed)
                for c in range(0, depth, 128):
                    peak = jnp.maximum(peak, size[:, c : c + 128])
        peak_ref[...] = peak

    @pl.when(step == 0)
    def _():
        peak_ref[...] = jnp.zeros_like(peak_ref)
        gate_ref[...] = jnp.zeros_like(gate_ref)
        up_ref[...] = jnp.zeros_like(up_ref)
        features = own_ref.shape[2]
        for source, base in ((own_ref, 0), (other_ref, half)):
            for r in range(0, half, chunk):
                total = jnp.zeros((chunk, 128), F32)
                for c in range(0, features, 128):
                    values = take(source, r, pl.ds(c, 128)).astype(F32)
                    total += values * values
                mean = jnp.sum(total, axis=-1, keepdims=True) / features
                inverse_ref[pl.ds(base + r, chunk), :] = jnp.broadcast_to(
                    lax.rsqrt(mean + EPSILON), (chunk, 128)
                )
        quantized(0, 0)

    slot = lax.rem(step, 2)
    block = q_ref[slot]
    gate_ref[...] += jnp.dot(block, wg_ref[...], preferred_element_type=F32)
    up_ref[...] += jnp.dot(block, wu_ref[...], preferred_element_type=F32)

    @pl.when(step < steps - 1)
    def _():
        quantized(step + 1, 1 - slot)

    @pl.when(step == steps - 1)
    def _():
        unit = act_ref[0] / PEAK

        @pl.loop(0, gate_ref.shape[0], step=32)
        def _(r):
            rows = pl.ds(pl.multiple_of(r, 32), 32)
            pre_gate = gate_ref[rows, :] * unit
            pre_up = up_ref[rows, :] * unit
            sigmoid = jax.nn.sigmoid(pre_gate)
            silu = pre_gate * sigmoid
            hidden_ref[rows, :] = (silu * pre_up).astype(BF16)
            silu_ref[rows, :] = silu
            slope_ref[rows, :] = pre_up * sigmoid * (1.0 + pre_gate * (1.0 - sigmoid))


def forward(act_history, own, other, gain, paired, depth=1024):
    half, features = own.shape[0] * own.shape[2], own.shape[3]
    width = paired.shape[1] // 2
    steps = features // depth
    rows = 2 * half
    whole = lambda *shape: pl.BlockSpec(shape, lambda i: (0,) * len(shape))
    token_rows = pl.BlockSpec((8, None, own.shape[2], features), lambda i: (0, 0, 0, 0))
    return pl.pallas_call(
        functools.partial(forward_kernel, steps),
        grid=(steps,),
        in_specs=[
            pl.BlockSpec(memory_space=SMEM),
            token_rows,
            token_rows,
            whole(1, features),
            pl.BlockSpec((depth, width), lambda i: (i, 0)),
            pl.BlockSpec((depth, width), lambda i: (i, 1)),
        ],
        out_specs=[
            whole(rows, width),
            whole(rows, width),
            whole(rows, width),
            whole(rows, 128),
            whole(32, 128),
        ],
        out_shape=[
            jax.ShapeDtypeStruct((rows, width), BF16),
            jax.ShapeDtypeStruct((rows, width), F32),
            jax.ShapeDtypeStruct((rows, width), F32),
            jax.ShapeDtypeStruct((rows, 128), F32),
            jax.ShapeDtypeStruct((32, 128), F32),
        ],
        scratch_shapes=[
            VMEM((2, rows, depth), BF16),
            VMEM((rows, width), F32),
            VMEM((rows, width), F32),
        ],
        compiler_params=options(62),
        cost_estimate=cost(rows * features * width * 2, paired.size * 2),
        name="forward",
    )(act_history, own, other, gain, paired, paired)


def both_rows(own_ref, other_ref):
    groups, rows, depth = own_ref.shape
    own = own_ref[...].reshape(groups * rows, depth)
    return jnp.concatenate([own, other_ref[...].reshape(groups * rows, depth)])


def backward_kernel(
    steps, history_ref, own_ref, other_ref, down_ref, slope_ref, silu_ref,
    gate_ref, up_ref, peak_ref, total_ref,
):
    step = pl.program_id(0)

    @pl.when(step == 0)
    def _():
        total_ref[...] = jnp.zeros_like(total_ref)
        peak_ref[...] = jnp.zeros_like(peak_ref)

    values = both_rows(own_ref, other_ref).astype(F32)
    peak_ref[...] = jnp.maximum(peak_ref[...], jnp.max(jnp.abs(values)))
    block = jnp.clip(values * (PEAK / history_ref[0]), -PEAK, PEAK).astype(BF16)
    total_ref[...] += lax.dot_general(block, down_ref[...], COLS, preferred_element_type=F32)

    @pl.when(step == steps - 1)
    def _():
        d_hidden = total_ref[...] * (history_ref[0] / PEAK)
        gate_ref[...] = (d_hidden * slope_ref[...]).astype(BF16)
        up_ref[...] = (d_hidden * silu_ref[...]).astype(BF16)


def backward(grad_history, own, other, down, slope, silu, depth=1024):
    half, features = own.shape[0] * own.shape[2], own.shape[3]
    strip = pl.BlockSpec((8, None, own.shape[2], depth), lambda i: (0, 1, 0, i))
    width = down.shape[0]
    steps = features // depth
    rows = 2 * half
    whole = lambda *shape: pl.BlockSpec(shape, lambda i: (0,) * len(shape))
    return pl.pallas_call(
        functools.partial(backward_kernel, steps),
        grid=(steps,),
        in_specs=[
            pl.BlockSpec(memory_space=SMEM),
            strip,
            strip,
            pl.BlockSpec((width, depth), lambda i: (0, i)),
            whole(rows, width),
            whole(rows, width),
        ],
        out_specs=[whole(rows, width), whole(rows, width), whole(8, 128)],
        out_shape=[
            jax.ShapeDtypeStruct((rows, width), BF16),
            jax.ShapeDtypeStruct((rows, width), BF16),
            jax.ShapeDtypeStruct((8, 128), F32),
        ],
        scratch_shapes=[VMEM((rows, width), F32)],
        compiler_params=options(62),
        cost_estimate=cost(rows * features * width, down.size * 2),
        name="backward",
    )(grad_history, own, other, down, slope, silu)


def out_kernel(hidden_ref, down_ref, own_ref, other_ref):
    half = own_ref.shape[0]
    share = jnp.dot(hidden_ref[...], down_ref[...], preferred_element_type=F32).astype(BF16)
    own_ref[...] = share[:half]
    other_ref[...] = share[half:]


def out_shares(hidden, down, depth=1024):
    rows, width = hidden.shape
    half, features = rows // 2, down.shape[1]
    strip = pl.BlockSpec((half, depth), lambda i: (0, i))
    return pl.pallas_call(
        out_kernel,
        grid=(features // depth,),
        in_specs=[
            pl.BlockSpec((rows, width), lambda i: (0, 0)),
            pl.BlockSpec((width, depth), lambda i: (0, i)),
        ],
        out_specs=[strip, strip],
        out_shape=[jax.ShapeDtypeStruct((half, features), BF16)] * 2,
        compiler_params=options(62),
        cost_estimate=cost(rows * features * width, down.size * 2),
        name="out_shares",
    )(hidden, down)


def normed_kernel(
    gate_ref, up_ref, wg_ref, wu_ref, own_ref, other_ref, inverse_ref,
    norm_own_ref, norm_other_ref, gain_ref,
):
    half = norm_own_ref.shape[0]
    normed = lax.dot_general(gate_ref[...], wg_ref[...], COLS, preferred_element_type=F32)
    normed += lax.dot_general(up_ref[...], wu_ref[...], COLS, preferred_element_type=F32)
    norm_own_ref[...] = normed[:half].astype(BF16)
    norm_other_ref[...] = normed[half:].astype(BF16)
    unit = both_rows(own_ref, other_ref).astype(F32) * inverse_ref[:, :1]
    gain_ref[...] = jnp.sum(normed * unit, axis=0, keepdims=True)


def normed_shares(d_gate, d_up, paired, own, other, inverse, depth=1024):
    half, features = own.shape[0] * own.shape[2], own.shape[3]
    rows, width = d_gate.shape
    token_rows = pl.BlockSpec((8, None, own.shape[2], depth), lambda i: (0, 0, 0, i))
    whole = lambda *shape: pl.BlockSpec(shape, lambda i: (0,) * len(shape))
    strip = pl.BlockSpec((half, depth), lambda i: (0, i))
    return pl.pallas_call(
        normed_kernel,
        grid=(features // depth,),
        in_specs=[
            whole(rows, width),
            whole(rows, width),
            pl.BlockSpec((depth, width), lambda i: (i, 0)),
            pl.BlockSpec((depth, width), lambda i: (i, 1)),
            token_rows,
            token_rows,
            whole(rows, 128),
        ],
        out_specs=[strip, strip, pl.BlockSpec((1, depth), lambda i: (0, i))],
        out_shape=[jax.ShapeDtypeStruct((half, features), BF16)] * 2
        + [jax.ShapeDtypeStruct((1, features), F32)],
        compiler_params=options(62),
        cost_estimate=cost(rows * features * width * 2, paired.size * 2),
        name="normed_shares",
    )(d_gate, d_up, paired, paired, own, other, inverse)


def pack_kernel(out_own, out_got, norm_own, norm_got, parts_ref):
    across = parts_ref.shape[0]
    rows = out_own.shape[0] // (2 * across)
    place = 0
    for own, got in ((out_own, out_got), (norm_own, norm_got)):
        total = (own[...].astype(F32) + got[...].astype(F32)).astype(BF16)
        for h in range(2):
            for y in range(across):
                base = (h * across + y) * rows
                parts_ref[y, place : place + rows] = total[base : base + rows]
            place += rows


def pack(out_own, out_got, norm_own, norm_got, rows, depth=1024):
    half, features = out_own.shape
    strip = pl.BlockSpec((half, depth), lambda i: (0, i))
    total = 4 * rows
    return pl.pallas_call(
        pack_kernel,
        grid=(features // depth,),
        in_specs=[strip] * 4,
        out_specs=pl.BlockSpec((4, total, depth), lambda i: (0, 0, i)),
        out_shape=jax.ShapeDtypeStruct((4, total, features), BF16),
        compiler_params=options(62),
        cost_estimate=cost(2 * half * features, 12 * half * features),
        name="pack",
    )(out_own, out_got, norm_own, norm_got)


def slice_block(own_ref, other_ref):
    parts = []
    for ring in range(4):
        for source in (own_ref, other_ref):
            block = source[:, ring]
            parts.append(block.reshape(block.shape[0] * block.shape[1], block.shape[2]))
    return jnp.concatenate(parts)


def stack_rows(pieces, all_ref):
    rows = pieces[0].shape[0]
    for ring, piece in enumerate(pieces):
        all_ref[ring * rows : (ring + 1) * rows, :] = piece[...]


def pair_kernel(at_ref, scale_ref, p0, p1, p2, p3, own_ref, other_ref, out_ref, all_ref):
    @pl.when(pl.program_id(0) == 0)
    def _():
        stack_rows((p0, p1, p2, p3), all_ref)

    block = slice_block(own_ref, other_ref)
    total = lax.dot_general(block, all_ref[...], ROWS, preferred_element_type=F32)
    out_ref[...] = (total * scale_ref[0]).astype(BF16)


def down_kernel(at_ref, scale_ref, p0, p1, p2, p3, own_ref, other_ref, out_ref, all_ref):
    @pl.when(pl.program_id(0) == 0)
    def _():
        stack_rows((p0, p1, p2, p3), all_ref)

    block = slice_block(own_ref, other_ref)
    total = lax.dot_general(all_ref[...], block, ROWS, preferred_element_type=F32)
    out_ref[...] = (total * scale_ref[0]).astype(BF16)


def contract(kernel, scale, pieces, own, other, first, count, depth=256):
    rows, width = pieces[0].shape
    piece = pl.BlockSpec((rows, width), lambda i, at: (0, 0))
    steps = count // depth
    block = (own.shape[0], 4, own.shape[2], depth)
    cut = pl.BlockSpec(block, lambda i, at: (0, 0, 0, at[0] * steps + i))
    if kernel is pair_kernel:
        shape, spec = (count, width), pl.BlockSpec((depth, width), lambda i, at: (i, 0))
    else:
        shape, spec = (width, count), pl.BlockSpec((width, depth), lambda i, at: (0, i))
    return pl.pallas_call(
        kernel,
        grid_spec=pltpu.PrefetchScalarGridSpec(
            num_scalar_prefetch=1,
            grid=(steps,),
            in_specs=[pl.BlockSpec(memory_space=SMEM)] + [piece] * 4 + [cut, cut],
            out_specs=spec,
            scratch_shapes=[VMEM((4 * rows, width), BF16)],
        ),
        out_shape=jax.ShapeDtypeStruct(shape, BF16),
        compiler_params=options(62),
        cost_estimate=cost(4 * rows * width * count, 8 * rows * (width + count)),
        name="contract_" + ("pair" if kernel is pair_kernel else "down"),
    )(first.reshape(1).astype(jnp.int32), scale, *pieces, own, other)


def join_kernel(g0, g1, u0, u1, out_ref):
    out_ref[:, 0, :] = (g0[...].astype(F32) + g1[...].astype(F32)).astype(BF16)
    out_ref[:, 1, :] = (u0[...].astype(F32) + u1[...].astype(F32)).astype(BF16)


def join(gate_kept, gate_got, up_kept, up_got, depth=128):
    rows, width = gate_kept.shape
    strip = pl.BlockSpec((depth, width), lambda i: (i, 0))
    return pl.pallas_call(
        join_kernel,
        grid=(rows // depth,),
        in_specs=[strip] * 4,
        out_specs=pl.BlockSpec((depth, 2, width), lambda i: (i, 0, 0)),
        out_shape=jax.ShapeDtypeStruct((rows, 2, width), BF16),
        compiler_params=options(62),
        cost_estimate=cost(rows * width, rows * width * 12),
        name="join",
    )(gate_kept, gate_got, up_kept, up_got)

RINGS = [[2 * k + core for k in range(8)] for core in range(2)]
CORE = [(i, i ^ 1) for i in range(16)]
ZPAIR = [(i, i ^ 4) for i in range(8)]
LINES = [[8 * high + 2 * y + core for y in range(4)] for high in range(2) for core in range(2)]
ZFAR = [(i, i ^ 8) for i in range(16)]


def send_y(block, step):
    ring = [
        (8 * high + 2 * y + core, 8 * high + 2 * ((y + step) % 4) + core)
        for high in range(2)
        for y in range(4)
        for core in range(2)
    ]
    return lax.ppermute(block, "tensor", ring)


def exchange(parts):
    return lax.all_to_all(parts, "tensor", 0, 0, tiled=True, axis_index_groups=RINGS)


def exchange_y(parts):
    return lax.all_to_all(parts, "tensor", 0, 0, tiled=True, axis_index_groups=LINES)


def gather_ring(block):
    return exchange(jnp.broadcast_to(block[None], (8,) + block.shape))


def swap_core(block):
    return lax.ppermute(block, "tensor", CORE)


def send_x(block, step):
    ring = [(z * 4 + x, z * 4 + (x + step) % 4) for z in range(2) for x in range(4)]
    return lax.ppermute(block, "dp", ring)


def quantize(values, unit):
    return jnp.clip(values * unit, -PEAK, PEAK).astype(BF16)


def together(*values):
    return lax.optimization_barrier(values)


def after(value, *others):
    return lax.optimization_barrier((value,) + others)[0]


def shards(tokens, gate_up, down_proj, norm_gain, act_history, grad_history, grad_out):
    own_rows, features = tokens.shape
    width = down_proj.shape[0]
    groups = lax.axis_size("dp")
    lanes = lax.axis_size("tensor")
    root = 1.0 / math.sqrt(own_rows * groups * lanes)
    pair_scale = act_history / PEAK * root
    down_scale = grad_history / PEAK * root
    dp = lax.axis_index("dp")
    z_lo = dp // 4
    x = dp % 4
    z_hi = lax.axis_index("tensor") // 8
    span = features // 8
    half = own_rows * 8

    rows_own = gather_ring(jnp.stack([tokens, grad_out]))
    paired = gate_up.reshape(features, 2 * width)

    values = after(tokens, paired).astype(F32)
    inverse_rms = lax.rsqrt(jnp.mean(values * values, axis=-1, keepdims=True) + EPSILON)
    unit_rows = values * inverse_rms
    q_mine = quantize(unit_rows * norm_gain, PEAK / act_history[0])
    g_mine = quantize(grad_out.astype(F32), PEAK / grad_history[0])

    both = jnp.stack([q_mine, g_mine]).reshape(2 * own_rows, 2, 4, span)

    def columns(step):
        cut = lax.dynamic_slice(both, (0, 0, (x + step) % 4, 0), (2 * own_rows, 2, 1, span))
        return cut.reshape(2 * own_rows, 2 * span)

    sliced = jnp.stack(
        [columns(0), send_x(columns(1), 1), send_x(columns(-1), -1), send_x(columns(2), 2)]
    )
    rows_own = after(rows_own, sliced)
    rows_other = swap_core(rows_own)
    sliced = after(sliced, rows_own).reshape(4, 2, own_rows, 2 * span)

    def gather_slices(kind):
        spread = gather_ring(sliced[:, kind].reshape(4 * own_rows, 2 * span))
        return spread.reshape(8, 4, own_rows, 2 * span)

    g_own = gather_slices(1)

    hidden, slope, silu, inverse, act_peak = forward(
        act_history, rows_own, rows_other, norm_gain.reshape(1, features), paired
    )
    hidden, g_own = together(hidden, g_own)

    g_other = swap_core(g_own)
    hidden_left, hidden_right = send_x(hidden, 1), send_x(hidden, -1)
    d_gate, d_up, grad_peak = backward(grad_history, rows_own, rows_other, down_proj, slope, silu)
    hidden, hidden_left, hidden_right, g_other, d_gate, d_up = together(
        hidden, hidden_left, hidden_right, g_other, d_gate, d_up
    )

    q_own = gather_slices(0)
    hidden_far = send_x(hidden, 2)
    gate_left, gate_right = send_x(d_gate, 1), send_x(d_gate, -1)
    norm_own, norm_other, gain_share = normed_shares(
        d_gate, d_up, paired, rows_own, rows_other, inverse
    )
    hidden, hidden_far, gate_left, gate_right, q_own, norm_own, norm_other, gain_share = together(
        hidden, hidden_far, gate_left, gate_right, q_own, norm_own, norm_other, gain_share
    )
    d_gate, d_up, gain_share = together(d_gate, d_up, gain_share)
    hidden_all = (hidden, hidden_left, hidden_right, hidden_far)

    def merge(first, second):
        total = first[:, :features] + second[:, :features]
        peak = jnp.maximum(first[:, features:], second[:, features:])
        return jnp.concatenate([total, peak], axis=1)

    q_other = swap_core(q_own)
    norm_got = swap_core(norm_other)
    gate_far = send_x(d_gate, 2)
    peaks = jnp.concatenate(
        [jnp.full((1, 64), jnp.max(act_peak)), jnp.full((1, 64), jnp.max(grad_peak))], axis=1
    )
    small = jnp.concatenate([gain_share, peaks], axis=1)
    small = merge(small, swap_core(small))
    small = merge(small, lax.ppermute(small, "dp", ZPAIR))
    down_part = contract(
        down_kernel, down_scale, hidden_all, g_own, g_other, z_lo * 0, 2 * span
    )
    hand = width // 2
    sent_down = lax.dynamic_slice(down_part, ((1 - z_lo) * hand, 0), (hand, 2 * span))
    kept_down = lax.dynamic_slice(down_part, (z_lo * hand, 0), (hand, 2 * span))
    sent_down, gate_far, q_other, norm_got, small, d_up, hidden = together(
        sent_down, gate_far, q_other, norm_got, small, d_up, hidden
    )
    gate_all = (d_gate, gate_left, gate_right, gate_far)

    def pair_part(pieces, place, scale=pair_scale):
        return contract(pair_kernel, scale, pieces, q_own, q_other, place, span)

    got_down = lax.ppermute(sent_down, "dp", ZPAIR)
    up_left, up_right = send_x(d_up, 1), send_x(d_up, -1)
    out_own, out_other = out_shares(hidden, down_proj)
    got_down, up_left, up_right, out_own, out_other, d_up, d_gate, norm_own, norm_got, small = (
        together(
            got_down, up_left, up_right, out_own, out_other, d_up, d_gate, norm_own, norm_got, small
        )
    )
    out_got = swap_core(out_other)
    gate_sent = pair_part((d_gate,) + gate_all[1:], 1 - z_lo)
    gate_sent, out_got, d_up, norm_own, norm_got, small = together(
        gate_sent, out_got, d_up, norm_own, norm_got, small
    )

    gate_got = lax.ppermute(gate_sent, "dp", ZPAIR)
    up_far = send_x(d_up, 2)
    small_far, small_left, small_right = send_x(small, 2), send_x(small, 1), send_x(small, -1)
    parts = pack(out_own, out_got, norm_own, norm_got, own_rows)
    up_far, parts, d_up, small, small_far, small_left, small_right = together(
        up_far, parts, d_up, small, small_far, small_left, small_right
    )
    sums = exchange_y(parts)

    up_all = (d_up, up_left, up_right, up_far)
    up_sent = pair_part(up_all, 1 - z_lo)
    up_sent, small, small_far, small_left, small_right, kept_down, got_down, late_scale = (
        together(
            up_sent, small, small_far, small_left, small_right, kept_down, got_down, pair_scale
        )
    )
    small = merge(merge(small, small_far), merge(small_left, small_right))
    up_got = lax.ppermute(up_sent, "dp", ZPAIR)
    small_far, small_left, small_right = send_y(small, 2), send_y(small, 1), send_y(small, -1)
    gate_kept = pair_part(gate_all, z_lo, late_scale)
    up_kept = pair_part(up_all, z_lo, late_scale)

    sum_down = (kept_down.astype(F32) + got_down.astype(F32)).astype(BF16)
    sum_down = sum_down.reshape(4, hand // 4, 2 * span)

    def own_part(step):
        return lax.dynamic_index_in_dim(sum_down, (x + step) % 4, 0, keepdims=False)

    turned = jnp.stack(
        [own_part(0), send_x(own_part(1), 1), send_x(own_part(2), 2), send_x(own_part(-1), -1)]
    )
    turned = turned[(x - jnp.arange(4)) % 4]
    grad_down = (
        turned.reshape(4, hand // 4, 2, span).transpose(1, 2, 0, 3).reshape(hand // 4, features)
    )

    up_got, gate_kept, up_kept, grad_down, small, small_far, small_left, small_right, sums = together(
        up_got, gate_kept, up_kept, grad_down, small, small_far, small_left, small_right, sums
    )
    small = merge(merge(small, small_far), merge(small_left, small_right))
    totals = jnp.sum(sums.astype(F32), axis=0)
    rows = totals.reshape(2, 2, own_rows, features)
    kept = lax.dynamic_index_in_dim(rows, z_hi, 1, keepdims=False)
    sent = lax.dynamic_index_in_dim(rows, 1 - z_hi, 1, keepdims=False).astype(BF16)
    rows = kept + lax.ppermute(sent, "tensor", ZFAR).astype(F32)
    mlp_out = rows[0].astype(BF16)
    d_normed = rows[1]
    gain_sum = small[0, :features]
    grad_gain = (gain_sum + lax.ppermute(gain_sum, "tensor", ZFAR)) * root
    scaled = d_normed * norm_gain
    grad_tokens = (
        inverse_rms * (scaled - unit_rows * jnp.mean(scaled * unit_rows, axis=-1, keepdims=True))
    ).astype(BF16)
    grad_gate_up = join(gate_kept, gate_got, up_kept, up_got)
    return (
        mlp_out,
        grad_tokens,
        grad_gate_up,
        grad_down,
        grad_gain,
        small[0, features : features + 1],
        small[0, features + 64 : features + 65],
    )


def solution(mesh):
    placed = (
        P(("dp", "tensor"), None),
        P(None, None, "tensor"),
        P("tensor", None),
        P(),
        P(),
        P(),
        P(("dp", "tensor"), None),
    )
    return jax.shard_map(
        shards,
        mesh=mesh,
        in_specs=placed,
        out_specs=(
            P(("dp", "tensor"), None),
            P(("dp", "tensor"), None),
            P("dp", None, "tensor"),
            P(("tensor", "dp"), None),
            P(),
            P(),
            P(),
        ),
        check_vma=False,
    )
```

time: 681 us -> 222 us (0.33)
  blocking collectives: 395 us -> 0 us
  waiting for transfers between devices: 140 us -> 40.2 us
  Pallas kernels: 0 us -> 67.6 us
  starting transfers between devices: 0.43 us -> 65.2 us
  matrix products: 54.1 us -> 0 us
  local copies, waits for them, and re-layouts: 61.7 us -> 35.1 us
  between operations: 16.2 us -> 2.6 us
    pmax x1 -> x0, blocking collectives: 326 us -> none  [shards(): peak_act = lax.pmax(local_act, ('dp', 'tensor'))]
    all_gather x2 -> x0, waiting for transfers between devices: 71.5 us -> none  [the longest x1 39.2 us: shards(): grad_rows = lax.all_gather(grad_quant, 'tensor', axis=0, tiled=True)]
    psum x1 -> x0, blocking collectives: 69.1 us -> none  [shards(): lax.psum(jnp.sum(d_normed * unit_rows, axis=0), ('dp', 'tensor')) * root]
    reduce_scatter x3 -> x0, waiting for transfers between devices: 68.1 us -> none  [the longest x1 60.9 us: shards(): lax.psum_scatter((lax.dot_general(block, grad_rows, CONTRACT_ROWS, prefer...]
    pallas_call x0 -> x11, Pallas kernels: none -> 67.6 us  [the longest x5 22.2 us: contract(): pl.pallas_call(kernel, grid_spec=pltpu.PrefetchScalarGridSpec(num_scalar_...]
    dot_general x6 -> x0, matrix products: 54.1 us -> none  [the longest x1 15.8 us: shards(): lax.dot_general(block, paired, CONTRACT_COLS, preferred_element_type=jnp....]
    ppermute x0 -> x33, starting transfers between devices: none -> 42.2 us  [the longest x18 27.1 us: send_x(): return lax.ppermute(block, 'dp', ring)]
    convert_element_type x1 -> x2, local copies, waits for them, and re-layouts: 36.7 us -> 0.71 us  [the longest x1 0.67 us: shards(): mlp_out = rows[0].astype(BF16)]
  transfers between devices with their start and end apart: 6 -> 37, of which waited for: 4 -> 14; matrix products, arithmetic and copies ran while one was open for 14% -> 16% of each run, Pallas kernels for 0% -> 31%
where the time goes in v2:
time: 222 us; the launch traced here: 221 us
  Pallas kernels  67.6 us (30%)
  starting transfers between devices  65.2 us (29%)
  waiting for transfers between devices  40.2 us (18%)
  local copies, waits for them, and re-layouts  35.1 us (16%)
  other arithmetic  10.1 us (5%)
  between operations  2.6 us (1%)
    ppermute x18, starting transfers between devices, send_x(): return lax.ppermute(block, 'dp', ring)  27.1 us
    pallas_call x5, Pallas kernels, contract(): pl.pallas_call(kernel, grid_spec=pltpu.PrefetchScalarGridSpec(num_scalar_...  22.2 us
    ppermute x18, waiting for transfers between devices, send_x(): return lax.ppermute(block, 'dp', ring)  22 us
    unnamed x40, local copies, waits for them, and re-layouts  19 us
    all_to_all x3, starting transfers between devices, exchange(): lax.all_to_all(parts, 'tensor', 0, 0, tiled=True, axis_index_groups=RINGS)  18.6 us
    pallas_call x1, Pallas kernels, forward(): pl.pallas_call(functools.partial(forward_kernel, steps), grid=(steps,), i...  12.1 us
    pallas_call x1, Pallas kernels, normed_shares(): pl.pallas_call(normed_kernel, grid=(features // depth,), in_specs=[whole(...  9.81 us
    ppermute x1, waiting for transfers between devices, shards(): got_down = lax.ppermute(sent_down, 'dp', ZPAIR)  8.19 us
  transfers between devices with their start and end apart: 37, of which 14 were waited for; matrix products, arithmetic and copies ran while one was open for 16% of the time, Pallas kernels for 31%

profile of v2, /device:TPU:0, one launch (start us, length us, event | category | flops | bytes accessed | tf_op | source)
XLA Modules:
  0.0 220.9 jit_solution(4128652201965875386)
XLA Ops:
  1.6 1.6 broadcast_in_dim.16
  3.2 7.9 %all-to-all-start = ((bf16[8,2,16,4096]{3,2,1,0:T(8,128)(2,1)}), bf16[8,2,16,4096]{3,2,1,0:T(8,128)(2,1)S(1)}, u32[]{:S(2)}, u32[]{:S(2)}) async-start(bf16[8,2,16,4096]{3,2,1,0:T(8,128)(2,1)} %broadcast_in_dim.16), calls=%async_computation | async-start | bytes 4194304 | tf_op jit(solution)/shard_map/all_to_all | solution.py:401
  11.1 16.1 %copy.24 = bf16[512,8,2,896]{3,1,2,0:T(8,128)(2,1)} copy(bf16[512,8,2,896]{3,2,1,0:T(2,128)(2,1)} %bitcast.69) | data formatting | bytes 29360128
  29.2 1.8 dynamic-slice_reduce_fusion.3
  31.0 1.6 collective-permute-start
  32.6 1.8 collective-permute-start.1
  34.4 1.9 collective-permute-start.2
  37.4 2.9 %collective-permute-done.2 = bf16[32,1024]{1,0:T(8,128)(2,1)S(1)} collective-permute-done((bf16[32,1024]{1,0:T(8,128)(2,1)S(1)}, bf16[32,1024]{1,0:T(8,128)(2,1)S(1)}, u32[]{:S(2)}, u32[]{:S(2)}) %collective-permute-start.2) | collective-permute-done | bytes 65568 | tf_op jit(solution)/shard_map/ppermute | solution.py:418
  40.4 1.3 copy-done
  42.8 7.2 %all-to-all-start.1 = ((bf16[8,64,1024]{2,1,0:T(8,128)(2,1)}), bf16[8,64,1024]{2,1,0:T(8,128)(2,1)}, u32[]{:S(2)}, u32[]{:S(2)}) async-start(bf16[8,64,1024]{2,1,0:T(8,128)(2,1)} %broadcast_in_dim.36), calls=%async_computation.1 | async-start | bytes 2097152 | tf_op jit(solution)/shard_map/all_to_all | solution.py:401
  50.0 12.1 %forward.1 = (bf16[256,896]{1,0:T(8,128)(2,1)}, f32[256,896]{1,0:T(8,128)}, f32[256,896]{1,0:T(8,128)}, f32[256,128]{1,0:T(8,128)}, f32[32,128]{1,0:T(8,128)}) custom-call(f32[1]{0:T(128)S(6)} %copy.30.act_ref, bf16[8,2,16,4096]{3,2,1,0:T(8,128)(2,1)} %copy-done, bf16[8,2,16,4096]{3,2,1,0:T(8,128)(2,1)} %collective-permute-done.3.other_ref, ...), custom_call_target="tpu_custom_call" | custom-call | flops 3758096384 | bytes 14680064 | tf_op jit(solution)/shard_map/forward/pallas_call | solution.py:112
  62.0 5.9 %all-to-all-done.1 = bf16[8,64,1024]{2,1,0:T(8,128)(2,1)} async-done(((bf16[8,64,1024]{2,1,0:T(8,128)(2,1)}), bf16[8,64,1024]{2,1,0:T(8,128)(2,1)}, u32[]{:S(2)}, u32[]{:S(2)}) %all-to-all-start.1) | async-done | bytes 1048608 | tf_op jit(solution)/shard_map/all_to_all | solution.py:401
  68.2 3.0 %collective-permute-start.5 = (bf16[256,896]{1,0:T(8,128)(2,1)}, bf16[256,896]{1,0:T(8,128)(2,1)S(1)}, u32[]{:S(2)}, u32[]{:S(2)}) collective-permute-start(bf16[256,896]{1,0:T(8,128)(2,1)} %get-tuple-element.121.p0.hidden_ref), channel_id=1, source_target_pairs={{0,48},{16,0},{32,16},{48,32},{64,112},{80,64},{96,80},{112,96},{1... | collective-permute-start | bytes 1376264 | tf_op jit(solution)/shard_map/ppermute | solution.py:418
  72.3 3.6 %all-to-all-start.2 = ((bf16[8,64,1024]{2,1,0:T(8,128)(2,1)}), bf16[8,64,1024]{2,1,0:T(8,128)(2,1)S(1)}, u32[]{:S(2)}, u32[]{:S(2)}) async-start(bf16[8,64,1024]{2,1,0:T(8,128)(2,1)} %broadcast_in_dim.38), calls=%async_computation.2 | async-start | bytes 2097152 | tf_op jit(solution)/shard_map/all_to_all | solution.py:401
  75.9 7.9 %backward.1 = (bf16[256,896]{1,0:T(8,128)(2,1)}, bf16[256,896]{1,0:T(8,128)(2,1)}, f32[8,128]{1,0:T(8,128)}) custom-call(f32[1]{0:T(128)S(6)} %copy.31.history_ref, bf16[8,2,16,4096]{3,2,1,0:T(8,128)(2,1)} %copy-done, bf16[8,2,16,4096]{3,2,1,0:T(8,128)(2,1)} %collective-permute-done.3.other_ref, bf16[896,4096]{1,0:T(8,128)(2,1)} %down_ref.3, ...), custom_call_target="tpu_custom_call" | custom-call | flops 1879048192 | bytes 7340032 | tf_op jit(solution)/shard_map/backward/pallas_call | solution.py:184
  86.2 2.2 collective-permute-start.9
  88.4 1.3 reduce_max.19
  90.3 9.8 %normed_shares.1 = (bf16[128,4096]{1,0:T(8,128)(2,1)}, bf16[128,4096]{1,0:T(8,128)(2,1)}, f32[1,4096]{1,0:T(1,128)}) custom-call(bf16[256,896]{1,0:T(8,128)(2,1)} %get-tuple-element.127.gate_ref.p0, bf16[256,896]{1,0:T(8,128)(2,1)} %get-tuple-element.143.up_ref.p0, bf16[4096,1792]{1,0:T(8,128)(2,1)} %bitcast.62, bf16[4096,1792]{1,0:T(8,128)(2,1)} %bitcast.63, ...), custom_call_target="tpu_custom_call" | custom-call | flops 3758096384 | bytes 14680064 | tf_op jit(solution)/shard_map/normed_shares/pallas_call | solution.py:253
  100.1 8.3 %collective-permute-done.8.p1 = bf16[256,896]{1,0:T(8,128)(2,1)S(1)} collective-permute-done((bf16[256,896]{1,0:T(8,128)(2,1)}, bf16[256,896]{1,0:T(8,128)(2,1)S(1)}, u32[]{:S(2)}, u32[]{:S(2)}) %collective-permute-start.8) | collective-permute-done | bytes 458784 | tf_op jit(solution)/shard_map/ppermute | solution.py:418
  111.8 5.9 %contract_down.1 = bf16[896,1024]{1,0:T(8,128)(2,1)} custom-call(s32[1]{0:T(128)} %constant.118.clone.1.at_ref, f32[1]{0:T(128)S(6)} %mul.73.scale_ref, bf16[256,896]{1,0:T(8,128)(2,1)} %get-tuple-element.121.p0.hidden_ref, bf16[256,896]{1,0:T(8,128)(2,1)} %copy-done.16, bf16[256,896]{1,0:T(8,128)(2,1)} %copy-done.17, ...), custom_call_target="tpu_custom_call" | custom-call | flops 1879048192 | bytes 3932160 | tf_op jit(solution)/shard_map/contract_down/pallas_call | solution.py:348
  119.6 2.8 %constant_dynamic-slice_fusion.1 = (bf16[448,1024]{1,0:T(8,128)(2,1)}, bf16[448,1024]{1,0:T(8,128)(2,1)}) fusion(bf16[896,1024]{1,0:T(8,128)(2,1)} %contract_down.1, s32[]{:T(128)S(6)} %select_n.102, s32[]{:T(128)S(6)} %select_n.101), kind=kLoop, calls=%fused_computation.48 | loop fusion | bytes 3670024 | tf_op jit(solution)/shard_map/dynamic_slice | solution.py:519
  123.1 2.1 collective-permute-done.10.p3
  126.2 3.2 %collective-permute-start.17 = (bf16[256,896]{1,0:T(8,128)(2,1)S(1)}, bf16[256,896]{1,0:T(8,128)(2,1)S(1)}, u32[]{:S(2)}, u32[]{:S(2)}) collective-permute-start(bf16[256,896]{1,0:T(8,128)(2,1)S(1)} %copy-done.3), channel_id=1, source_target_pairs={{0,48},{16,0},{32,16},{48,32},{64,112},{80,64},{96,80},{112,96},{1... | collective-permute-start | bytes 1376264 | tf_op jit(solution)/shard_map/ppermute | solution.py:418
  129.4 6.3 %out_shares.1 = (bf16[128,4096]{1,0:T(8,128)(2,1)}, bf16[128,4096]{1,0:T(8,128)(2,1)}) custom-call(bf16[256,896]{1,0:T(8,128)(2,1)} %get-tuple-element.121.p0.hidden_ref, bf16[896,4096]{1,0:T(8,128)(2,1)} %down_ref.3), custom_call_target="tpu_custom_call" | custom-call | flops 1879048192 | bytes 7340032 | tf_op jit(solution)/shard_map/out_shares/pallas_call | solution.py:219
  135.8 3.4 %collective-permute-done.16.p1 = bf16[256,896]{1,0:T(8,128)(2,1)S(1)} collective-permute-done((bf16[256,896]{1,0:T(8,128)(2,1)S(1)}, bf16[256,896]{1,0:T(8,128)(2,1)S(1)}, u32[]{:S(2)}, u32[]{:S(2)}) %collective-permute-start.16) | collective-permute-done | bytes 458784 | tf_op jit(solution)/shard_map/ppermute | solution.py:418
  139.2 8.2 %collective-permute-done.15 = bf16[448,1024]{1,0:T(8,128)(2,1)} collective-permute-done((bf16[448,1024]{1,0:T(8,128)(2,1)}, bf16[448,1024]{1,0:T(8,128)(2,1)}, u32[]{:S(2)}, u32[]{:S(2)}) %collective-permute-start.15) | collective-permute-done | bytes 917536 | tf_op jit(solution)/shard_map/ppermute | solution.py:528
  147.4 4.1 %contract_pair.4 = bf16[512,896]{1,0:T(8,128)(2,1)} custom-call(s32[1]{0:T(128)} %bitcast.at_ref, f32[1]{0:T(128)S(6)} %mul.72.scale_ref, bf16[256,896]{1,0:T(8,128)(2,1)} %get-tuple-element.127.gate_ref.p0, bf16[256,896]{1,0:T(8,128)(2,1)} %copy-done.7, bf16[256,896]{1,0:T(8,128)(2,1)} %collective-permute-done.9.p2, ...), custom_call_target="tpu_custom_call" | custom-call | flops 939524096 | bytes 2883584 | tf_op jit(solution)/shard_map/contract_pair/pallas_call | solution.py:348
  151.5 1.3 collective-permute-start.19
  152.8 2.4 %collective-permute-start.20 = (f32[1,4224]{1,0:T(1,128)S(1)}, f32[1,4224]{1,0:T(1,128)S(1)}, u32[]{:S(2)}, u32[]{:S(2)}) collective-permute-start(f32[1,4224]{1,0:T(1,128)S(1)} %pad_maximum_fusion.5), channel_id=1, source_target_pairs={{0,32},{16,48},{32,0},{48,16},{64,96},{80,112},{96,64},{112,80},{1... | collective-permute-start | bytes 50696 | tf_op jit(solution)/shard_map/ppermute | solution.py:418
  155.2 3.2 %collective-permute-start.22 = (f32[1,4224]{1,0:T(1,128)S(1)}, f32[1,4224]{1,0:T(1,128)S(1)}, u32[]{:S(2)}, u32[]{:S(2)}) collective-permute-start(f32[1,4224]{1,0:T(1,128)S(1)} %pad_maximum_fusion.5), channel_id=1, source_target_pairs={{0,48},{16,0},{32,16},{48,32},{64,112},{80,64},{96,80},{112,96},{1... | collective-permute-start | bytes 50696 | tf_op jit(solution)/shard_map/ppermute | solution.py:418
  159.5 4.3 %pack.1 = bf16[4,64,4096]{2,1,0:T(8,128)(2,1)} custom-call(bf16[128,4096]{1,0:T(8,128)(2,1)} %get-tuple-element.138.out_own, bf16[128,4096]{1,0:T(8,128)(2,1)} %collective-permute-done.18.out_got, bf16[128,4096]{1,0:T(8,128)(2,1)} %get-tuple-element.140.norm_own, bf16[128,4096]{1,0:T(8,128)(2,1)} %collective-permute-done.12.norm_got), custom_call_target="tpu_custom_call" | custom-call | flops 2097152 | bytes 6291456 | tf_op jit(solution)/shard_map/pack/pallas_call | solution.py:291
  163.9 2.8 %collective-permute-done.20 = f32[1,4224]{1,0:T(1,128)S(1)} collective-permute-done((f32[1,4224]{1,0:T(1,128)S(1)}, f32[1,4224]{1,0:T(1,128)S(1)}, u32[]{:S(2)}, u32[]{:S(2)}) %collective-permute-start.20) | collective-permute-done | bytes 16928 | tf_op jit(solution)/shard_map/ppermute | solution.py:418
  167.6 4.0 %contract_pair.5 = bf16[512,896]{1,0:T(8,128)(2,1)} custom-call(s32[1]{0:T(128)} %bitcast.at_ref, f32[1]{0:T(128)S(6)} %mul.72.scale_ref, bf16[256,896]{1,0:T(8,128)(2,1)} %get-tuple-element.143.up_ref.p0, bf16[256,896]{1,0:T(8,128)(2,1)} %copy-done.8, bf16[256,896]{1,0:T(8,128)(2,1)} %copy-done.9, bf16[256,896]{1,0:T(8,128)(2,1)} %copy-done.10, ...), custom_call_target="tpu_custom_call" | custom-call | flops 939524096 | bytes 2883584 | tf_op jit(solution)/shard_map/contract_pair/pallas_call | solution.py:348
  172.6 4.5 %all-to-all-start.3 = ((bf16[4,64,4096]{2,1,0:T(8,128)(2,1)}), bf16[4,64,4096]{2,1,0:T(8,128)(2,1)}, u32[]{:S(2)}, u32[]{:S(2)}) async-start(bf16[4,64,4096]{2,1,0:T(8,128)(2,1)} %pack.1), calls=%async_computation.3 | async-start | bytes 4194304 | tf_op jit(solution)/shard_map/all_to_all | solution.py:405
  177.1 1.5 add_convert_fusion
  178.8 2.1 collective-permute-start.25
  180.9 1.8 collective-permute-start.26
  182.7 4.1 %contract_pair.7.u0 = bf16[512,896]{1,0:T(8,128)(2,1)} custom-call(s32[1]{0:T(128)} %bitcast.16.at_ref, f32[1]{0:T(128)S(6)} %mul.72.scale_ref, bf16[256,896]{1,0:T(8,128)(2,1)} %get-tuple-element.143.up_ref.p0, bf16[256,896]{1,0:T(8,128)(2,1)} %copy-done.8, bf16[256,896]{1,0:T(8,128)(2,1)} %copy-done.9, bf16[256,896]{1,0:T(8,128)(2,1)} %copy-done.10, ...), custom_call_target="tpu_custom_call" | custom-call | flops 939524096 | bytes 2883584 | tf_op jit(solution)/shard_map/contract_pair/pallas_call | solution.py:348
  186.8 4.1 %contract_pair.6.g0 = bf16[512,896]{1,0:T(8,128)(2,1)} custom-call(s32[1]{0:T(128)} %bitcast.16.at_ref, f32[1]{0:T(128)S(6)} %mul.72.scale_ref, bf16[256,896]{1,0:T(8,128)(2,1)} %get-tuple-element.127.gate_ref.p0, bf16[256,896]{1,0:T(8,128)(2,1)} %copy-done.7, bf16[256,896]{1,0:T(8,128)(2,1)} %collective-permute-done.9.p2, ...), custom_call_target="tpu_custom_call" | custom-call | flops 939524096 | bytes 2883584 | tf_op jit(solution)/shard_map/contract_pair/pallas_call | solution.py:348
  190.8 1.4 collective-permute-done.24
  192.2 3.2 %collective-permute-start.27 = (f32[1,4224]{1,0:T(1,128)S(1)}, f32[1,4224]{1,0:T(1,128)S(1)}, u32[]{:S(2)}, u32[]{:S(2)}) collective-permute-start(f32[1,4224]{1,0:T(1,128)S(1)} %pad_maximum_fusion.6), channel_id=1, source_target_pairs={{0,4},{1,5},{2,6},{3,7},{4,0},{5,1},{6,2},{7,3},{8,12},{9,13},{10,... | collective-permute-start | bytes 50696 | tf_op jit(solution)/shard_map/ppermute | solution.py:397
  196.0 2.7 %collective-permute-start.29 = (f32[1,4224]{1,0:T(1,128)S(1)}, f32[1,4224]{1,0:T(1,128)S(1)}, u32[]{:S(2)}, u32[]{:S(2)}) collective-permute-start(f32[1,4224]{1,0:T(1,128)S(1)} %pad_maximum_fusion.6), channel_id=1, source_target_pairs={{0,6},{1,7},{2,0},{3,1},{4,2},{5,3},{6,4},{7,5},{8,14},{9,15},{10,... | collective-permute-start | bytes 50696 | tf_op jit(solution)/shard_map/ppermute | solution.py:397
  201.2 1.6 reshape.142
  202.8 1.4 collective-permute-done.27
  204.3 3.8 %collective-permute-start.32 = (f32[4096]{0:T(1024)S(1)}, f32[4096]{0:T(1024)S(1)}, u32[]{:S(2)}, u32[]{:S(2)}) collective-permute-start(f32[4096]{0:T(1024)S(1)} %bitcast.86), channel_id=1, source_target_pairs={{0,8},{1,9},{2,10},{3,11},{4,12},{5,13},{6,14},{7,15},{8,0},{9,1},... | collective-permute-start | bytes 49160 | tf_op jit(solution)/shard_map/ppermute | solution.py:590
  208.2 2.0 convert_reduce_fusion
  210.9 5.0 %join.1 = bf16[512,2,896]{2,1,0:T(2,128)(2,1)} custom-call(bf16[512,896]{1,0:T(8,128)(2,1)} %contract_pair.6.g0, bf16[512,896]{1,0:T(8,128)(2,1)} %collective-permute-done.31.g1, bf16[512,896]{1,0:T(8,128)(2,1)} %contract_pair.7.u0, bf16[512,896]{1,0:T(8,128)(2,1)} %collective-permute-done.23.u1), custom_call_target="tpu_custom_call" | custom-call | flops 917504 | bytes 5505024 | tf_op jit(solution)/shard_map/join/pallas_call | solution.py:372
  216.5 2.6 %collective-permute-done.30 = bf16[2,16,4096]{2,1,0:T(8,128)(2,1)S(1)} collective-permute-done((bf16[2,16,4096]{2,1,0:T(8,128)(2,1)S(1)}, bf16[2,16,4096]{2,1,0:T(8,128)(2,1)S(1)}, u32[]{:S(2)}, u32[]{:S(2)}) %collective-permute-start.30) | collective-permute-done | bytes 262176 | tf_op jit(solution)/shard_map/ppermute | solution.py:586
  (126 shorter events, 24.6 us)
Async XLA Ops:
  3.2 37.2 %all-to-all-start = ((bf16[8,2,16,4096]{3,2,1,0:T(8,128)(2,1)}), bf16[8,2,16,4096]{3,2,1,0:T(8,128)(2,1)S(1)}, u32[]{:S(2)}, u32[]{:S(2)}) async-start(bf16[8,2,16,4096]{3,2,1,0:T(8,128)(2,1)} %broadcast_in_dim.16), calls=%async_computation | async-start | bytes 4194304 | tf_op jit(solution)/shard_map/all_to_all | solution.py:401
  11.0 16.8 %copy-start.11 = (bf16[16,4096]{1,0:T(8,128)(2,1)S(1)}, bf16[16,4096]{1,0:T(8,128)(2,1)}, u32[]{:S(2)}) copy-start(bf16[16,4096]{1,0:T(8,128)(2,1)} %param.13) | copy-start | bytes 393220
  11.1 16.8 %copy-start.5 = (bf16[16,4096]{1,0:T(8,128)(2,1)S(1)}, bf16[16,4096]{1,0:T(8,128)(2,1)}, u32[]{:S(2)}) copy-start(bf16[16,4096]{1,0:T(8,128)(2,1)} %param.7) | copy-start | bytes 393220
  11.1 17.8 %copy-start.12 = (f32[4096]{0:T(1024)S(1)}, f32[4096]{0:T(1024)}, u32[]{:S(2)}) copy-start(f32[4096]{0:T(1024)} %param.10) | copy-start | bytes 49156
  31.0 5.5 %collective-permute-start = (bf16[32,1024]{1,0:T(8,128)(2,1)S(1)}, bf16[32,1024]{1,0:T(8,128)(2,1)S(1)}, u32[]{:S(2)}, u32[]{:S(2)}) collective-permute-start(bf16[32,1024]{1,0:T(8,128)(2,1)S(1)} %bitcast.88), channel_id=1, source_target_pairs={{0,16},{16,32},{32,48},{48,0},{64,80},{80,96},{96,112},{112,64},{1... | collective-permute-start | bytes 196616 | tf_op jit(solution)/shard_map/ppermute | solution.py:418
  32.6 4.8 %collective-permute-start.1 = (bf16[32,1024]{1,0:T(8,128)(2,1)S(1)}, bf16[32,1024]{1,0:T(8,128)(2,1)S(1)}, u32[]{:S(2)}, u32[]{:S(2)}) collective-permute-start(bf16[32,1024]{1,0:T(8,128)(2,1)S(1)} %bitcast.89), channel_id=1, source_target_pairs={{0,48},{16,0},{32,16},{48,32},{64,112},{80,64},{96,80},{112,96},{1... | collective-permute-start | bytes 196616 | tf_op jit(solution)/shard_map/ppermute | solution.py:418
  34.4 5.8 %collective-permute-start.2 = (bf16[32,1024]{1,0:T(8,128)(2,1)S(1)}, bf16[32,1024]{1,0:T(8,128)(2,1)S(1)}, u32[]{:S(2)}, u32[]{:S(2)}) collective-permute-start(bf16[32,1024]{1,0:T(8,128)(2,1)S(1)} %bitcast.90), channel_id=1, source_target_pairs={{0,32},{16,48},{32,0},{48,16},{64,96},{80,112},{96,64},{112,80},{1... | collective-permute-start | bytes 196616 | tf_op jit(solution)/shard_map/ppermute | solution.py:418
  41.7 8.3 %collective-permute-start.3 = (bf16[8,2,16,4096]{3,2,1,0:T(8,128)(2,1)S(1)}, bf16[8,2,16,4096]{3,2,1,0:T(8,128)(2,1)}, u32[]{:S(2)}, u32[]{:S(2)}) collective-permute-start(bf16[8,2,16,4096]{3,2,1,0:T(8,128)(2,1)S(1)} %all-to-all-done.own_ref), channel_id=1, source_target_pairs={{0,1},{1,0},{2,3},{3,2},{4,5},{5,4},{6,7},{7,6},{8,9},{9,8},{10,11... | collective-permute-start | bytes 6291464 | tf_op jit(solution)/shard_map/ppermute | solution.py:413
  42.8 25.2 %all-to-all-start.1 = ((bf16[8,64,1024]{2,1,0:T(8,128)(2,1)}), bf16[8,64,1024]{2,1,0:T(8,128)(2,1)}, u32[]{:S(2)}, u32[]{:S(2)}) async-start(bf16[8,64,1024]{2,1,0:T(8,128)(2,1)} %broadcast_in_dim.36), calls=%async_computation.1 | async-start | bytes 2097152 | tf_op jit(solution)/shard_map/all_to_all | solution.py:401
  67.9 15.9 %collective-permute-start.6 = (bf16[8,4,16,1024]{3,2,1,0:T(8,128)(2,1)}, bf16[8,4,16,1024]{3,2,1,0:T(8,128)(2,1)}, u32[]{:S(2)}, u32[]{:S(2)}) collective-permute-start(bf16[8,4,16,1024]{3,2,1,0:T(8,128)(2,1)} %bitcast.13.own_ref), channel_id=1, source_target_pairs={{0,1},{1,0},{2,3},{3,2},{4,5},{5,4},{6,7},{7,6},{8,9},{9,8},{10,11... | collective-permute-start | bytes 3145736 | tf_op jit(solution)/shard_map/ppermute | solution.py:413
  67.9 15.8 %collective-permute-start.4 = (bf16[256,896]{1,0:T(8,128)(2,1)}, bf16[256,896]{1,0:T(8,128)(2,1)S(1)}, u32[]{:S(2)}, u32[]{:S(2)}) collective-permute-start(bf16[256,896]{1,0:T(8,128)(2,1)} %get-tuple-element.121.p0.hidden_ref), channel_id=1, source_target_pairs={{0,16},{16,32},{32,48},{48,0},{64,80},{80,96},{96,112},{112,64},{1... | collective-permute-start | bytes 1376264 | tf_op jit(solution)/shard_map/ppermute | solution.py:418
  68.2 15.6 %collective-permute-start.5 = (bf16[256,896]{1,0:T(8,128)(2,1)}, bf16[256,896]{1,0:T(8,128)(2,1)S(1)}, u32[]{:S(2)}, u32[]{:S(2)}) collective-permute-start(bf16[256,896]{1,0:T(8,128)(2,1)} %get-tuple-element.121.p0.hidden_ref), channel_id=1, source_target_pairs={{0,48},{16,0},{32,16},{48,32},{64,112},{80,64},{96,80},{112,96},{1... | collective-permute-start | bytes 1376264 | tf_op jit(solution)/shard_map/ppermute | solution.py:418
  72.3 27.8 %all-to-all-start.2 = ((bf16[8,64,1024]{2,1,0:T(8,128)(2,1)}), bf16[8,64,1024]{2,1,0:T(8,128)(2,1)S(1)}, u32[]{:S(2)}, u32[]{:S(2)}) async-start(bf16[8,64,1024]{2,1,0:T(8,128)(2,1)} %broadcast_in_dim.38), calls=%async_computation.2 | async-start | bytes 2097152 | tf_op jit(solution)/shard_map/all_to_all | solution.py:401
  75.8 13.9 %copy-start.15 = (f32[32,128]{1,0:T(8,128)S(1)}, f32[32,128]{1,0:T(8,128)}, u32[]{:S(2)}) copy-start(f32[32,128]{1,0:T(8,128)} %get-tuple-element.116) | copy-start | bytes 49156
  84.5 15.6 %collective-permute-start.7 = (bf16[256,896]{1,0:T(8,128)(2,1)}, bf16[256,896]{1,0:T(8,128)(2,1)}, u32[]{:S(2)}, u32[]{:S(2)}) collective-permute-start(bf16[256,896]{1,0:T(8,128)(2,1)} %get-tuple-element.121.p0.hidden_ref), channel_id=1, source_target_pairs={{0,32},{16,48},{32,0},{48,16},{64,96},{80,112},{96,64},{112,80},{1... | collective-permute-start | bytes 1376264 | tf_op jit(solution)/shard_map/ppermute | solution.py:418
  85.1 23.3 %collective-permute-start.8 = (bf16[256,896]{1,0:T(8,128)(2,1)}, bf16[256,896]{1,0:T(8,128)(2,1)S(1)}, u32[]{:S(2)}, u32[]{:S(2)}) collective-permute-start(bf16[256,896]{1,0:T(8,128)(2,1)} %get-tuple-element.127.gate_ref.p0), channel_id=1, source_target_pairs={{0,16},{16,32},{32,48},{48,0},{64,80},{80,96},{96,112},{112,64},{1... | collective-permute-start | bytes 1376264 | tf_op jit(solution)/shard_map/ppermute | solution.py:418
  86.2 22.3 %collective-permute-start.9 = (bf16[256,896]{1,0:T(8,128)(2,1)}, bf16[256,896]{1,0:T(8,128)(2,1)}, u32[]{:S(2)}, u32[]{:S(2)}) collective-permute-start(bf16[256,896]{1,0:T(8,128)(2,1)} %get-tuple-element.127.gate_ref.p0), channel_id=1, source_target_pairs={{0,48},{16,0},{32,16},{48,32},{64,112},{80,64},{96,80},{112,96},{1... | collective-permute-start | bytes 1376264 | tf_op jit(solution)/shard_map/ppermute | solution.py:418
  90.3 20.3 %copy-start.2 = (bf16[256,896]{1,0:T(8,128)(2,1)S(1)}, bf16[256,896]{1,0:T(8,128)(2,1)}, u32[]{:S(2)}) copy-start(bf16[256,896]{1,0:T(8,128)(2,1)} %get-tuple-element.127.gate_ref.p0) | copy-start | bytes 1376260
  100.1 17.6 %copy-start.1 = (bf16[8,64,1024]{2,1,0:T(8,128)(2,1)}, bf16[8,64,1024]{2,1,0:T(8,128)(2,1)S(1)}, u32[]{:S(2)}) copy-start(bf16[8,64,1024]{2,1,0:T(8,128)(2,1)S(1)} %all-to-all-done.2) | copy-start | bytes 3145732
  110.6 7.2 %collective-permute-start.13 = (f32[1,4224]{1,0:T(1,128)S(1)}, f32[1,4224]{1,0:T(1,128)S(1)}, u32[]{:S(2)}, u32[]{:S(2)}) collective-permute-start(f32[1,4224]{1,0:T(1,128)S(1)} %concatenate.16), channel_id=1, source_target_pairs={{0,1},{1,0},{2,3},{3,2},{4,5},{5,4},{6,7},{7,6},{8,9},{9,8},{10,11... | collective-permute-start | bytes 50696 | tf_op jit(solution)/shard_map/ppermute | solution.py:413
  110.6 14.5 %collective-permute-start.10 = (bf16[256,896]{1,0:T(8,128)(2,1)S(1)}, bf16[256,896]{1,0:T(8,128)(2,1)}, u32[]{:S(2)}, u32[]{:S(2)}) collective-permute-start(bf16[256,896]{1,0:T(8,128)(2,1)S(1)} %copy-done.2), channel_id=1, source_target_pairs={{0,32},{16,48},{32,0},{48,16},{64,96},{80,112},{96,64},{112,80},{1... | collective-permute-start | bytes 1376264 | tf_op jit(solution)/shard_map/ppermute | solution.py:418
  111.3 13.9 %collective-permute-start.11 = (bf16[8,4,16,1024]{3,2,1,0:T(8,128)(2,1)S(1)}, bf16[8,4,16,1024]{3,2,1,0:T(8,128)(2,1)}, u32[]{:S(2)}, u32[]{:S(2)}) collective-permute-start(bf16[8,4,16,1024]{3,2,1,0:T(8,128)(2,1)S(1)} %bitcast.64), channel_id=1, source_target_pairs={{0,1},{1,0},{2,3},{3,2},{4,5},{5,4},{6,7},{7,6},{8,9},{9,8},{10,11... | collective-permute-start | bytes 3145736 | tf_op jit(solution)/shard_map/ppermute | solution.py:413
  111.5 13.7 %collective-permute-start.12 = (bf16[128,4096]{1,0:T(8,128)(2,1)}, bf16[128,4096]{1,0:T(8,128)(2,1)}, u32[]{:S(2)}, u32[]{:S(2)}) collective-permute-start(bf16[128,4096]{1,0:T(8,128)(2,1)} %get-tuple-element.114), channel_id=1, source_target_pairs={{0,1},{1,0},{2,3},{3,2},{4,5},{5,4},{6,7},{7,6},{8,9},{9,8},{10,11... | collective-permute-start | bytes 3145736 | tf_op jit(solution)/shard_map/ppermute | solution.py:413
  117.7 8.5 %copy-start.3 = (bf16[256,896]{1,0:T(8,128)(2,1)S(1)}, bf16[256,896]{1,0:T(8,128)(2,1)}, u32[]{:S(2)}) copy-start(bf16[256,896]{1,0:T(8,128)(2,1)} %get-tuple-element.143.up_ref.p0) | copy-start | bytes 1376260
  118.5 3.9 %collective-permute-start.14 = (f32[1,4224]{1,0:T(1,128)S(1)}, f32[1,4224]{1,0:T(1,128)S(1)}, u32[]{:S(2)}, u32[]{:S(2)}) collective-permute-start(f32[1,4224]{1,0:T(1,128)S(1)} %pad_maximum_fusion.4), channel_id=1, source_target_pairs={{0,64},{16,80},{32,96},{48,112},{64,0},{80,16},{96,32},{112,48},{1... | collective-permute-start | bytes 50696 | tf_op jit(solution)/shard_map/ppermute | solution.py:513
  125.2 22.2 %collective-permute-start.15 = (bf16[448,1024]{1,0:T(8,128)(2,1)}, bf16[448,1024]{1,0:T(8,128)(2,1)}, u32[]{:S(2)}, u32[]{:S(2)}) collective-permute-start(bf16[448,1024]{1,0:T(8,128)(2,1)} %get-tuple-element.119), channel_id=1, source_target_pairs={{0,64},{16,80},{32,96},{48,112},{64,0},{80,16},{96,32},{112,48},{1... | collective-permute-start | bytes 2752520 | tf_op jit(solution)/shard_map/ppermute | solution.py:528
  126.2 13.0 %collective-permute-start.16 = (bf16[256,896]{1,0:T(8,128)(2,1)S(1)}, bf16[256,896]{1,0:T(8,128)(2,1)S(1)}, u32[]{:S(2)}, u32[]{:S(2)}) collective-permute-start(bf16[256,896]{1,0:T(8,128)(2,1)S(1)} %copy-done.3), channel_id=1, source_target_pairs={{0,16},{16,32},{32,48},{48,0},{64,80},{80,96},{96,112},{112,64},{1... | collective-permute-start | bytes 1376264 | tf_op jit(solution)/shard_map/ppermute | solution.py:418
  126.2 13.0 %collective-permute-start.17 = (bf16[256,896]{1,0:T(8,128)(2,1)S(1)}, bf16[256,896]{1,0:T(8,128)(2,1)S(1)}, u32[]{:S(2)}, u32[]{:S(2)}) collective-permute-start(bf16[256,896]{1,0:T(8,128)(2,1)S(1)} %copy-done.3), channel_id=1, source_target_pairs={{0,48},{16,0},{32,16},{48,32},{64,112},{80,64},{96,80},{112,96},{1... | collective-permute-start | bytes 1376264 | tf_op jit(solution)/shard_map/ppermute | solution.py:418
  139.2 12.3 %copy-start.8 = (bf16[256,896]{1,0:T(8,128)(2,1)}, bf16[256,896]{1,0:T(8,128)(2,1)S(1)}, u32[]{:S(2)}) copy-start(bf16[256,896]{1,0:T(8,128)(2,1)S(1)} %collective-permute-done.16.p1) | copy-start | bytes 1376260
  139.2 12.3 %copy-start.9 = (bf16[256,896]{1,0:T(8,128)(2,1)}, bf16[256,896]{1,0:T(8,128)(2,1)S(1)}, u32[]{:S(2)}) copy-start(bf16[256,896]{1,0:T(8,128)(2,1)S(1)} %collective-permute-done.17.p2) | copy-start | bytes 1376260
  147.4 4.1 %collective-permute-start.18 = (bf16[128,4096]{1,0:T(8,128)(2,1)}, bf16[128,4096]{1,0:T(8,128)(2,1)}, u32[]{:S(2)}, u32[]{:S(2)}) collective-permute-start(bf16[128,4096]{1,0:T(8,128)(2,1)} %get-tuple-element.132), channel_id=1, source_target_pairs={{0,1},{1,0},{2,3},{3,2},{4,5},{5,4},{6,7},{7,6},{8,9},{9,8},{10,11... | collective-permute-start | bytes 3145736 | tf_op jit(solution)/shard_map/ppermute | solution.py:413
  151.5 15.2 %collective-permute-start.19 = (bf16[256,896]{1,0:T(8,128)(2,1)S(1)}, bf16[256,896]{1,0:T(8,128)(2,1)S(1)}, u32[]{:S(2)}, u32[]{:S(2)}) collective-permute-start(bf16[256,896]{1,0:T(8,128)(2,1)S(1)} %copy-done.3), channel_id=1, source_target_pairs={{0,32},{16,48},{32,0},{48,16},{64,96},{80,112},{96,64},{112,80},{1... | collective-permute-start | bytes 1376264 | tf_op jit(solution)/shard_map/ppermute | solution.py:418
  152.8 13.8 %collective-permute-start.20 = (f32[1,4224]{1,0:T(1,128)S(1)}, f32[1,4224]{1,0:T(1,128)S(1)}, u32[]{:S(2)}, u32[]{:S(2)}) collective-permute-start(f32[1,4224]{1,0:T(1,128)S(1)} %pad_maximum_fusion.5), channel_id=1, source_target_pairs={{0,32},{16,48},{32,0},{48,16},{64,96},{80,112},{96,64},{112,80},{1... | collective-permute-start | bytes 50696 | tf_op jit(solution)/shard_map/ppermute | solution.py:418
  155.2 11.5 %collective-permute-start.21 = (f32[1,4224]{1,0:T(1,128)S(1)}, f32[1,4224]{1,0:T(1,128)S(1)}, u32[]{:S(2)}, u32[]{:S(2)}) collective-permute-start(f32[1,4224]{1,0:T(1,128)S(1)} %pad_maximum_fusion.5), channel_id=1, source_target_pairs={{0,16},{16,32},{32,48},{48,0},{64,80},{80,96},{96,112},{112,64},{1... | collective-permute-start | bytes 50696 | tf_op jit(solution)/shard_map/ppermute | solution.py:418
  155.2 11.5 %collective-permute-start.22 = (f32[1,4224]{1,0:T(1,128)S(1)}, f32[1,4224]{1,0:T(1,128)S(1)}, u32[]{:S(2)}, u32[]{:S(2)}) collective-permute-start(f32[1,4224]{1,0:T(1,128)S(1)} %pad_maximum_fusion.5), channel_id=1, source_target_pairs={{0,48},{16,0},{32,16},{48,32},{64,112},{80,64},{96,80},{112,96},{1... | collective-permute-start | bytes 50696 | tf_op jit(solution)/shard_map/ppermute | solution.py:418
  158.5 52.4 %collective-permute-start.31 = (bf16[512,896]{1,0:T(8,128)(2,1)}, bf16[512,896]{1,0:T(8,128)(2,1)}, u32[]{:S(2)}, u32[]{:S(2)}) collective-permute-start(bf16[512,896]{1,0:T(8,128)(2,1)} %contract_pair.4), channel_id=1, source_target_pairs={{0,64},{16,80},{32,96},{48,112},{64,0},{80,16},{96,32},{112,48},{1... | collective-permute-start | bytes 2752520 | tf_op jit(solution)/shard_map/ppermute | solution.py:542
  171.6 32.7 %collective-permute-start.23 = (bf16[512,896]{1,0:T(8,128)(2,1)}, bf16[512,896]{1,0:T(8,128)(2,1)}, u32[]{:S(2)}, u32[]{:S(2)}) collective-permute-start(bf16[512,896]{1,0:T(8,128)(2,1)} %contract_pair.5), channel_id=1, source_target_pairs={{0,64},{16,80},{32,96},{48,112},{64,0},{80,16},{96,32},{112,48},{1... | collective-permute-start | bytes 2752520 | tf_op jit(solution)/shard_map/ppermute | solution.py:559
  172.6 31.7 %all-to-all-start.3 = ((bf16[4,64,4096]{2,1,0:T(8,128)(2,1)}), bf16[4,64,4096]{2,1,0:T(8,128)(2,1)}, u32[]{:S(2)}, u32[]{:S(2)}) async-start(bf16[4,64,4096]{2,1,0:T(8,128)(2,1)} %pack.1), calls=%async_computation.3 | async-start | bytes 4194304 | tf_op jit(solution)/shard_map/all_to_all | solution.py:405
  178.7 13.5 %collective-permute-start.24 = (bf16[112,1024]{1,0:T(8,128)(2,1)S(1)}, bf16[112,1024]{1,0:T(8,128)(2,1)S(1)}, u32[]{:S(2)}, u32[]{:S(2)}) collective-permute-start(bf16[112,1024]{1,0:T(8,128)(2,1)S(1)} %get-tuple-element.180), channel_id=1, source_target_pairs={{0,16},{16,32},{32,48},{48,0},{64,80},{80,96},{96,112},{112,64},{1... | collective-permute-start | bytes 688136 | tf_op jit(solution)/shard_map/ppermute | solution.py:418
  178.8 16.6 %collective-permute-start.25 = (bf16[112,1024]{1,0:T(8,128)(2,1)S(1)}, bf16[112,1024]{1,0:T(8,128)(2,1)S(1)}, u32[]{:S(2)}, u32[]{:S(2)}) collective-permute-start(bf16[112,1024]{1,0:T(8,128)(2,1)S(1)} %get-tuple-element.179), channel_id=1, source_target_pairs={{0,32},{16,48},{32,0},{48,16},{64,96},{80,112},{96,64},{112,80},{1... | collective-permute-start | bytes 688136 | tf_op jit(solution)/shard_map/ppermute | solution.py:418
  180.9 15.1 %collective-permute-start.26 = (bf16[112,1024]{1,0:T(8,128)(2,1)S(1)}, bf16[112,1024]{1,0:T(8,128)(2,1)S(1)}, u32[]{:S(2)}, u32[]{:S(2)}) collective-permute-start(bf16[112,1024]{1,0:T(8,128)(2,1)S(1)} %get-tuple-element.178), channel_id=1, source_target_pairs={{0,48},{16,0},{32,16},{48,32},{64,112},{80,64},{96,80},{112,96},{1... | collective-permute-start | bytes 688136 | tf_op jit(solution)/shard_map/ppermute | solution.py:418
  192.2 12.0 %collective-permute-start.27 = (f32[1,4224]{1,0:T(1,128)S(1)}, f32[1,4224]{1,0:T(1,128)S(1)}, u32[]{:S(2)}, u32[]{:S(2)}) collective-permute-start(f32[1,4224]{1,0:T(1,128)S(1)} %pad_maximum_fusion.6), channel_id=1, source_target_pairs={{0,4},{1,5},{2,6},{3,7},{4,0},{5,1},{6,2},{7,3},{8,12},{9,13},{10,... | collective-permute-start | bytes 50696 | tf_op jit(solution)/shard_map/ppermute | solution.py:397
  195.4 8.9 %collective-permute-start.28 = (f32[1,4224]{1,0:T(1,128)S(1)}, f32[1,4224]{1,0:T(1,128)S(1)}, u32[]{:S(2)}, u32[]{:S(2)}) collective-permute-start(f32[1,4224]{1,0:T(1,128)S(1)} %pad_maximum_fusion.6), channel_id=1, source_target_pairs={{0,2},{1,3},{2,4},{3,5},{4,6},{5,7},{6,0},{7,1},{8,10},{9,11},{10,... | collective-permute-start | bytes 50696 | tf_op jit(solution)/shard_map/ppermute | solution.py:397
  196.0 8.3 %collective-permute-start.29 = (f32[1,4224]{1,0:T(1,128)S(1)}, f32[1,4224]{1,0:T(1,128)S(1)}, u32[]{:S(2)}, u32[]{:S(2)}) collective-permute-start(f32[1,4224]{1,0:T(1,128)S(1)} %pad_maximum_fusion.6), channel_id=1, source_target_pairs={{0,6},{1,7},{2,0},{3,1},{4,2},{5,3},{6,4},{7,5},{8,14},{9,15},{10,... | collective-permute-start | bytes 50696 | tf_op jit(solution)/shard_map/ppermute | solution.py:397
  204.3 11.6 %collective-permute-start.32 = (f32[4096]{0:T(1024)S(1)}, f32[4096]{0:T(1024)S(1)}, u32[]{:S(2)}, u32[]{:S(2)}) collective-permute-start(f32[4096]{0:T(1024)S(1)} %bitcast.86), channel_id=1, source_target_pairs={{0,8},{1,9},{2,10},{3,11},{4,12},{5,13},{6,14},{7,15},{8,0},{9,1},... | collective-permute-start | bytes 49160 | tf_op jit(solution)/shard_map/ppermute | solution.py:590
  210.2 8.9 %collective-permute-start.30 = (bf16[2,16,4096]{2,1,0:T(8,128)(2,1)S(1)}, bf16[2,16,4096]{2,1,0:T(8,128)(2,1)S(1)}, u32[]{:S(2)}, u32[]{:S(2)}) collective-permute-start(bf16[2,16,4096]{2,1,0:T(8,128)(2,1)S(1)} %fusion.11), channel_id=1, source_target_pairs={{0,8},{1,9},{2,10},{3,11},{4,12},{5,13},{6,14},{7,15},{8,0},{9,1},... | collective-permute-start | bytes 786440 | tf_op jit(solution)/shard_map/ppermute | solution.py:586
  210.9 8.3 %copy-start.6 = (bf16[16,4096]{1,0:T(8,128)(2,1)S(1)}, bf16[16,4096]{1,0:T(8,128)(2,1)}, u32[]{:S(2)}) copy-start(bf16[16,4096]{1,0:T(8,128)(2,1)} %param.7) | copy-start | bytes 393220
  210.9 8.3 %copy-start.13 = (f32[4096]{0:T(1024)S(1)}, f32[4096]{0:T(1024)}, u32[]{:S(2)}) copy-start(f32[4096]{0:T(1024)} %param.10) | copy-start | bytes 49156
  (7 other events, 25.5 us)

commit v3 on v2

--- a/solution.py
+++ b/solution.py
@@ -226,7 +226,7 @@
         out_specs=[strip, strip],
         out_shape=[jax.ShapeDtypeStruct((half, features), BF16)] * 2,
         compiler_params=options(62),
-        cost_estimate=cost(rows * features * width, down.size * 2),
+        cost_estimate=cost(rows * features * width // 50, down.size // 25),
         name="out_shares",
     )(hidden, down)
 
@@ -271,7 +271,7 @@
     )(d_gate, d_up, paired, paired, own, other, inverse)
 
 
-def pack_kernel(out_own, out_got, norm_own, norm_got, parts_ref):
+def pack_kernel(out_own, out_got, norm_own, norm_got, gain_ref, parts_ref):
     across = parts_ref.shape[0]
     rows = out_own.shape[0] // (2 * across)
     place = 0
@@ -282,22 +282,28 @@
                 base = (h * across + y) * rows
                 parts_ref[y, place : place + rows] = total[base : base + rows]
             place += rows
-
-
-def pack(out_own, out_got, norm_own, norm_got, rows, depth=1024):
+    gain = gain_ref[...]
+    upper = gain.astype(BF16)
+    lower = (gain - upper.astype(F32)).astype(BF16)
+    both = jnp.concatenate([upper, lower])
+    for y in range(across):
+        parts_ref[y, place:] = both
+
+
+def pack(out_own, out_got, norm_own, norm_got, gain, rows, depth=1024):
     half, features = out_own.shape
     strip = pl.BlockSpec((half, depth), lambda i: (0, i))
-    total = 4 * rows
+    total = 4 * rows + 2
     return pl.pallas_call(
         pack_kernel,
         grid=(features // depth,),
-        in_specs=[strip] * 4,
+        in_specs=[strip] * 4 + [pl.BlockSpec((1, depth), lambda i: (0, i))],
         out_specs=pl.BlockSpec((4, total, depth), lambda i: (0, 0, i)),
         out_shape=jax.ShapeDtypeStruct((4, total, features), BF16),
         compiler_params=options(62),
-        cost_estimate=cost(2 * half * features, 12 * half * features),
+        cost_estimate=cost(half * features // 25, half * features // 4),
         name="pack",
-    )(out_own, out_got, norm_own, norm_got)
+    )(out_own, out_got, norm_own, norm_got, gain)
 
 
 def slice_block(own_ref, other_ref):
@@ -335,12 +341,12 @@
     out_ref[...] = (total * scale_ref[0]).astype(BF16)
 
 
-def contract(kernel, scale, pieces, own, other, first, count, depth=256):
+def contract(kernel, scale, pieces, own, other, kind, first, count, share=1, depth=256):
     rows, width = pieces[0].shape
     piece = pl.BlockSpec((rows, width), lambda i, at: (0, 0))
     steps = count // depth
-    block = (own.shape[0], 4, own.shape[2], depth)
-    cut = pl.BlockSpec(block, lambda i, at: (0, 0, 0, at[0] * steps + i))
+    block = (own.shape[0], 4, None, own.shape[3], depth)
+    cut = pl.BlockSpec(block, lambda i, at: (0, 0, kind, 0, at[0] * steps + i))
     if kernel is pair_kernel:
         shape, spec = (count, width), pl.BlockSpec((depth, width), lambda i, at: (i, 0))
     else:
@@ -356,7 +362,7 @@
         ),
         out_shape=jax.ShapeDtypeStruct(shape, BF16),
         compiler_params=options(62),
-        cost_estimate=cost(4 * rows * width * count, 8 * rows * (width + count)),
+        cost_estimate=cost(4 * rows * width * count // share, 8 * rows * (width + count) // share),
         name="contract_" + ("pair" if kernel is pair_kernel else "down"),
     )(first.reshape(1).astype(jnp.int32), scale, *pieces, own, other)
 
@@ -465,101 +471,80 @@
     )
     rows_own = after(rows_own, sliced)
     rows_other = swap_core(rows_own)
-    sliced = after(sliced, rows_own).reshape(4, 2, own_rows, 2 * span)
-
-    def gather_slices(kind):
-        spread = gather_ring(sliced[:, kind].reshape(4 * own_rows, 2 * span))
-        return spread.reshape(8, 4, own_rows, 2 * span)
-
-    g_own = gather_slices(1)
 
     hidden, slope, silu, inverse, act_peak = forward(
         act_history, rows_own, rows_other, norm_gain.reshape(1, features), paired
     )
-    hidden, g_own = together(hidden, g_own)
-
-    g_other = swap_core(g_own)
+    hidden, sliced = together(hidden, sliced)
+
+    slices_own = gather_ring(sliced.reshape(8 * own_rows, 2 * span))
     hidden_left, hidden_right = send_x(hidden, 1), send_x(hidden, -1)
     d_gate, d_up, grad_peak = backward(grad_history, rows_own, rows_other, down_proj, slope, silu)
-    hidden, hidden_left, hidden_right, g_other, d_gate, d_up = together(
-        hidden, hidden_left, hidden_right, g_other, d_gate, d_up
-    )
-
-    q_own = gather_slices(0)
+    hidden, hidden_left, hidden_right, d_gate, d_up = together(
+        hidden, hidden_left, hidden_right, d_gate, d_up
+    )
+
     hidden_far = send_x(hidden, 2)
     gate_left, gate_right = send_x(d_gate, 1), send_x(d_gate, -1)
     norm_own, norm_other, gain_share = normed_shares(
         d_gate, d_up, paired, rows_own, rows_other, inverse
     )
-    hidden, hidden_far, gate_left, gate_right, q_own, norm_own, norm_other, gain_share = together(
-        hidden, hidden_far, gate_left, gate_right, q_own, norm_own, norm_other, gain_share
-    )
-    d_gate, d_up, gain_share = together(d_gate, d_up, gain_share)
-    hidden_all = (hidden, hidden_left, hidden_right, hidden_far)
-
-    def merge(first, second):
-        total = first[:, :features] + second[:, :features]
-        peak = jnp.maximum(first[:, features:], second[:, features:])
-        return jnp.concatenate([total, peak], axis=1)
-
-    q_other = swap_core(q_own)
-    norm_got = swap_core(norm_other)
-    gate_far = send_x(d_gate, 2)
+    out_own, out_other = out_shares(after(hidden, norm_own), down_proj)
+    gain_share = gain_share + swap_core(gain_share)
     peaks = jnp.concatenate(
         [jnp.full((1, 64), jnp.max(act_peak)), jnp.full((1, 64), jnp.max(grad_peak))], axis=1
     )
-    small = jnp.concatenate([gain_share, peaks], axis=1)
-    small = merge(small, swap_core(small))
-    small = merge(small, lax.ppermute(small, "dp", ZPAIR))
+    small = jnp.concatenate([gain_share.reshape(-1, 128), peaks])
+    small = jnp.broadcast_to(small[None], (groups,) + small.shape)
+    hidden, hidden_far, gate_left, gate_right, norm_own, norm_other, small, d_gate, d_up = together(
+        hidden, hidden_far, gate_left, gate_right, norm_own, norm_other, small, d_gate, d_up
+    )
+    slices_own, norm_other, out_own, out_other = together(
+        slices_own, norm_other, out_own, out_other
+    )
+    slices_own = slices_own.reshape(8, 4, 2, own_rows, 2 * span)
+    slices_other = swap_core(slices_own)
+    hidden_all = (hidden, hidden_left, hidden_right, hidden_far)
+
+    norm_got = swap_core(norm_other)
+    out_got = swap_core(out_other)
+    small = lax.all_to_all(small, "dp", 0, 0, tiled=True)
+    gate_far = send_x(d_gate, 2)
     down_part = contract(
-        down_kernel, down_scale, hidden_all, g_own, g_other, z_lo * 0, 2 * span
+        down_kernel, down_scale, hidden_all, slices_own, slices_other, 1, z_lo * 0, 2 * span
     )
     hand = width // 2
     sent_down = lax.dynamic_slice(down_part, ((1 - z_lo) * hand, 0), (hand, 2 * span))
     kept_down = lax.dynamic_slice(down_part, (z_lo * hand, 0), (hand, 2 * span))
-    sent_down, gate_far, q_other, norm_got, small, d_up, hidden = together(
-        sent_down, gate_far, q_other, norm_got, small, d_up, hidden
+    sent_down, gate_far, norm_got, out_got, small, d_up = together(
+        sent_down, gate_far, norm_got, out_got, small, d_up
     )
     gate_all = (d_gate, gate_left, gate_right, gate_far)
 
-    def pair_part(pieces, place, scale=pair_scale):
-        return contract(pair_kernel, scale, pieces, q_own, q_other, place, span)
+    def pair_part(pieces, place, share=1, scale=pair_scale):
+        return contract(
+            pair_kernel, scale, pieces, slices_own, slices_other, 0, place, span, share
+        )
 
     got_down = lax.ppermute(sent_down, "dp", ZPAIR)
-    up_left, up_right = send_x(d_up, 1), send_x(d_up, -1)
-    out_own, out_other = out_shares(hidden, down_proj)
-    got_down, up_left, up_right, out_own, out_other, d_up, d_gate, norm_own, norm_got, small = (
-        together(
-            got_down, up_left, up_right, out_own, out_other, d_up, d_gate, norm_own, norm_got, small
-        )
-    )
-    out_got = swap_core(out_other)
-    gate_sent = pair_part((d_gate,) + gate_all[1:], 1 - z_lo)
-    gate_sent, out_got, d_up, norm_own, norm_got, small = together(
-        gate_sent, out_got, d_up, norm_own, norm_got, small
+    up_all = (d_up, send_x(d_up, 1), send_x(d_up, -1), send_x(d_up, 2))
+    gate_sent = pair_part(gate_all, 1 - z_lo)
+    gain_sum = jnp.sum(small[:, :-1], axis=0).reshape(1, features)
+    peak = jnp.max(small[:, -1], axis=0)
+    parts = pack(out_own, out_got, norm_own, norm_got, after(gain_sum, gate_sent), own_rows)
+    sums = exchange_y(parts)
+    got_down, up_all, gate_sent, parts, late_scale = together(
+        got_down, up_all, gate_sent, parts, pair_scale
     )
 
     gate_got = lax.ppermute(gate_sent, "dp", ZPAIR)
-    up_far = send_x(d_up, 2)
-    small_far, small_left, small_right = send_x(small, 2), send_x(small, 1), send_x(small, -1)
-    parts = pack(out_own, out_got, norm_own, norm_got, own_rows)
-    up_far, parts, d_up, small, small_far, small_left, small_right = together(
-        up_far, parts, d_up, small, small_far, small_left, small_right
-    )
-    sums = exchange_y(parts)
-
-    up_all = (d_up, up_left, up_right, up_far)
-    up_sent = pair_part(up_all, 1 - z_lo)
-    up_sent, small, small_far, small_left, small_right, kept_down, got_down, late_scale = (
-        together(
-            up_sent, small, small_far, small_left, small_right, kept_down, got_down, pair_scale
-        )
-    )
-    small = merge(merge(small, small_far), merge(small_left, small_right))
+    up_sent = pair_part(up_all, 1 - z_lo, 50, late_scale)
     up_got = lax.ppermute(up_sent, "dp", ZPAIR)
-    small_far, small_left, small_right = send_y(small, 2), send_y(small, 1), send_y(small, -1)
-    gate_kept = pair_part(gate_all, z_lo, late_scale)
-    up_kept = pair_part(up_all, z_lo, late_scale)
+    gate_kept = pair_part(gate_all, z_lo, 50, after(late_scale, up_sent))
+    up_kept = pair_part(up_all, z_lo, 50, after(late_scale, up_sent))
+    gate_got, gate_kept, up_kept, kept_down, got_down = together(
+        gate_got, gate_kept, up_kept, kept_down, got_down
+    )
 
     sum_down = (kept_down.astype(F32) + got_down.astype(F32)).astype(BF16)
     sum_down = sum_down.reshape(4, hand // 4, 2 * span)
@@ -575,19 +560,23 @@
         turned.reshape(4, hand // 4, 2, span).transpose(1, 2, 0, 3).reshape(hand // 4, features)
     )
 
-    up_got, gate_kept, up_kept, grad_down, small, small_far, small_left, small_right, sums = together(
-        up_got, gate_kept, up_kept, grad_down, small, small_far, small_left, small_right, sums
-    )
-    small = merge(merge(small, small_far), merge(small_left, small_right))
+    gate_got, up_got, gate_kept, up_kept, grad_down, sums = together(
+        gate_got, up_got, gate_kept, up_kept, grad_down, sums
+    )
     totals = jnp.sum(sums.astype(F32), axis=0)
-    rows = totals.reshape(2, 2, own_rows, features)
+    rows = totals[: 4 * own_rows].reshape(2, 2, own_rows, features)
     kept = lax.dynamic_index_in_dim(rows, z_hi, 1, keepdims=False)
     sent = lax.dynamic_index_in_dim(rows, 1 - z_hi, 1, keepdims=False).astype(BF16)
-    rows = kept + lax.ppermute(sent, "tensor", ZFAR).astype(F32)
+    gain_sum = totals[4 * own_rows] + totals[4 * own_rows + 1]
+    gain_high = lax.reduce_precision(gain_sum, 8, 7)
+    gain_sent = jnp.stack([gain_high, gain_sum - gain_high]).astype(BF16)
+    sent = jnp.concatenate([sent.reshape(2 * own_rows, features), gain_sent])
+    got = lax.ppermute(sent, "tensor", ZFAR).astype(F32)
+    rows = kept + got[: 2 * own_rows].reshape(kept.shape)
     mlp_out = rows[0].astype(BF16)
     d_normed = rows[1]
-    gain_sum = small[0, :features]
-    grad_gain = (gain_sum + lax.ppermute(gain_sum, "tensor", ZFAR)) * root
+    gain_sent = gain_sent.astype(F32)
+    grad_gain = ((gain_sent[0] + gain_sent[1]) + (got[-2] + got[-1])) * root
     scaled = d_normed * norm_gain
     grad_tokens = (
         inverse_rms * (scaled - unit_rows * jnp.mean(scaled * unit_rows, axis=-1, keepdims=True))
@@ -599,8 +588,8 @@
         grad_gate_up,
         grad_down,
         grad_gain,
-        small[0, features : features + 1],
-        small[0, features + 64 : features + 65],
+        peak[:1],
+        peak[64:65],
     )
 
 

time: 222 us -> 210 us (0.946)
  starting transfers between devices: 65.2 us -> 50.7 us
    ppermute x6 -> x1, starting transfers between devices: 11.4 us -> 2.97 us  [shards(): got = lax.ppermute(sent, 'tensor', ZFAR).astype(F32)]
    ppermute x1, waiting for transfers between devices: 8.19 us -> 0.01 us  [shards(): got_down = lax.ppermute(sent_down, 'dp', ZPAIR)]
    ppermute x18 -> x15, starting transfers between devices: 27.1 us -> 20.1 us  [send_x(): return lax.ppermute(block, 'dp', ring)]
    all_to_all x3 -> x2, waiting for transfers between devices: 5.92 us -> 0.01 us  [exchange(): lax.all_to_all(parts, 'tensor', 0, 0, tiled=True, axis_index_groups=RINGS)]
    ppermute x18 -> x15, waiting for transfers between devices: 22 us -> 27.5 us  [send_x(): return lax.ppermute(block, 'dp', ring)]
    ppermute x1, waiting for transfers between devices: 0.01 us -> 4.73 us  [shards(): gate_got = lax.ppermute(gate_sent, 'dp', ZPAIR)]
    ppermute x6 -> x5, waiting for transfers between devices: 0.02 us -> 4.17 us  [swap_core(): return lax.ppermute(block, 'tensor', CORE)]
    all_to_all x0 -> x1, starting transfers between devices: none -> 4.01 us  [shards(): small = lax.all_to_all(small, 'dp', 0, 0, tiled=True)]
  transfers between devices with their start and end apart: 37 -> 28, of which waited for: 14 -> 14; matrix products, arithmetic and copies ran while one was open for 16% -> 16% of each run, Pallas kernels for 31% -> 27%
where the time goes in v3:
time: 210 us; the launch traced here: 209 us
  Pallas kernels  67.8 us (32%)
  starting transfers between devices  50.7 us (24%)
  waiting for transfers between devices  41.2 us (20%)
  local copies, waits for them, and re-layouts  36.4 us (17%)
  other arithmetic  10.6 us (5%)
  between operations  2.52 us (1%)
    ppermute x15, waiting for transfers between devices, send_x(): return lax.ppermute(block, 'dp', ring)  27.5 us
    pallas_call x5, Pallas kernels, contract(): pl.pallas_call(kernel, grid_spec=pltpu.PrefetchScalarGridSpec(num_scalar_...  22.2 us
    unnamed x40, local copies, waits for them, and re-layouts  20.3 us
    ppermute x15, starting transfers between devices, send_x(): return lax.ppermute(block, 'dp', ring)  20.1 us
    all_to_all x2, starting transfers between devices, exchange(): lax.all_to_all(parts, 'tensor', 0, 0, tiled=True, axis_index_groups=RINGS)  15.3 us
    pallas_call x1, Pallas kernels, forward(): pl.pallas_call(functools.partial(forward_kernel, steps), grid=(steps,), i...  12 us
    pallas_call x1, Pallas kernels, normed_shares(): pl.pallas_call(normed_kernel, grid=(features // depth,), in_specs=[whole(...  9.79 us
    pallas_call x1, Pallas kernels, backward(): pl.pallas_call(functools.partial(backward_kernel, steps), grid=(steps,),...  7.95 us
  transfers between devices with their start and end apart: 28, of which 14 were waited for; matrix products, arithmetic and copies ran while one was open for 16% of the time, Pallas kernels for 27%

profile of v3, /device:TPU:0, one launch (start us, length us, event | category | flops | bytes accessed | tf_op | source)
XLA Modules:
  0.0 209.1 jit_solution(7493661521559409677)
XLA Ops:
  1.6 1.6 broadcast_in_dim.12
  3.2 8.0 %all-to-all-start = ((bf16[8,2,16,4096]{3,2,1,0:T(8,128)(2,1)}), bf16[8,2,16,4096]{3,2,1,0:T(8,128)(2,1)S(1)}, u32[]{:S(2)}, u32[]{:S(2)}) async-start(bf16[8,2,16,4096]{3,2,1,0:T(8,128)(2,1)} %broadcast_in_dim.12), calls=%async_computation | async-start | bytes 4194304 | tf_op jit(solution)/shard_map/all_to_all | solution.py:407
  11.9 16.1 %copy.41 = bf16[512,8,2,896]{3,1,2,0:T(8,128)(2,1)} copy(bf16[512,8,2,896]{3,2,1,0:T(2,128)(2,1)} %bitcast.66) | data formatting | bytes 29360128
  29.3 1.8 dynamic-slice_reduce_fusion.3
  31.2 3.1 %collective-permute-start.2 = (bf16[32,1024]{1,0:T(8,128)(2,1)S(1)}, bf16[32,1024]{1,0:T(8,128)(2,1)S(1)}, u32[]{:S(2)}, u32[]{:S(2)}) collective-permute-start(bf16[32,1024]{1,0:T(8,128)(2,1)S(1)} %bitcast.85), channel_id=1, source_target_pairs={{0,32},{16,48},{32,0},{48,16},{64,96},{80,112},{96,64},{112,80},{1... | collective-permute-start | bytes 196616 | tf_op jit(solution)/shard_map/ppermute | solution.py:424
  35.0 2.7 %collective-permute-start.1 = (bf16[32,1024]{1,0:T(8,128)(2,1)S(1)}, bf16[32,1024]{1,0:T(8,128)(2,1)S(1)}, u32[]{:S(2)}, u32[]{:S(2)}) collective-permute-start(bf16[32,1024]{1,0:T(8,128)(2,1)S(1)} %bitcast.87), channel_id=1, source_target_pairs={{0,48},{16,0},{32,16},{48,32},{64,112},{80,64},{96,80},{112,96},{1... | collective-permute-start | bytes 196616 | tf_op jit(solution)/shard_map/ppermute | solution.py:424
  37.7 2.1 %collective-permute-done = bf16[32,1024]{1,0:T(8,128)(2,1)S(1)} collective-permute-done((bf16[32,1024]{1,0:T(8,128)(2,1)S(1)}, bf16[32,1024]{1,0:T(8,128)(2,1)S(1)}, u32[]{:S(2)}, u32[]{:S(2)}) %collective-permute-start) | collective-permute-done | bytes 65568 | tf_op jit(solution)/shard_map/ppermute | solution.py:424
  39.9 1.3 copy-done
  41.2 4.2 %collective-permute-done.3.other_ref = bf16[8,2,16,4096]{3,2,1,0:T(8,128)(2,1)S(1)} collective-permute-done((bf16[8,2,16,4096]{3,2,1,0:T(8,128)(2,1)S(1)}, bf16[8,2,16,4096]{3,2,1,0:T(8,128)(2,1)S(1)}, u32[]{:S(2)}, u32[]{:S(2)}) %collective-permute-start.3) | collective-permute-done | bytes 2097184 | tf_op jit(solution)/shard_map/ppermute | solution.py:419
  45.4 1.4 copy-done.1
  46.7 12.0 %forward.1 = (bf16[256,896]{1,0:T(8,128)(2,1)}, f32[256,896]{1,0:T(8,128)}, f32[256,896]{1,0:T(8,128)}, f32[256,128]{1,0:T(8,128)}, f32[32,128]{1,0:T(8,128)}) custom-call(f32[1]{0:T(128)S(6)} %copy.47.act_ref, bf16[8,2,16,4096]{3,2,1,0:T(8,128)(2,1)} %copy-done, bf16[8,2,16,4096]{3,2,1,0:T(8,128)(2,1)} %copy-done.1, f32[1,4096]{1,0:T(1,128)} %bitcast.76, ...), custom_call_target="tpu_custom_call" | custom-call | flops 3758096384 | bytes 14680064 | tf_op jit(solution)/shard_map/forward/pallas_call | solution.py:112
  58.8 1.6 broadcast_in_dim.17
  60.4 7.3 %all-to-all-start.1 = ((bf16[8,128,1024]{2,1,0:T(8,128)(2,1)}), bf16[8,128,1024]{2,1,0:T(8,128)(2,1)}, u32[]{:S(2)}, u32[]{:S(2)}) async-start(bf16[8,128,1024]{2,1,0:T(8,128)(2,1)} %broadcast_in_dim.17), calls=%async_computation.1 | async-start | bytes 4194304 | tf_op jit(solution)/shard_map/all_to_all | solution.py:407
  67.7 3.4 %collective-permute-start.5 = (bf16[256,896]{1,0:T(8,128)(2,1)S(1)}, bf16[256,896]{1,0:T(8,128)(2,1)S(1)}, u32[]{:S(2)}, u32[]{:S(2)}) collective-permute-start(bf16[256,896]{1,0:T(8,128)(2,1)S(1)} %copy-done.10), channel_id=1, source_target_pairs={{0,48},{16,0},{32,16},{48,32},{64,112},{80,64},{96,80},{112,96},{1... | collective-permute-start | bytes 1376264 | tf_op jit(solution)/shard_map/ppermute | solution.py:424
  71.7 8.0 %backward.1 = (bf16[256,896]{1,0:T(8,128)(2,1)}, bf16[256,896]{1,0:T(8,128)(2,1)}, f32[8,128]{1,0:T(8,128)}) custom-call(f32[1]{0:T(128)S(6)} %copy.48.history_ref, bf16[8,2,16,4096]{3,2,1,0:T(8,128)(2,1)} %copy-done, bf16[8,2,16,4096]{3,2,1,0:T(8,128)(2,1)} %copy-done.1, bf16[896,4096]{1,0:T(8,128)(2,1)} %down_ref.3, ...), custom_call_target="tpu_custom_call" | custom-call | flops 1879048192 | bytes 7340032 | tf_op jit(solution)/shard_map/backward/pallas_call | solution.py:184
  79.6 1.3 reduce_max.28
  80.9 3.4 %collective-permute-done.4.p1 = bf16[256,896]{1,0:T(8,128)(2,1)S(1)} collective-permute-done((bf16[256,896]{1,0:T(8,128)(2,1)S(1)}, bf16[256,896]{1,0:T(8,128)(2,1)S(1)}, u32[]{:S(2)}, u32[]{:S(2)}) %collective-permute-start.4) | collective-permute-done | bytes 458784 | tf_op jit(solution)/shard_map/ppermute | solution.py:424
  85.5 1.6 collective-permute-start.7
  87.1 9.8 %normed_shares.1 = (bf16[128,4096]{1,0:T(8,128)(2,1)}, bf16[128,4096]{1,0:T(8,128)(2,1)}, f32[1,4096]{1,0:T(1,128)}) custom-call(bf16[256,896]{1,0:T(8,128)(2,1)} %get-tuple-element.96.gate_ref.p0, bf16[256,896]{1,0:T(8,128)(2,1)} %get-tuple-element.114.up_ref.p0, bf16[4096,1792]{1,0:T(8,128)(2,1)} %bitcast.64, bf16[4096,1792]{1,0:T(8,128)(2,1)} %bitcast.65, ...), custom_call_target="tpu_custom_call" | custom-call | flops 3758096384 | bytes 14680064 | tf_op jit(solution)/shard_map/normed_shares/pallas_call | solution.py:253
  98.4 6.4 %out_shares.1 = (bf16[128,4096]{1,0:T(8,128)(2,1)}, bf16[128,4096]{1,0:T(8,128)(2,1)}) custom-call(bf16[256,896]{1,0:T(8,128)(2,1)} %get-tuple-element.92.hidden_ref.p0, bf16[896,4096]{1,0:T(8,128)(2,1)} %down_ref.3), custom_call_target="tpu_custom_call" | custom-call | flops 37580960 | bytes 146800 | tf_op jit(solution)/shard_map/out_shares/pallas_call | solution.py:219
  104.9 1.8 collective-permute-done.6.p3
  106.7 1.3 collective-permute-done.7.p1
  109.2 1.8 collective-permute-start.11
  111.0 4.0 %all-to-all-start.2 = ((f32[8,33,128]{2,1,0:T(8,128)}), f32[8,33,128]{2,1,0:T(8,128)}, u32[]{:S(2)}, u32[]{:S(2)}) async-start(f32[8,33,128]{2,1,0:T(8,128)} %broadcast_in_dim.15), calls=%async_computation.2 | async-start | bytes 327680 | tf_op jit(solution)/shard_map/all_to_all | solution.py:511
  115.0 6.0 %contract_down.1 = bf16[896,1024]{1,0:T(8,128)(2,1)} custom-call(s32[1]{0:T(128)} %constant.110.clone.1.at_ref, f32[1]{0:T(128)S(6)} %mul.75.scale_ref, bf16[256,896]{1,0:T(8,128)(2,1)} %get-tuple-element.92.hidden_ref.p0, bf16[256,896]{1,0:T(8,128)(2,1)} %copy-done.13, bf16[256,896]{1,0:T(8,128)(2,1)} %copy-done.12, ...), custom_call_target="tpu_custom_call" | custom-call | flops 1879048192 | bytes 3932160 | tf_op jit(solution)/shard_map/contract_down/pallas_call | solution.py:354
  121.0 2.6 %constant_dynamic-slice_fusion.1 = (bf16[448,1024]{1,0:T(8,128)(2,1)S(1)}, bf16[448,1024]{1,0:T(8,128)(2,1)}) fusion(bf16[896,1024]{1,0:T(8,128)(2,1)} %contract_down.1, s32[]{:T(128)S(6)} %select_n.102, s32[]{:T(128)S(6)} %select_n.101), kind=kLoop, calls=%fused_computation.51 | loop fusion | bytes 3670024 | tf_op jit(solution)/shard_map/dynamic_slice | solution.py:518
  123.6 2.4 %all-to-all-done.2 = f32[8,33,128]{2,1,0:T(8,128)} async-done(((f32[8,33,128]{2,1,0:T(8,128)}), f32[8,33,128]{2,1,0:T(8,128)}, u32[]{:S(2)}, u32[]{:S(2)}) %all-to-all-start.2) | async-done | bytes 135200 | tf_op jit(solution)/shard_map/all_to_all | solution.py:511
  127.1 1.5 collective-permute-start.17
  130.6 4.0 %contract_pair.4 = bf16[512,896]{1,0:T(8,128)(2,1)} custom-call(s32[1]{0:T(128)} %bitcast.14.at_ref, f32[1]{0:T(128)S(6)} %mul.86.scale_ref, bf16[256,896]{1,0:T(8,128)(2,1)} %get-tuple-element.96.gate_ref.p0, bf16[256,896]{1,0:T(8,128)(2,1)} %copy-done.8, bf16[256,896]{1,0:T(8,128)(2,1)} %copy-done.7, bf16[256,896]{1,0:T(8,128)(2,1)} %collective-permute-done.11.p3, ...), custom_call_target="tpu_custom_call" | custom-call | flops 939524096 | bytes 2883584 | tf_op jit(solution)/shard_map/contract_pair/pallas_call | solution.py:354
  134.6 1.5 slice_reduce_fusion
  136.2 4.4 %pack.1 = bf16[4,66,4096]{2,1,0:T(8,128)(2,1)} custom-call(bf16[128,4096]{1,0:T(8,128)(2,1)} %get-tuple-element.106.out_own, bf16[128,4096]{1,0:T(8,128)(2,1)} %collective-permute-done.13.out_got, bf16[128,4096]{1,0:T(8,128)(2,1)} %get-tuple-element.108.norm_own, bf16[128,4096]{1,0:T(8,128)(2,1)} %collective-permute-done.12.norm_got, f32[1,4096]{1,0:T(1,128)} %bitcast.83), custom_call_target="tpu_custom_call" | custom-call | flops 41942 | bytes 131072 | tf_op jit(solution)/shard_map/pack/pallas_call | solution.py:297
  140.6 1.5 collective-permute-done.17.p3
  142.1 7.1 %collective-permute-done.16.p2 = bf16[256,896]{1,0:T(8,128)(2,1)} collective-permute-done((bf16[256,896]{1,0:T(8,128)(2,1)S(1)}, bf16[256,896]{1,0:T(8,128)(2,1)}, u32[]{:S(2)}, u32[]{:S(2)}) %collective-permute-start.16) | collective-permute-done | bytes 458784 | tf_op jit(solution)/shard_map/ppermute | solution.py:424
  149.2 1.5 collective-permute-done.15.p1
  151.7 4.5 %all-to-all-start.3 = ((bf16[4,66,4096]{2,1,0:T(8,128)(2,1)}), bf16[4,66,4096]{2,1,0:T(8,128)(2,1)}, u32[]{:S(2)}, u32[]{:S(2)}) async-start(bf16[4,66,4096]{2,1,0:T(8,128)(2,1)} %pack.1), calls=%async_computation.3 | async-start | bytes 4718592 | tf_op jit(solution)/shard_map/all_to_all | solution.py:411
  156.3 4.1 %contract_pair.5 = bf16[512,896]{1,0:T(8,128)(2,1)} custom-call(s32[1]{0:T(128)} %bitcast.14.at_ref, f32[1]{0:T(128)S(6)} %mul.86.scale_ref, bf16[256,896]{1,0:T(8,128)(2,1)} %get-tuple-element.114.up_ref.p0, bf16[256,896]{1,0:T(8,128)(2,1)} %collective-permute-done.15.p1, bf16[256,896]{1,0:T(8,128)(2,1)} %collective-permute-done.16.p2, ...), custom_call_target="tpu_custom_call" | custom-call | flops 18790480 | bytes 57671 | tf_op jit(solution)/shard_map/contract_pair/pallas_call | solution.py:354
  161.4 4.0 %contract_pair.7.u0 = bf16[512,896]{1,0:T(8,128)(2,1)} custom-call(s32[1]{0:T(128)} %bitcast.16.at_ref, f32[1]{0:T(128)S(6)} %mul.86.scale_ref, bf16[256,896]{1,0:T(8,128)(2,1)} %get-tuple-element.114.up_ref.p0, bf16[256,896]{1,0:T(8,128)(2,1)} %collective-permute-done.15.p1, bf16[256,896]{1,0:T(8,128)(2,1)} %collective-permute-done.16.p2, ...), custom_call_target="tpu_custom_call" | custom-call | flops 18790480 | bytes 57671 | tf_op jit(solution)/shard_map/contract_pair/pallas_call | solution.py:354
  165.4 4.1 %contract_pair.6.g0 = bf16[512,896]{1,0:T(8,128)(2,1)} custom-call(s32[1]{0:T(128)} %bitcast.16.at_ref, f32[1]{0:T(128)S(6)} %mul.86.scale_ref, bf16[256,896]{1,0:T(8,128)(2,1)} %get-tuple-element.96.gate_ref.p0, bf16[256,896]{1,0:T(8,128)(2,1)} %copy-done.8, bf16[256,896]{1,0:T(8,128)(2,1)} %copy-done.7, bf16[256,896]{1,0:T(8,128)(2,1)} %collective-permute-done.11.p3, ...), custom_call_target="tpu_custom_call" | custom-call | flops 18790480 | bytes 57671 | tf_op jit(solution)/shard_map/contract_pair/pallas_call | solution.py:354
  169.5 4.7 %collective-permute-done.18.g1 = bf16[512,896]{1,0:T(8,128)(2,1)} collective-permute-done((bf16[512,896]{1,0:T(8,128)(2,1)}, bf16[512,896]{1,0:T(8,128)(2,1)}, u32[]{:S(2)}, u32[]{:S(2)}) %collective-permute-start.18) | collective-permute-done | bytes 917536 | tf_op jit(solution)/shard_map/ppermute | solution.py:540
  174.2 1.5 add_convert_fusion
  180.2 4.0 %collective-permute-done.22 = bf16[112,1024]{1,0:T(8,128)(2,1)S(1)} collective-permute-done((bf16[112,1024]{1,0:T(8,128)(2,1)S(1)}, bf16[112,1024]{1,0:T(8,128)(2,1)S(1)}, u32[]{:S(2)}, u32[]{:S(2)}) %collective-permute-start.22) | collective-permute-done | bytes 229408 | tf_op jit(solution)/shard_map/ppermute | solution.py:424
  184.1 2.4 %collective-permute-done.21 = bf16[112,1024]{1,0:T(8,128)(2,1)S(1)} collective-permute-done((bf16[112,1024]{1,0:T(8,128)(2,1)S(1)}, bf16[112,1024]{1,0:T(8,128)(2,1)S(1)}, u32[]{:S(2)}, u32[]{:S(2)}) %collective-permute-start.21) | collective-permute-done | bytes 229408 | tf_op jit(solution)/shard_map/ppermute | solution.py:424
  186.6 2.4 %collective-permute-done.20 = bf16[112,1024]{1,0:T(8,128)(2,1)S(1)} collective-permute-done((bf16[112,1024]{1,0:T(8,128)(2,1)S(1)}, bf16[112,1024]{1,0:T(8,128)(2,1)S(1)}, u32[]{:S(2)}, u32[]{:S(2)}) %collective-permute-start.20) | collective-permute-done | bytes 229408 | tf_op jit(solution)/shard_map/ppermute | solution.py:424
  191.5 1.6 reshape.153
  193.1 2.2 %convert_reduce_fusion = f32[66,4096]{1,0:T(8,128)S(1)} fusion(bf16[4,66,4096]{2,1,0:T(8,128)(2,1)} %all-to-all-done.3), kind=kLoop, calls=%fused_computation.1 | loop fusion | flops 1892352 | bytes 3244032 | tf_op jit(solution)/shard_map/reduce_sum | solution.py:566
  195.6 3.0 %collective-permute-start.23 = (bf16[34,4096]{1,0:T(8,128)(2,1)S(1)}, bf16[34,4096]{1,0:T(8,128)(2,1)S(1)}, u32[]{:S(2)}, u32[]{:S(2)}) collective-permute-start(bf16[34,4096]{1,0:T(8,128)(2,1)S(1)} %pad_maximum_fusion.1), channel_id=1, source_target_pairs={{0,8},{1,9},{2,10},{3,11},{4,12},{5,13},{6,14},{7,15},{8,0},{9,1},... | collective-permute-start | bytes 835592 | tf_op jit(solution)/shard_map/ppermute | solution.py:574
  198.5 4.9 %join.1 = bf16[512,2,896]{2,1,0:T(2,128)(2,1)} custom-call(bf16[512,896]{1,0:T(8,128)(2,1)} %contract_pair.6.g0, bf16[512,896]{1,0:T(8,128)(2,1)} %collective-permute-done.18.g1, bf16[512,896]{1,0:T(8,128)(2,1)} %contract_pair.7.u0, bf16[512,896]{1,0:T(8,128)(2,1)} %collective-permute-done.19.u1), custom_call_target="tpu_custom_call" | custom-call | flops 917504 | bytes 5505024 | tf_op jit(solution)/shard_map/join/pallas_call | solution.py:378
  203.5 2.4 %collective-permute-done.23 = bf16[34,4096]{1,0:T(8,128)(2,1)S(1)} collective-permute-done((bf16[34,4096]{1,0:T(8,128)(2,1)S(1)}, bf16[34,4096]{1,0:T(8,128)(2,1)S(1)}, u32[]{:S(2)}, u32[]{:S(2)}) %collective-permute-start.23) | collective-permute-done | bytes 278560 | tf_op jit(solution)/shard_map/ppermute | solution.py:574
  (107 shorter events, 22.4 us)
Async XLA Ops:
  3.2 8.7 %copy-start.11 = (bf16[16,4096]{1,0:T(8,128)(2,1)S(1)}, bf16[16,4096]{1,0:T(8,128)(2,1)}, u32[]{:S(2)}) copy-start(bf16[16,4096]{1,0:T(8,128)(2,1)} %param.13) | copy-start | bytes 393220
  3.2 36.7 %all-to-all-start = ((bf16[8,2,16,4096]{3,2,1,0:T(8,128)(2,1)}), bf16[8,2,16,4096]{3,2,1,0:T(8,128)(2,1)S(1)}, u32[]{:S(2)}, u32[]{:S(2)}) async-start(bf16[8,2,16,4096]{3,2,1,0:T(8,128)(2,1)} %broadcast_in_dim.12), calls=%async_computation | async-start | bytes 4194304 | tf_op jit(solution)/shard_map/all_to_all | solution.py:407
  11.9 16.1 %copy-start.4 = (bf16[16,4096]{1,0:T(8,128)(2,1)S(1)}, bf16[16,4096]{1,0:T(8,128)(2,1)}, u32[]{:S(2)}) copy-start(bf16[16,4096]{1,0:T(8,128)(2,1)} %param.7) | copy-start | bytes 393220
  11.9 17.0 %copy-start.14 = (f32[4096]{0:T(1024)S(1)}, f32[4096]{0:T(1024)}, u32[]{:S(2)}) copy-start(f32[4096]{0:T(1024)} %param.10) | copy-start | bytes 49156
  31.2 6.5 %collective-permute-start.2 = (bf16[32,1024]{1,0:T(8,128)(2,1)S(1)}, bf16[32,1024]{1,0:T(8,128)(2,1)S(1)}, u32[]{:S(2)}, u32[]{:S(2)}) collective-permute-start(bf16[32,1024]{1,0:T(8,128)(2,1)S(1)} %bitcast.85), channel_id=1, source_target_pairs={{0,32},{16,48},{32,0},{48,16},{64,96},{80,112},{96,64},{112,80},{1... | collective-permute-start | bytes 196616 | tf_op jit(solution)/shard_map/ppermute | solution.py:424
  34.3 5.5 %collective-permute-start = (bf16[32,1024]{1,0:T(8,128)(2,1)S(1)}, bf16[32,1024]{1,0:T(8,128)(2,1)S(1)}, u32[]{:S(2)}, u32[]{:S(2)}) collective-permute-start(bf16[32,1024]{1,0:T(8,128)(2,1)S(1)} %bitcast.86), channel_id=1, source_target_pairs={{0,16},{16,32},{32,48},{48,0},{64,80},{80,96},{96,112},{112,64},{1... | collective-permute-start | bytes 196616 | tf_op jit(solution)/shard_map/ppermute | solution.py:424
  35.0 4.9 %collective-permute-start.1 = (bf16[32,1024]{1,0:T(8,128)(2,1)S(1)}, bf16[32,1024]{1,0:T(8,128)(2,1)S(1)}, u32[]{:S(2)}, u32[]{:S(2)}) collective-permute-start(bf16[32,1024]{1,0:T(8,128)(2,1)S(1)} %bitcast.87), channel_id=1, source_target_pairs={{0,48},{16,0},{32,16},{48,32},{64,112},{80,64},{96,80},{112,96},{1... | collective-permute-start | bytes 196616 | tf_op jit(solution)/shard_map/ppermute | solution.py:424
  39.9 1.3 copy-start
  41.2 4.2 %collective-permute-start.3 = (bf16[8,2,16,4096]{3,2,1,0:T(8,128)(2,1)S(1)}, bf16[8,2,16,4096]{3,2,1,0:T(8,128)(2,1)S(1)}, u32[]{:S(2)}, u32[]{:S(2)}) collective-permute-start(bf16[8,2,16,4096]{3,2,1,0:T(8,128)(2,1)S(1)} %all-to-all-done.own_ref), channel_id=1, source_target_pairs={{0,1},{1,0},{2,3},{3,2},{4,5},{5,4},{6,7},{7,6},{8,9},{9,8},{10,11... | collective-permute-start | bytes 6291464 | tf_op jit(solution)/shard_map/ppermute | solution.py:419
  45.4 1.4 copy-start.1
  60.4 7.3 %copy-start.10 = (bf16[256,896]{1,0:T(8,128)(2,1)S(1)}, bf16[256,896]{1,0:T(8,128)(2,1)}, u32[]{:S(2)}) copy-start(bf16[256,896]{1,0:T(8,128)(2,1)} %get-tuple-element.92.hidden_ref.p0) | copy-start | bytes 1376260
  60.4 10.7 %copy-start.17 = (f32[32,128]{1,0:T(8,128)S(1)}, f32[32,128]{1,0:T(8,128)}, u32[]{:S(2)}) copy-start(f32[32,128]{1,0:T(8,128)} %get-tuple-element.84) | copy-start | bytes 49156
  60.4 48.4 %all-to-all-start.1 = ((bf16[8,128,1024]{2,1,0:T(8,128)(2,1)}), bf16[8,128,1024]{2,1,0:T(8,128)(2,1)}, u32[]{:S(2)}, u32[]{:S(2)}) async-start(bf16[8,128,1024]{2,1,0:T(8,128)(2,1)} %broadcast_in_dim.17), calls=%async_computation.1 | async-start | bytes 4194304 | tf_op jit(solution)/shard_map/all_to_all | solution.py:407
  67.7 13.2 %collective-permute-start.5 = (bf16[256,896]{1,0:T(8,128)(2,1)S(1)}, bf16[256,896]{1,0:T(8,128)(2,1)S(1)}, u32[]{:S(2)}, u32[]{:S(2)}) collective-permute-start(bf16[256,896]{1,0:T(8,128)(2,1)S(1)} %copy-done.10), channel_id=1, source_target_pairs={{0,48},{16,0},{32,16},{48,32},{64,112},{80,64},{96,80},{112,96},{1... | collective-permute-start | bytes 1376264 | tf_op jit(solution)/shard_map/ppermute | solution.py:424
  71.1 13.2 %collective-permute-start.4 = (bf16[256,896]{1,0:T(8,128)(2,1)S(1)}, bf16[256,896]{1,0:T(8,128)(2,1)S(1)}, u32[]{:S(2)}, u32[]{:S(2)}) collective-permute-start(bf16[256,896]{1,0:T(8,128)(2,1)S(1)} %copy-done.10), channel_id=1, source_target_pairs={{0,16},{16,32},{32,48},{48,0},{64,80},{80,96},{96,112},{112,64},{1... | collective-permute-start | bytes 1376264 | tf_op jit(solution)/shard_map/ppermute | solution.py:424
  80.9 3.4 %copy-start.12 = (bf16[256,896]{1,0:T(8,128)(2,1)}, bf16[256,896]{1,0:T(8,128)(2,1)S(1)}, u32[]{:S(2)}) copy-start(bf16[256,896]{1,0:T(8,128)(2,1)S(1)} %collective-permute-done.5.p2) | copy-start | bytes 1376260
  84.3 0.8 copy-start.13
  85.1 21.6 %collective-permute-start.8 = (bf16[256,896]{1,0:T(8,128)(2,1)}, bf16[256,896]{1,0:T(8,128)(2,1)S(1)}, u32[]{:S(2)}, u32[]{:S(2)}) collective-permute-start(bf16[256,896]{1,0:T(8,128)(2,1)} %get-tuple-element.96.gate_ref.p0), channel_id=1, source_target_pairs={{0,48},{16,0},{32,16},{48,32},{64,112},{80,64},{96,80},{112,96},{1... | collective-permute-start | bytes 1376264 | tf_op jit(solution)/shard_map/ppermute | solution.py:424
  85.5 22.5 %collective-permute-start.7 = (bf16[256,896]{1,0:T(8,128)(2,1)}, bf16[256,896]{1,0:T(8,128)(2,1)S(1)}, u32[]{:S(2)}, u32[]{:S(2)}) collective-permute-start(bf16[256,896]{1,0:T(8,128)(2,1)} %get-tuple-element.96.gate_ref.p0), channel_id=1, source_target_pairs={{0,16},{16,32},{32,48},{48,0},{64,80},{80,96},{96,112},{112,64},{1... | collective-permute-start | bytes 1376264 | tf_op jit(solution)/shard_map/ppermute | solution.py:424
  87.1 19.6 %collective-permute-start.6 = (bf16[256,896]{1,0:T(8,128)(2,1)S(1)}, bf16[256,896]{1,0:T(8,128)(2,1)}, u32[]{:S(2)}, u32[]{:S(2)}) collective-permute-start(bf16[256,896]{1,0:T(8,128)(2,1)S(1)} %copy-done.10), channel_id=1, source_target_pairs={{0,32},{16,48},{32,0},{48,16},{64,96},{80,112},{96,64},{112,80},{1... | collective-permute-start | bytes 1376264 | tf_op jit(solution)/shard_map/ppermute | solution.py:424
  96.9 7.9 %collective-permute-start.9 = (f32[1,4096]{1,0:T(1,128)}, f32[1,4096]{1,0:T(1,128)S(1)}, u32[]{:S(2)}, u32[]{:S(2)}) collective-permute-start(f32[1,4096]{1,0:T(1,128)} %get-tuple-element.83), channel_id=1, source_target_pairs={{0,1},{1,0},{2,3},{3,2},{4,5},{5,4},{6,7},{7,6},{8,9},{9,8},{10,11... | collective-permute-start | bytes 49160 | tf_op jit(solution)/shard_map/ppermute | solution.py:419
  98.4 6.4 %copy-start.16 = (f32[1,4096]{1,0:T(1,128)S(1)}, f32[1,4096]{1,0:T(1,128)}, u32[]{:S(2)}) copy-start(f32[1,4096]{1,0:T(1,128)} %get-tuple-element.83) | copy-start | bytes 49156
  98.4 10.8 %copy-start.2 = (bf16[256,896]{1,0:T(8,128)(2,1)S(1)}, bf16[256,896]{1,0:T(8,128)(2,1)}, u32[]{:S(2)}) copy-start(bf16[256,896]{1,0:T(8,128)(2,1)} %get-tuple-element.96.gate_ref.p0) | copy-start | bytes 1376260
  106.7 8.3 %copy-start.7 = (bf16[256,896]{1,0:T(8,128)(2,1)}, bf16[256,896]{1,0:T(8,128)(2,1)S(1)}, u32[]{:S(2)}) copy-start(bf16[256,896]{1,0:T(8,128)(2,1)S(1)} %collective-permute-done.8.p2) | copy-start | bytes 1376260
  108.0 7.0 %copy-start.8 = (bf16[256,896]{1,0:T(8,128)(2,1)}, bf16[256,896]{1,0:T(8,128)(2,1)S(1)}, u32[]{:S(2)}) copy-start(bf16[256,896]{1,0:T(8,128)(2,1)S(1)} %collective-permute-done.7.p1) | copy-start | bytes 1376260
  108.7 6.3 %collective-permute-start.10 = (bf16[8,4,2,16,1024]{4,3,2,1,0:T(8,128)(2,1)}, bf16[8,4,2,16,1024]{4,3,2,1,0:T(8,128)(2,1)}, u32[]{:S(2)}, u32[]{:S(2)}) collective-permute-start(bf16[8,4,2,16,1024]{4,3,2,1,0:T(8,128)(2,1)} %bitcast.13.own_ref), channel_id=1, source_target_pairs={{0,1},{1,0},{2,3},{3,2},{4,5},{5,4},{6,7},{7,6},{8,9},{9,8},{10,11... | collective-permute-start | bytes 6291464 | tf_op jit(solution)/shard_map/ppermute | solution.py:419
  108.7 17.3 %collective-permute-start.12 = (bf16[128,4096]{1,0:T(8,128)(2,1)}, bf16[128,4096]{1,0:T(8,128)(2,1)}, u32[]{:S(2)}, u32[]{:S(2)}) collective-permute-start(bf16[128,4096]{1,0:T(8,128)(2,1)} %get-tuple-element.97), channel_id=1, source_target_pairs={{0,1},{1,0},{2,3},{3,2},{4,5},{5,4},{6,7},{7,6},{8,9},{9,8},{10,11... | collective-permute-start | bytes 3145736 | tf_op jit(solution)/shard_map/ppermute | solution.py:419
  109.2 16.8 %collective-permute-start.13 = (bf16[128,4096]{1,0:T(8,128)(2,1)}, bf16[128,4096]{1,0:T(8,128)(2,1)}, u32[]{:S(2)}, u32[]{:S(2)}) collective-permute-start(bf16[128,4096]{1,0:T(8,128)(2,1)} %get-tuple-element.98), channel_id=1, source_target_pairs={{0,1},{1,0},{2,3},{3,2},{4,5},{5,4},{6,7},{7,6},{8,9},{9,8},{10,11... | collective-permute-start | bytes 3145736 | tf_op jit(solution)/shard_map/ppermute | solution.py:419
  109.2 16.8 %collective-permute-start.11 = (bf16[256,896]{1,0:T(8,128)(2,1)S(1)}, bf16[256,896]{1,0:T(8,128)(2,1)}, u32[]{:S(2)}, u32[]{:S(2)}) collective-permute-start(bf16[256,896]{1,0:T(8,128)(2,1)S(1)} %copy-done.2), channel_id=1, source_target_pairs={{0,32},{16,48},{32,0},{48,16},{64,96},{80,112},{96,64},{112,80},{1... | collective-permute-start | bytes 1376264 | tf_op jit(solution)/shard_map/ppermute | solution.py:424
  111.0 15.0 %all-to-all-start.2 = ((f32[8,33,128]{2,1,0:T(8,128)}), f32[8,33,128]{2,1,0:T(8,128)}, u32[]{:S(2)}, u32[]{:S(2)}) async-start(f32[8,33,128]{2,1,0:T(8,128)} %broadcast_in_dim.15), calls=%async_computation.2 | async-start | bytes 327680 | tf_op jit(solution)/shard_map/all_to_all | solution.py:511
  121.0 6.1 %copy-start.3 = (bf16[256,896]{1,0:T(8,128)(2,1)S(1)}, bf16[256,896]{1,0:T(8,128)(2,1)}, u32[]{:S(2)}) copy-start(bf16[256,896]{1,0:T(8,128)(2,1)} %get-tuple-element.114.up_ref.p0) | copy-start | bytes 1376260
  126.0 24.7 %collective-permute-start.14 = (bf16[448,1024]{1,0:T(8,128)(2,1)}, bf16[448,1024]{1,0:T(8,128)(2,1)}, u32[]{:S(2)}, u32[]{:S(2)}) collective-permute-start(bf16[448,1024]{1,0:T(8,128)(2,1)} %get-tuple-element.101), channel_id=1, source_target_pairs={{0,64},{16,80},{32,96},{48,112},{64,0},{80,16},{96,32},{112,48},{1... | collective-permute-start | bytes 2752520 | tf_op jit(solution)/shard_map/ppermute | solution.py:529
  127.1 15.0 %collective-permute-start.17 = (bf16[256,896]{1,0:T(8,128)(2,1)S(1)}, bf16[256,896]{1,0:T(8,128)(2,1)S(1)}, u32[]{:S(2)}, u32[]{:S(2)}) collective-permute-start(bf16[256,896]{1,0:T(8,128)(2,1)S(1)} %copy-done.3), channel_id=1, source_target_pairs={{0,32},{16,48},{32,0},{48,16},{64,96},{80,112},{96,64},{112,80},{1... | collective-permute-start | bytes 1376264 | tf_op jit(solution)/shard_map/ppermute | solution.py:424
  128.6 20.6 %collective-permute-start.16 = (bf16[256,896]{1,0:T(8,128)(2,1)S(1)}, bf16[256,896]{1,0:T(8,128)(2,1)}, u32[]{:S(2)}, u32[]{:S(2)}) collective-permute-start(bf16[256,896]{1,0:T(8,128)(2,1)S(1)} %copy-done.3), channel_id=1, source_target_pairs={{0,48},{16,0},{32,16},{48,32},{64,112},{80,64},{96,80},{112,96},{1... | collective-permute-start | bytes 1376264 | tf_op jit(solution)/shard_map/ppermute | solution.py:424
  129.8 20.9 %collective-permute-start.15 = (bf16[256,896]{1,0:T(8,128)(2,1)S(1)}, bf16[256,896]{1,0:T(8,128)(2,1)}, u32[]{:S(2)}, u32[]{:S(2)}) collective-permute-start(bf16[256,896]{1,0:T(8,128)(2,1)S(1)} %copy-done.3), channel_id=1, source_target_pairs={{0,16},{16,32},{32,48},{48,0},{64,80},{80,96},{96,112},{112,64},{1... | collective-permute-start | bytes 1376264 | tf_op jit(solution)/shard_map/ppermute | solution.py:424
  142.1 9.7 %copy-start.9 = (bf16[256,896]{1,0:T(8,128)(2,1)}, bf16[256,896]{1,0:T(8,128)(2,1)S(1)}, u32[]{:S(2)}) copy-start(bf16[256,896]{1,0:T(8,128)(2,1)S(1)} %collective-permute-done.17.p3) | copy-start | bytes 1376260
  150.7 23.5 %collective-permute-start.18 = (bf16[512,896]{1,0:T(8,128)(2,1)}, bf16[512,896]{1,0:T(8,128)(2,1)}, u32[]{:S(2)}, u32[]{:S(2)}) collective-permute-start(bf16[512,896]{1,0:T(8,128)(2,1)} %contract_pair.4), channel_id=1, source_target_pairs={{0,64},{16,80},{32,96},{48,112},{64,0},{80,16},{96,32},{112,48},{1... | collective-permute-start | bytes 2752520 | tf_op jit(solution)/shard_map/ppermute | solution.py:540
  151.7 41.4 %all-to-all-start.3 = ((bf16[4,66,4096]{2,1,0:T(8,128)(2,1)}), bf16[4,66,4096]{2,1,0:T(8,128)(2,1)}, u32[]{:S(2)}, u32[]{:S(2)}) async-start(bf16[4,66,4096]{2,1,0:T(8,128)(2,1)} %pack.1), calls=%async_computation.3 | async-start | bytes 4718592 | tf_op jit(solution)/shard_map/all_to_all | solution.py:411
  160.3 32.8 %collective-permute-start.19 = (bf16[512,896]{1,0:T(8,128)(2,1)}, bf16[512,896]{1,0:T(8,128)(2,1)}, u32[]{:S(2)}, u32[]{:S(2)}) collective-permute-start(bf16[512,896]{1,0:T(8,128)(2,1)} %contract_pair.5), channel_id=1, source_target_pairs={{0,64},{16,80},{32,96},{48,112},{64,0},{80,16},{96,32},{112,48},{1... | collective-permute-start | bytes 2752520 | tf_op jit(solution)/shard_map/ppermute | solution.py:542
  175.9 8.3 %collective-permute-start.22 = (bf16[112,1024]{1,0:T(8,128)(2,1)S(1)}, bf16[112,1024]{1,0:T(8,128)(2,1)S(1)}, u32[]{:S(2)}, u32[]{:S(2)}) collective-permute-start(bf16[112,1024]{1,0:T(8,128)(2,1)S(1)} %get-tuple-element.140), channel_id=1, source_target_pairs={{0,48},{16,0},{32,16},{48,32},{64,112},{80,64},{96,80},{112,96},{1... | collective-permute-start | bytes 688136 | tf_op jit(solution)/shard_map/ppermute | solution.py:424
  177.0 9.5 %collective-permute-start.21 = (bf16[112,1024]{1,0:T(8,128)(2,1)S(1)}, bf16[112,1024]{1,0:T(8,128)(2,1)S(1)}, u32[]{:S(2)}, u32[]{:S(2)}) collective-permute-start(bf16[112,1024]{1,0:T(8,128)(2,1)S(1)} %get-tuple-element.141), channel_id=1, source_target_pairs={{0,32},{16,48},{32,0},{48,16},{64,96},{80,112},{96,64},{112,80},{1... | collective-permute-start | bytes 688136 | tf_op jit(solution)/shard_map/ppermute | solution.py:424
  177.9 11.0 %collective-permute-start.20 = (bf16[112,1024]{1,0:T(8,128)(2,1)S(1)}, bf16[112,1024]{1,0:T(8,128)(2,1)S(1)}, u32[]{:S(2)}, u32[]{:S(2)}) collective-permute-start(bf16[112,1024]{1,0:T(8,128)(2,1)S(1)} %get-tuple-element.142), channel_id=1, source_target_pairs={{0,16},{16,32},{32,48},{48,0},{64,80},{80,96},{96,112},{112,64},{1... | collective-permute-start | bytes 688136 | tf_op jit(solution)/shard_map/ppermute | solution.py:424
  195.6 10.3 %collective-permute-start.23 = (bf16[34,4096]{1,0:T(8,128)(2,1)S(1)}, bf16[34,4096]{1,0:T(8,128)(2,1)S(1)}, u32[]{:S(2)}, u32[]{:S(2)}) collective-permute-start(bf16[34,4096]{1,0:T(8,128)(2,1)S(1)} %pad_maximum_fusion.1), channel_id=1, source_target_pairs={{0,8},{1,9},{2,10},{3,11},{4,12},{5,13},{6,14},{7,15},{8,0},{9,1},... | collective-permute-start | bytes 835592 | tf_op jit(solution)/shard_map/ppermute | solution.py:574
  203.5 3.3 %copy-start.15 = (f32[4096]{0:T(1024)S(1)}, f32[4096]{0:T(1024)}, u32[]{:S(2)}) copy-start(f32[4096]{0:T(1024)} %param.10) | copy-start | bytes 49156
  205.9 0.7 copy-start.5
  206.6 1.8 copy-start.6

commit v4 on v3

--- a/solution.py
+++ b/solution.py
@@ -367,6 +367,26 @@
     )(first.reshape(1).astype(jnp.int32), scale, *pieces, own, other)
 
 
+def add_kernel(kept_ref, got_ref, out_ref):
+    total = kept_ref[...].astype(F32) + got_ref[...].astype(F32)
+    out_ref[...] = total.astype(BF16)
+
+
+def add(kept, got, depth=512):
+    rows, columns = kept.shape
+    strip = pl.BlockSpec((rows, depth), lambda i: (0, i))
+    return pl.pallas_call(
+        add_kernel,
+        grid=(columns // depth,),
+        in_specs=[strip, strip],
+        out_specs=strip,
+        out_shape=jax.ShapeDtypeStruct((rows, columns), BF16),
+        compiler_params=options(62),
+        cost_estimate=cost(rows * columns // 50, rows * columns // 8),
+        name="add",
+    )(kept, got)
+
+
 def join_kernel(g0, g1, u0, u1, out_ref):
     out_ref[:, 0, :] = (g0[...].astype(F32) + g1[...].astype(F32)).astype(BF16)
     out_ref[:, 1, :] = (u0[...].astype(F32) + u1[...].astype(F32)).astype(BF16)
@@ -541,12 +561,11 @@
     up_sent = pair_part(up_all, 1 - z_lo, 50, late_scale)
     up_got = lax.ppermute(up_sent, "dp", ZPAIR)
     gate_kept = pair_part(gate_all, z_lo, 50, after(late_scale, up_sent))
-    up_kept = pair_part(up_all, z_lo, 50, after(late_scale, up_sent))
-    gate_got, gate_kept, up_kept, kept_down, got_down = together(
-        gate_got, gate_kept, up_kept, kept_down, got_down
-    )
-
-    sum_down = (kept_down.astype(F32) + got_down.astype(F32)).astype(BF16)
+    sum_down = add(kept_down, after(got_down, gate_kept))
+    gate_got, gate_kept, sum_down, late_scale = together(
+        gate_got, gate_kept, sum_down, late_scale
+    )
+
     sum_down = sum_down.reshape(4, hand // 4, 2 * span)
 
     def own_part(step):
@@ -555,6 +574,8 @@
     turned = jnp.stack(
         [own_part(0), send_x(own_part(1), 1), send_x(own_part(2), 2), send_x(own_part(-1), -1)]
     )
+    up_kept = pair_part(up_all, z_lo, scale=after(late_scale, sum_down))
+    turned, up_kept = together(turned, up_kept)
     turned = turned[(x - jnp.arange(4)) % 4]
     grad_down = (
         turned.reshape(4, hand // 4, 2, span).transpose(1, 2, 0, 3).reshape(hand // 4, features)

time: 210 us -> 210 us (level)
  waiting for transfers between devices: 41.2 us -> 37.9 us
  Pallas kernels: 67.8 us -> 70.2 us
    ppermute x15, waiting for transfers between devices: 27.5 us -> 18.3 us  [send_x(): return lax.ppermute(block, 'dp', ring)]
    ppermute x1, waiting for transfers between devices: 4.73 us -> 10.9 us  [shards(): gate_got = lax.ppermute(gate_sent, 'dp', ZPAIR)]
    pallas_call x0 -> x1, Pallas kernels: none -> 2.39 us  [add(): pl.pallas_call(add_kernel, grid=(columns // depth,), in_specs=[strip, str...]
  transfers between devices with their start and end apart: 28 -> 28, of which waited for: 14 -> 12; matrix products, arithmetic and copies ran while one was open for 16% -> 16% of each run, Pallas kernels for 27% -> 28%
where the time goes in v4:
time: 210 us; the launch traced here: 208 us
  Pallas kernels  70.2 us (33%)
  starting transfers between devices  51.6 us (25%)
  waiting for transfers between devices  37.9 us (18%)
  local copies, waits for them, and re-layouts  37.3 us (18%)
  other arithmetic  9.09 us (4%)
  between operations  2.49 us (1%)
    pallas_call x5, Pallas kernels, contract(): pl.pallas_call(kernel, grid_spec=pltpu.PrefetchScalarGridSpec(num_scalar_...  22.3 us
    ppermute x15, starting transfers between devices, send_x(): return lax.ppermute(block, 'dp', ring)  20.9 us
    unnamed x40, local copies, waits for them, and re-layouts  19.6 us
    ppermute x15, waiting for transfers between devices, send_x(): return lax.ppermute(block, 'dp', ring)  18.3 us
    all_to_all x2, starting transfers between devices, exchange(): lax.all_to_all(parts, 'tensor', 0, 0, tiled=True, axis_index_groups=RINGS)  15.3 us
    pallas_call x1, Pallas kernels, forward(): pl.pallas_call(functools.partial(forward_kernel, steps), grid=(steps,), i...  12 us
    ppermute x1, waiting for transfers between devices, shards(): gate_got = lax.ppermute(gate_sent, 'dp', ZPAIR)  10.9 us
    pallas_call x1, Pallas kernels, normed_shares(): pl.pallas_call(normed_kernel, grid=(features // depth,), in_specs=[whole(...  9.79 us
  transfers between devices with their start and end apart: 28, of which 12 were waited for; matrix products, arithmetic and copies ran while one was open for 16% of the time, Pallas kernels for 28%

profile of v4, /device:TPU:0, one launch (start us, length us, event | category | flops | bytes accessed | tf_op | source)
XLA Modules:
  0.0 208.4 jit_solution(7100653897382524265)
XLA Ops:
  1.6 1.6 broadcast_in_dim.12
  3.2 8.0 %all-to-all-start = ((bf16[8,2,16,4096]{3,2,1,0:T(8,128)(2,1)}), bf16[8,2,16,4096]{3,2,1,0:T(8,128)(2,1)S(1)}, u32[]{:S(2)}, u32[]{:S(2)}) async-start(bf16[8,2,16,4096]{3,2,1,0:T(8,128)(2,1)} %broadcast_in_dim.12), calls=%async_computation | async-start | bytes 4194304 | tf_op jit(solution)/shard_map/all_to_all | solution.py:427
  11.9 16.1 %copy.41 = bf16[512,8,2,896]{3,1,2,0:T(8,128)(2,1)} copy(bf16[512,8,2,896]{3,2,1,0:T(2,128)(2,1)} %bitcast.66) | data formatting | bytes 29360128
  29.3 1.8 dynamic-slice_reduce_fusion.3
  31.2 3.1 %collective-permute-start.2 = (bf16[32,1024]{1,0:T(8,128)(2,1)S(1)}, bf16[32,1024]{1,0:T(8,128)(2,1)S(1)}, u32[]{:S(2)}, u32[]{:S(2)}) collective-permute-start(bf16[32,1024]{1,0:T(8,128)(2,1)S(1)} %bitcast.85), channel_id=1, source_target_pairs={{0,32},{16,48},{32,0},{48,16},{64,96},{80,112},{96,64},{112,80},{1... | collective-permute-start | bytes 196616 | tf_op jit(solution)/shard_map/ppermute | solution.py:444
  35.0 2.7 %collective-permute-start.1 = (bf16[32,1024]{1,0:T(8,128)(2,1)S(1)}, bf16[32,1024]{1,0:T(8,128)(2,1)S(1)}, u32[]{:S(2)}, u32[]{:S(2)}) collective-permute-start(bf16[32,1024]{1,0:T(8,128)(2,1)S(1)} %bitcast.87), channel_id=1, source_target_pairs={{0,48},{16,0},{32,16},{48,32},{64,112},{80,64},{96,80},{112,96},{1... | collective-permute-start | bytes 196616 | tf_op jit(solution)/shard_map/ppermute | solution.py:444
  37.7 2.1 %collective-permute-done = bf16[32,1024]{1,0:T(8,128)(2,1)S(1)} collective-permute-done((bf16[32,1024]{1,0:T(8,128)(2,1)S(1)}, bf16[32,1024]{1,0:T(8,128)(2,1)S(1)}, u32[]{:S(2)}, u32[]{:S(2)}) %collective-permute-start) | collective-permute-done | bytes 65568 | tf_op jit(solution)/shard_map/ppermute | solution.py:444
  39.9 1.3 copy-done
  41.2 4.2 %collective-permute-done.3.other_ref = bf16[8,2,16,4096]{3,2,1,0:T(8,128)(2,1)S(1)} collective-permute-done((bf16[8,2,16,4096]{3,2,1,0:T(8,128)(2,1)S(1)}, bf16[8,2,16,4096]{3,2,1,0:T(8,128)(2,1)S(1)}, u32[]{:S(2)}, u32[]{:S(2)}) %collective-permute-start.3) | collective-permute-done | bytes 2097184 | tf_op jit(solution)/shard_map/ppermute | solution.py:439
  45.4 1.4 copy-done.1
  46.7 12.0 %forward.1 = (bf16[256,896]{1,0:T(8,128)(2,1)}, f32[256,896]{1,0:T(8,128)}, f32[256,896]{1,0:T(8,128)}, f32[256,128]{1,0:T(8,128)}, f32[32,128]{1,0:T(8,128)}) custom-call(f32[1]{0:T(128)S(6)} %copy.47.act_ref, bf16[8,2,16,4096]{3,2,1,0:T(8,128)(2,1)} %copy-done, bf16[8,2,16,4096]{3,2,1,0:T(8,128)(2,1)} %copy-done.1, f32[1,4096]{1,0:T(1,128)} %bitcast.76, ...), custom_call_target="tpu_custom_call" | custom-call | flops 3758096384 | bytes 14680064 | tf_op jit(solution)/shard_map/forward/pallas_call | solution.py:112
  58.8 1.6 broadcast_in_dim.17
  60.4 7.3 %all-to-all-start.1 = ((bf16[8,128,1024]{2,1,0:T(8,128)(2,1)}), bf16[8,128,1024]{2,1,0:T(8,128)(2,1)}, u32[]{:S(2)}, u32[]{:S(2)}) async-start(bf16[8,128,1024]{2,1,0:T(8,128)(2,1)} %broadcast_in_dim.17), calls=%async_computation.1 | async-start | bytes 4194304 | tf_op jit(solution)/shard_map/all_to_all | solution.py:427
  67.7 3.4 %collective-permute-start.5 = (bf16[256,896]{1,0:T(8,128)(2,1)S(1)}, bf16[256,896]{1,0:T(8,128)(2,1)S(1)}, u32[]{:S(2)}, u32[]{:S(2)}) collective-permute-start(bf16[256,896]{1,0:T(8,128)(2,1)S(1)} %copy-done.10), channel_id=1, source_target_pairs={{0,48},{16,0},{32,16},{48,32},{64,112},{80,64},{96,80},{112,96},{1... | collective-permute-start | bytes 1376264 | tf_op jit(solution)/shard_map/ppermute | solution.py:444
  71.7 8.0 %backward.1 = (bf16[256,896]{1,0:T(8,128)(2,1)}, bf16[256,896]{1,0:T(8,128)(2,1)}, f32[8,128]{1,0:T(8,128)}) custom-call(f32[1]{0:T(128)S(6)} %copy.48.history_ref, bf16[8,2,16,4096]{3,2,1,0:T(8,128)(2,1)} %copy-done, bf16[8,2,16,4096]{3,2,1,0:T(8,128)(2,1)} %copy-done.1, bf16[896,4096]{1,0:T(8,128)(2,1)} %down_ref.3, ...), custom_call_target="tpu_custom_call" | custom-call | flops 1879048192 | bytes 7340032 | tf_op jit(solution)/shard_map/backward/pallas_call | solution.py:184
  79.7 1.3 reduce_max.28
  80.9 3.3 %collective-permute-done.4.p1 = bf16[256,896]{1,0:T(8,128)(2,1)S(1)} collective-permute-done((bf16[256,896]{1,0:T(8,128)(2,1)S(1)}, bf16[256,896]{1,0:T(8,128)(2,1)S(1)}, u32[]{:S(2)}, u32[]{:S(2)}) %collective-permute-start.4) | collective-permute-done | bytes 458784 | tf_op jit(solution)/shard_map/ppermute | solution.py:444
  85.4 1.7 collective-permute-start.7
  87.1 9.8 %normed_shares.1 = (bf16[128,4096]{1,0:T(8,128)(2,1)}, bf16[128,4096]{1,0:T(8,128)(2,1)}, f32[1,4096]{1,0:T(1,128)}) custom-call(bf16[256,896]{1,0:T(8,128)(2,1)} %get-tuple-element.99.gate_ref.p0, bf16[256,896]{1,0:T(8,128)(2,1)} %get-tuple-element.117.up_ref.p0, bf16[4096,1792]{1,0:T(8,128)(2,1)} %bitcast.64, bf16[4096,1792]{1,0:T(8,128)(2,1)} %bitcast.65, ...), custom_call_target="tpu_custom_call" | custom-call | flops 3758096384 | bytes 14680064 | tf_op jit(solution)/shard_map/normed_shares/pallas_call | solution.py:253
  98.5 6.4 %out_shares.1 = (bf16[128,4096]{1,0:T(8,128)(2,1)}, bf16[128,4096]{1,0:T(8,128)(2,1)}) custom-call(bf16[256,896]{1,0:T(8,128)(2,1)} %get-tuple-element.95.hidden_ref.p0, bf16[896,4096]{1,0:T(8,128)(2,1)} %down_ref.3), custom_call_target="tpu_custom_call" | custom-call | flops 37580960 | bytes 146800 | tf_op jit(solution)/shard_map/out_shares/pallas_call | solution.py:219
  104.9 1.6 collective-permute-done.6.p3
  106.6 1.3 collective-permute-done.7.p1
  109.1 1.8 collective-permute-start.11
  110.9 4.0 %all-to-all-start.2 = ((f32[8,33,128]{2,1,0:T(8,128)}), f32[8,33,128]{2,1,0:T(8,128)}, u32[]{:S(2)}, u32[]{:S(2)}) async-start(f32[8,33,128]{2,1,0:T(8,128)} %broadcast_in_dim.15), calls=%async_computation.2 | async-start | bytes 327680 | tf_op jit(solution)/shard_map/all_to_all | solution.py:531
  115.0 6.0 %contract_down.1 = bf16[896,1024]{1,0:T(8,128)(2,1)} custom-call(s32[1]{0:T(128)} %constant.110.clone.1.at_ref, f32[1]{0:T(128)S(6)} %mul.75.scale_ref, bf16[256,896]{1,0:T(8,128)(2,1)} %get-tuple-element.95.hidden_ref.p0, bf16[256,896]{1,0:T(8,128)(2,1)} %copy-done.13, bf16[256,896]{1,0:T(8,128)(2,1)} %copy-done.12, ...), custom_call_target="tpu_custom_call" | custom-call | flops 1879048192 | bytes 3932160 | tf_op jit(solution)/shard_map/contract_down/pallas_call | solution.py:354
  120.9 2.9 %constant_dynamic-slice_fusion.1 = (bf16[448,1024]{1,0:T(8,128)(2,1)}, bf16[448,1024]{1,0:T(8,128)(2,1)}) fusion(bf16[896,1024]{1,0:T(8,128)(2,1)} %contract_down.1, s32[]{:T(128)S(6)} %select_n.102, s32[]{:T(128)S(6)} %select_n.101), kind=kLoop, calls=%fused_computation.50 | loop fusion | bytes 3670024 | tf_op jit(solution)/shard_map/dynamic_slice | solution.py:538
  123.9 2.0 all-to-all-done.2
  127.0 1.9 collective-permute-start.17
  130.9 4.0 %contract_pair.4 = bf16[512,896]{1,0:T(8,128)(2,1)} custom-call(s32[1]{0:T(128)} %bitcast.14.at_ref, f32[1]{0:T(128)S(6)} %mul.86.scale_ref, bf16[256,896]{1,0:T(8,128)(2,1)} %get-tuple-element.99.gate_ref.p0, bf16[256,896]{1,0:T(8,128)(2,1)} %copy-done.6, bf16[256,896]{1,0:T(8,128)(2,1)} %copy-done.5, bf16[256,896]{1,0:T(8,128)(2,1)} %collective-permute-done.11.p3, ...), custom_call_target="tpu_custom_call" | custom-call | flops 939524096 | bytes 2883584 | tf_op jit(solution)/shard_map/contract_pair/pallas_call | solution.py:354
  134.9 1.5 slice_reduce_fusion
  136.4 4.4 %pack.1 = bf16[4,66,4096]{2,1,0:T(8,128)(2,1)} custom-call(bf16[128,4096]{1,0:T(8,128)(2,1)} %get-tuple-element.109.out_own, bf16[128,4096]{1,0:T(8,128)(2,1)} %collective-permute-done.13.out_got, bf16[128,4096]{1,0:T(8,128)(2,1)} %get-tuple-element.111.norm_own, bf16[128,4096]{1,0:T(8,128)(2,1)} %collective-permute-done.12.norm_got, f32[1,4096]{1,0:T(1,128)} %bitcast.83), custom_call_target="tpu_custom_call" | custom-call | flops 41942 | bytes 131072 | tf_op jit(solution)/shard_map/pack/pallas_call | solution.py:297
  140.9 4.5 %all-to-all-start.3 = ((bf16[4,66,4096]{2,1,0:T(8,128)(2,1)}), bf16[4,66,4096]{2,1,0:T(8,128)(2,1)}, u32[]{:S(2)}, u32[]{:S(2)}) async-start(bf16[4,66,4096]{2,1,0:T(8,128)(2,1)} %pack.1), calls=%async_computation.3 | async-start | bytes 4718592 | tf_op jit(solution)/shard_map/all_to_all | solution.py:431
  145.4 4.0 %collective-permute-done.16.p2 = bf16[256,896]{1,0:T(8,128)(2,1)S(1)} collective-permute-done((bf16[256,896]{1,0:T(8,128)(2,1)S(1)}, bf16[256,896]{1,0:T(8,128)(2,1)S(1)}, u32[]{:S(2)}, u32[]{:S(2)}) %collective-permute-start.16) | collective-permute-done | bytes 458784 | tf_op jit(solution)/shard_map/ppermute | solution.py:444
  151.5 4.1 %contract_pair.5 = bf16[512,896]{1,0:T(8,128)(2,1)} custom-call(s32[1]{0:T(128)} %bitcast.14.at_ref, f32[1]{0:T(128)S(6)} %mul.86.scale_ref, bf16[256,896]{1,0:T(8,128)(2,1)} %get-tuple-element.117.up_ref.p0, bf16[256,896]{1,0:T(8,128)(2,1)} %copy-done.9, bf16[256,896]{1,0:T(8,128)(2,1)} %copy-done.8, bf16[256,896]{1,0:T(8,128)(2,1)} %copy-done.7, ...), custom_call_target="tpu_custom_call" | custom-call | flops 18790480 | bytes 57671 | tf_op jit(solution)/shard_map/contract_pair/pallas_call | solution.py:354
  156.6 4.1 %contract_pair.6.g0 = bf16[512,896]{1,0:T(8,128)(2,1)} custom-call(s32[1]{0:T(128)} %bitcast.16.at_ref, f32[1]{0:T(128)S(6)} %mul.86.scale_ref, bf16[256,896]{1,0:T(8,128)(2,1)} %get-tuple-element.99.gate_ref.p0, bf16[256,896]{1,0:T(8,128)(2,1)} %copy-done.6, bf16[256,896]{1,0:T(8,128)(2,1)} %copy-done.5, bf16[256,896]{1,0:T(8,128)(2,1)} %collective-permute-done.11.p3, ...), custom_call_target="tpu_custom_call" | custom-call | flops 18790480 | bytes 57671 | tf_op jit(solution)/shard_map/contract_pair/pallas_call | solution.py:354
  160.7 2.4 %add.176 = bf16[448,1024]{1,0:T(8,128)(2,1)} custom-call(bf16[448,1024]{1,0:T(8,128)(2,1)} %get-tuple-element.143.kept_ref, bf16[448,1024]{1,0:T(8,128)(2,1)} %collective-permute-done.14.got_ref), custom_call_target="tpu_custom_call" | custom-call | flops 18350 | bytes 57344 | tf_op jit(solution)/shard_map/add/pallas_call | solution.py:378
  163.1 10.9 %collective-permute-done.18.g1 = bf16[512,896]{1,0:T(8,128)(2,1)} collective-permute-done((bf16[512,896]{1,0:T(8,128)(2,1)}, bf16[512,896]{1,0:T(8,128)(2,1)}, u32[]{:S(2)}, u32[]{:S(2)}) %collective-permute-start.18) | collective-permute-done | bytes 917536 | tf_op jit(solution)/shard_map/ppermute | solution.py:560
  174.0 1.3 constant_dynamic-slice_fusion
  175.4 1.6 collective-permute-start.22
  180.0 4.1 %contract_pair.7.u0 = bf16[512,896]{1,0:T(8,128)(2,1)} custom-call(s32[1]{0:T(128)} %bitcast.16.at_ref, f32[1]{0:T(128)S(6)} %mul.86.scale_ref, bf16[256,896]{1,0:T(8,128)(2,1)} %get-tuple-element.117.up_ref.p0, bf16[256,896]{1,0:T(8,128)(2,1)} %copy-done.9, bf16[256,896]{1,0:T(8,128)(2,1)} %copy-done.8, bf16[256,896]{1,0:T(8,128)(2,1)} %copy-done.7, ...), custom_call_target="tpu_custom_call" | custom-call | flops 939524096 | bytes 2883584 | tf_op jit(solution)/shard_map/contract_pair/pallas_call | solution.py:354
  184.1 2.5 %collective-permute-done.21 = bf16[112,1024]{1,0:T(8,128)(2,1)S(1)} collective-permute-done((bf16[112,1024]{1,0:T(8,128)(2,1)S(1)}, bf16[112,1024]{1,0:T(8,128)(2,1)S(1)}, u32[]{:S(2)}, u32[]{:S(2)}) %collective-permute-start.21) | collective-permute-done | bytes 229408 | tf_op jit(solution)/shard_map/ppermute | solution.py:444
  186.5 2.4 %collective-permute-done.20 = bf16[112,1024]{1,0:T(8,128)(2,1)S(1)} collective-permute-done((bf16[112,1024]{1,0:T(8,128)(2,1)S(1)}, bf16[112,1024]{1,0:T(8,128)(2,1)S(1)}, u32[]{:S(2)}, u32[]{:S(2)}) %collective-permute-start.20) | collective-permute-done | bytes 229408 | tf_op jit(solution)/shard_map/ppermute | solution.py:444
  190.3 1.2 copy.46
  191.5 1.6 reshape.153
  193.1 2.2 %convert_reduce_fusion = f32[66,4096]{1,0:T(8,128)S(1)} fusion(bf16[4,66,4096]{2,1,0:T(8,128)(2,1)} %all-to-all-done.3), kind=kLoop, calls=%fused_computation.1 | loop fusion | flops 1892352 | bytes 3244032 | tf_op jit(solution)/shard_map/reduce_sum | solution.py:587
  195.5 3.0 %collective-permute-start.23 = (bf16[34,4096]{1,0:T(8,128)(2,1)S(1)}, bf16[34,4096]{1,0:T(8,128)(2,1)S(1)}, u32[]{:S(2)}, u32[]{:S(2)}) collective-permute-start(bf16[34,4096]{1,0:T(8,128)(2,1)S(1)} %pad_maximum_fusion.1), channel_id=1, source_target_pairs={{0,8},{1,9},{2,10},{3,11},{4,12},{5,13},{6,14},{7,15},{8,0},{9,1},... | collective-permute-start | bytes 835592 | tf_op jit(solution)/shard_map/ppermute | solution.py:595
  198.5 4.9 %join.1 = bf16[512,2,896]{2,1,0:T(2,128)(2,1)} custom-call(bf16[512,896]{1,0:T(8,128)(2,1)} %contract_pair.6.g0, bf16[512,896]{1,0:T(8,128)(2,1)} %collective-permute-done.18.g1, bf16[512,896]{1,0:T(8,128)(2,1)} %contract_pair.7.u0, bf16[512,896]{1,0:T(8,128)(2,1)} %collective-permute-done.19.u1), custom_call_target="tpu_custom_call" | custom-call | flops 917504 | bytes 5505024 | tf_op jit(solution)/shard_map/join/pallas_call | solution.py:398
  203.5 2.4 %collective-permute-done.23 = bf16[34,4096]{1,0:T(8,128)(2,1)S(1)} collective-permute-done((bf16[34,4096]{1,0:T(8,128)(2,1)S(1)}, bf16[34,4096]{1,0:T(8,128)(2,1)S(1)}, u32[]{:S(2)}, u32[]{:S(2)}) %collective-permute-start.23) | collective-permute-done | bytes 278560 | tf_op jit(solution)/shard_map/ppermute | solution.py:595
  (107 shorter events, 20.3 us)
Async XLA Ops:
  3.2 8.7 %copy-start.11 = (bf16[16,4096]{1,0:T(8,128)(2,1)S(1)}, bf16[16,4096]{1,0:T(8,128)(2,1)}, u32[]{:S(2)}) copy-start(bf16[16,4096]{1,0:T(8,128)(2,1)} %param.13) | copy-start | bytes 393220
  3.2 36.7 %all-to-all-start = ((bf16[8,2,16,4096]{3,2,1,0:T(8,128)(2,1)}), bf16[8,2,16,4096]{3,2,1,0:T(8,128)(2,1)S(1)}, u32[]{:S(2)}, u32[]{:S(2)}) async-start(bf16[8,2,16,4096]{3,2,1,0:T(8,128)(2,1)} %broadcast_in_dim.12), calls=%async_computation | async-start | bytes 4194304 | tf_op jit(solution)/shard_map/all_to_all | solution.py:427
  11.9 16.1 %copy-start.4 = (bf16[16,4096]{1,0:T(8,128)(2,1)S(1)}, bf16[16,4096]{1,0:T(8,128)(2,1)}, u32[]{:S(2)}) copy-start(bf16[16,4096]{1,0:T(8,128)(2,1)} %param.7) | copy-start | bytes 393220
  11.9 17.0 %copy-start.14 = (f32[4096]{0:T(1024)S(1)}, f32[4096]{0:T(1024)}, u32[]{:S(2)}) copy-start(f32[4096]{0:T(1024)} %param.10) | copy-start | bytes 49156
  31.2 6.5 %collective-permute-start.2 = (bf16[32,1024]{1,0:T(8,128)(2,1)S(1)}, bf16[32,1024]{1,0:T(8,128)(2,1)S(1)}, u32[]{:S(2)}, u32[]{:S(2)}) collective-permute-start(bf16[32,1024]{1,0:T(8,128)(2,1)S(1)} %bitcast.85), channel_id=1, source_target_pairs={{0,32},{16,48},{32,0},{48,16},{64,96},{80,112},{96,64},{112,80},{1... | collective-permute-start | bytes 196616 | tf_op jit(solution)/shard_map/ppermute | solution.py:444
  34.3 5.5 %collective-permute-start = (bf16[32,1024]{1,0:T(8,128)(2,1)S(1)}, bf16[32,1024]{1,0:T(8,128)(2,1)S(1)}, u32[]{:S(2)}, u32[]{:S(2)}) collective-permute-start(bf16[32,1024]{1,0:T(8,128)(2,1)S(1)} %bitcast.86), channel_id=1, source_target_pairs={{0,16},{16,32},{32,48},{48,0},{64,80},{80,96},{96,112},{112,64},{1... | collective-permute-start | bytes 196616 | tf_op jit(solution)/shard_map/ppermute | solution.py:444
  35.0 4.9 %collective-permute-start.1 = (bf16[32,1024]{1,0:T(8,128)(2,1)S(1)}, bf16[32,1024]{1,0:T(8,128)(2,1)S(1)}, u32[]{:S(2)}, u32[]{:S(2)}) collective-permute-start(bf16[32,1024]{1,0:T(8,128)(2,1)S(1)} %bitcast.87), channel_id=1, source_target_pairs={{0,48},{16,0},{32,16},{48,32},{64,112},{80,64},{96,80},{112,96},{1... | collective-permute-start | bytes 196616 | tf_op jit(solution)/shard_map/ppermute | solution.py:444
  39.9 1.3 copy-start
  41.2 4.2 %collective-permute-start.3 = (bf16[8,2,16,4096]{3,2,1,0:T(8,128)(2,1)S(1)}, bf16[8,2,16,4096]{3,2,1,0:T(8,128)(2,1)S(1)}, u32[]{:S(2)}, u32[]{:S(2)}) collective-permute-start(bf16[8,2,16,4096]{3,2,1,0:T(8,128)(2,1)S(1)} %all-to-all-done.own_ref), channel_id=1, source_target_pairs={{0,1},{1,0},{2,3},{3,2},{4,5},{5,4},{6,7},{7,6},{8,9},{9,8},{10,11... | collective-permute-start | bytes 6291464 | tf_op jit(solution)/shard_map/ppermute | solution.py:439
  45.4 1.4 copy-start.1
  60.4 7.3 %copy-start.10 = (bf16[256,896]{1,0:T(8,128)(2,1)S(1)}, bf16[256,896]{1,0:T(8,128)(2,1)}, u32[]{:S(2)}) copy-start(bf16[256,896]{1,0:T(8,128)(2,1)} %get-tuple-element.95.hidden_ref.p0) | copy-start | bytes 1376260
  60.4 10.7 %copy-start.17 = (f32[32,128]{1,0:T(8,128)S(1)}, f32[32,128]{1,0:T(8,128)}, u32[]{:S(2)}) copy-start(f32[32,128]{1,0:T(8,128)} %get-tuple-element.87) | copy-start | bytes 49156
  60.4 48.2 %all-to-all-start.1 = ((bf16[8,128,1024]{2,1,0:T(8,128)(2,1)}), bf16[8,128,1024]{2,1,0:T(8,128)(2,1)}, u32[]{:S(2)}, u32[]{:S(2)}) async-start(bf16[8,128,1024]{2,1,0:T(8,128)(2,1)} %broadcast_in_dim.17), calls=%async_computation.1 | async-start | bytes 4194304 | tf_op jit(solution)/shard_map/all_to_all | solution.py:427
  67.7 13.2 %collective-permute-start.5 = (bf16[256,896]{1,0:T(8,128)(2,1)S(1)}, bf16[256,896]{1,0:T(8,128)(2,1)S(1)}, u32[]{:S(2)}, u32[]{:S(2)}) collective-permute-start(bf16[256,896]{1,0:T(8,128)(2,1)S(1)} %copy-done.10), channel_id=1, source_target_pairs={{0,48},{16,0},{32,16},{48,32},{64,112},{80,64},{96,80},{112,96},{1... | collective-permute-start | bytes 1376264 | tf_op jit(solution)/shard_map/ppermute | solution.py:444
  71.1 13.2 %collective-permute-start.4 = (bf16[256,896]{1,0:T(8,128)(2,1)S(1)}, bf16[256,896]{1,0:T(8,128)(2,1)S(1)}, u32[]{:S(2)}, u32[]{:S(2)}) collective-permute-start(bf16[256,896]{1,0:T(8,128)(2,1)S(1)} %copy-done.10), channel_id=1, source_target_pairs={{0,16},{16,32},{32,48},{48,0},{64,80},{80,96},{96,112},{112,64},{1... | collective-permute-start | bytes 1376264 | tf_op jit(solution)/shard_map/ppermute | solution.py:444
  80.9 15.9 %copy-start.12 = (bf16[256,896]{1,0:T(8,128)(2,1)}, bf16[256,896]{1,0:T(8,128)(2,1)S(1)}, u32[]{:S(2)}) copy-start(bf16[256,896]{1,0:T(8,128)(2,1)S(1)} %collective-permute-done.5.p2) | copy-start | bytes 1376260
  84.3 0.8 copy-start.13
  85.1 21.5 %collective-permute-start.8 = (bf16[256,896]{1,0:T(8,128)(2,1)}, bf16[256,896]{1,0:T(8,128)(2,1)S(1)}, u32[]{:S(2)}, u32[]{:S(2)}) collective-permute-start(bf16[256,896]{1,0:T(8,128)(2,1)} %get-tuple-element.99.gate_ref.p0), channel_id=1, source_target_pairs={{0,48},{16,0},{32,16},{48,32},{64,112},{80,64},{96,80},{112,96},{1... | collective-permute-start | bytes 1376264 | tf_op jit(solution)/shard_map/ppermute | solution.py:444
  85.4 22.5 %collective-permute-start.7 = (bf16[256,896]{1,0:T(8,128)(2,1)}, bf16[256,896]{1,0:T(8,128)(2,1)S(1)}, u32[]{:S(2)}, u32[]{:S(2)}) collective-permute-start(bf16[256,896]{1,0:T(8,128)(2,1)} %get-tuple-element.99.gate_ref.p0), channel_id=1, source_target_pairs={{0,16},{16,32},{32,48},{48,0},{64,80},{80,96},{96,112},{112,64},{1... | collective-permute-start | bytes 1376264 | tf_op jit(solution)/shard_map/ppermute | solution.py:444
  87.1 19.5 %collective-permute-start.6 = (bf16[256,896]{1,0:T(8,128)(2,1)S(1)}, bf16[256,896]{1,0:T(8,128)(2,1)}, u32[]{:S(2)}, u32[]{:S(2)}) collective-permute-start(bf16[256,896]{1,0:T(8,128)(2,1)S(1)} %copy-done.10), channel_id=1, source_target_pairs={{0,32},{16,48},{32,0},{48,16},{64,96},{80,112},{96,64},{112,80},{1... | collective-permute-start | bytes 1376264 | tf_op jit(solution)/shard_map/ppermute | solution.py:444
  96.9 8.0 %collective-permute-start.9 = (f32[1,4096]{1,0:T(1,128)}, f32[1,4096]{1,0:T(1,128)S(1)}, u32[]{:S(2)}, u32[]{:S(2)}) collective-permute-start(f32[1,4096]{1,0:T(1,128)} %get-tuple-element.86), channel_id=1, source_target_pairs={{0,1},{1,0},{2,3},{3,2},{4,5},{5,4},{6,7},{7,6},{8,9},{9,8},{10,11... | collective-permute-start | bytes 49160 | tf_op jit(solution)/shard_map/ppermute | solution.py:439
  98.5 6.4 %copy-start.16 = (f32[1,4096]{1,0:T(1,128)S(1)}, f32[1,4096]{1,0:T(1,128)}, u32[]{:S(2)}) copy-start(f32[1,4096]{1,0:T(1,128)} %get-tuple-element.86) | copy-start | bytes 49156
  98.5 10.6 %copy-start.3 = (bf16[256,896]{1,0:T(8,128)(2,1)S(1)}, bf16[256,896]{1,0:T(8,128)(2,1)}, u32[]{:S(2)}) copy-start(bf16[256,896]{1,0:T(8,128)(2,1)} %get-tuple-element.99.gate_ref.p0) | copy-start | bytes 1376260
  106.6 14.3 %copy-start.5 = (bf16[256,896]{1,0:T(8,128)(2,1)}, bf16[256,896]{1,0:T(8,128)(2,1)S(1)}, u32[]{:S(2)}) copy-start(bf16[256,896]{1,0:T(8,128)(2,1)S(1)} %collective-permute-done.8.p2) | copy-start | bytes 1376260
  107.9 13.1 %copy-start.6 = (bf16[256,896]{1,0:T(8,128)(2,1)}, bf16[256,896]{1,0:T(8,128)(2,1)S(1)}, u32[]{:S(2)}) copy-start(bf16[256,896]{1,0:T(8,128)(2,1)S(1)} %collective-permute-done.7.p1) | copy-start | bytes 1376260
  108.6 6.4 %collective-permute-start.10 = (bf16[8,4,2,16,1024]{4,3,2,1,0:T(8,128)(2,1)}, bf16[8,4,2,16,1024]{4,3,2,1,0:T(8,128)(2,1)}, u32[]{:S(2)}, u32[]{:S(2)}) collective-permute-start(bf16[8,4,2,16,1024]{4,3,2,1,0:T(8,128)(2,1)} %bitcast.13.own_ref), channel_id=1, source_target_pairs={{0,1},{1,0},{2,3},{3,2},{4,5},{5,4},{6,7},{7,6},{8,9},{9,8},{10,11... | collective-permute-start | bytes 6291464 | tf_op jit(solution)/shard_map/ppermute | solution.py:439
  108.6 17.3 %collective-permute-start.12 = (bf16[128,4096]{1,0:T(8,128)(2,1)}, bf16[128,4096]{1,0:T(8,128)(2,1)}, u32[]{:S(2)}, u32[]{:S(2)}) collective-permute-start(bf16[128,4096]{1,0:T(8,128)(2,1)} %get-tuple-element.100), channel_id=1, source_target_pairs={{0,1},{1,0},{2,3},{3,2},{4,5},{5,4},{6,7},{7,6},{8,9},{9,8},{10,11... | collective-permute-start | bytes 3145736 | tf_op jit(solution)/shard_map/ppermute | solution.py:439
  109.1 16.8 %collective-permute-start.13 = (bf16[128,4096]{1,0:T(8,128)(2,1)}, bf16[128,4096]{1,0:T(8,128)(2,1)}, u32[]{:S(2)}, u32[]{:S(2)}) collective-permute-start(bf16[128,4096]{1,0:T(8,128)(2,1)} %get-tuple-element.101), channel_id=1, source_target_pairs={{0,1},{1,0},{2,3},{3,2},{4,5},{5,4},{6,7},{7,6},{8,9},{9,8},{10,11... | collective-permute-start | bytes 3145736 | tf_op jit(solution)/shard_map/ppermute | solution.py:439
  109.1 16.8 %collective-permute-start.11 = (bf16[256,896]{1,0:T(8,128)(2,1)S(1)}, bf16[256,896]{1,0:T(8,128)(2,1)}, u32[]{:S(2)}, u32[]{:S(2)}) collective-permute-start(bf16[256,896]{1,0:T(8,128)(2,1)S(1)} %copy-done.3), channel_id=1, source_target_pairs={{0,32},{16,48},{32,0},{48,16},{64,96},{80,112},{96,64},{112,80},{1... | collective-permute-start | bytes 1376264 | tf_op jit(solution)/shard_map/ppermute | solution.py:444
  110.9 14.9 %all-to-all-start.2 = ((f32[8,33,128]{2,1,0:T(8,128)}), f32[8,33,128]{2,1,0:T(8,128)}, u32[]{:S(2)}, u32[]{:S(2)}) async-start(f32[8,33,128]{2,1,0:T(8,128)} %broadcast_in_dim.15), calls=%async_computation.2 | async-start | bytes 327680 | tf_op jit(solution)/shard_map/all_to_all | solution.py:531
  120.9 6.0 %copy-start.2 = (bf16[256,896]{1,0:T(8,128)(2,1)S(1)}, bf16[256,896]{1,0:T(8,128)(2,1)}, u32[]{:S(2)}) copy-start(bf16[256,896]{1,0:T(8,128)(2,1)} %get-tuple-element.117.up_ref.p0) | copy-start | bytes 1376260
  125.9 24.6 %collective-permute-start.14 = (bf16[448,1024]{1,0:T(8,128)(2,1)}, bf16[448,1024]{1,0:T(8,128)(2,1)}, u32[]{:S(2)}, u32[]{:S(2)}) collective-permute-start(bf16[448,1024]{1,0:T(8,128)(2,1)} %get-tuple-element.104), channel_id=1, source_target_pairs={{0,64},{16,80},{32,96},{48,112},{64,0},{80,16},{96,32},{112,48},{1... | collective-permute-start | bytes 2752520 | tf_op jit(solution)/shard_map/ppermute | solution.py:549
  127.0 18.4 %collective-permute-start.17 = (bf16[256,896]{1,0:T(8,128)(2,1)S(1)}, bf16[256,896]{1,0:T(8,128)(2,1)S(1)}, u32[]{:S(2)}, u32[]{:S(2)}) collective-permute-start(bf16[256,896]{1,0:T(8,128)(2,1)S(1)} %copy-done.2), channel_id=1, source_target_pairs={{0,32},{16,48},{32,0},{48,16},{64,96},{80,112},{96,64},{112,80},{1... | collective-permute-start | bytes 1376264 | tf_op jit(solution)/shard_map/ppermute | solution.py:444
  128.8 20.5 %collective-permute-start.16 = (bf16[256,896]{1,0:T(8,128)(2,1)S(1)}, bf16[256,896]{1,0:T(8,128)(2,1)S(1)}, u32[]{:S(2)}, u32[]{:S(2)}) collective-permute-start(bf16[256,896]{1,0:T(8,128)(2,1)S(1)} %copy-done.2), channel_id=1, source_target_pairs={{0,48},{16,0},{32,16},{48,32},{64,112},{80,64},{96,80},{112,96},{1... | collective-permute-start | bytes 1376264 | tf_op jit(solution)/shard_map/ppermute | solution.py:444
  130.0 20.5 %collective-permute-start.15 = (bf16[256,896]{1,0:T(8,128)(2,1)S(1)}, bf16[256,896]{1,0:T(8,128)(2,1)S(1)}, u32[]{:S(2)}, u32[]{:S(2)}) collective-permute-start(bf16[256,896]{1,0:T(8,128)(2,1)S(1)} %copy-done.2), channel_id=1, source_target_pairs={{0,16},{16,32},{32,48},{48,0},{64,80},{80,96},{96,112},{112,64},{1... | collective-permute-start | bytes 1376264 | tf_op jit(solution)/shard_map/ppermute | solution.py:444
  140.9 52.2 %all-to-all-start.3 = ((bf16[4,66,4096]{2,1,0:T(8,128)(2,1)}), bf16[4,66,4096]{2,1,0:T(8,128)(2,1)}, u32[]{:S(2)}, u32[]{:S(2)}) async-start(bf16[4,66,4096]{2,1,0:T(8,128)(2,1)} %pack.1), calls=%async_computation.3 | async-start | bytes 4718592 | tf_op jit(solution)/shard_map/all_to_all | solution.py:431
  145.4 6.1 %copy-start.7 = (bf16[256,896]{1,0:T(8,128)(2,1)}, bf16[256,896]{1,0:T(8,128)(2,1)S(1)}, u32[]{:S(2)}) copy-start(bf16[256,896]{1,0:T(8,128)(2,1)S(1)} %collective-permute-done.17.p3) | copy-start | bytes 1376260
  149.3 2.2 %copy-start.8 = (bf16[256,896]{1,0:T(8,128)(2,1)}, bf16[256,896]{1,0:T(8,128)(2,1)S(1)}, u32[]{:S(2)}) copy-start(bf16[256,896]{1,0:T(8,128)(2,1)S(1)} %collective-permute-done.16.p2) | copy-start | bytes 1376260
  150.5 1.0 copy-start.9
  150.5 23.5 %collective-permute-start.18 = (bf16[512,896]{1,0:T(8,128)(2,1)}, bf16[512,896]{1,0:T(8,128)(2,1)}, u32[]{:S(2)}, u32[]{:S(2)}) collective-permute-start(bf16[512,896]{1,0:T(8,128)(2,1)} %contract_pair.4), channel_id=1, source_target_pairs={{0,64},{16,80},{32,96},{48,112},{64,0},{80,16},{96,32},{112,48},{1... | collective-permute-start | bytes 2752520 | tf_op jit(solution)/shard_map/ppermute | solution.py:560
  155.6 37.5 %collective-permute-start.19 = (bf16[512,896]{1,0:T(8,128)(2,1)}, bf16[512,896]{1,0:T(8,128)(2,1)}, u32[]{:S(2)}, u32[]{:S(2)}) collective-permute-start(bf16[512,896]{1,0:T(8,128)(2,1)} %contract_pair.5), channel_id=1, source_target_pairs={{0,64},{16,80},{32,96},{48,112},{64,0},{80,16},{96,32},{112,48},{1... | collective-permute-start | bytes 2752520 | tf_op jit(solution)/shard_map/ppermute | solution.py:562
  175.4 8.7 %collective-permute-start.22 = (bf16[112,1024]{1,0:T(8,128)(2,1)S(1)}, bf16[112,1024]{1,0:T(8,128)(2,1)S(1)}, u32[]{:S(2)}, u32[]{:S(2)}) collective-permute-start(bf16[112,1024]{1,0:T(8,128)(2,1)S(1)} %get-tuple-element.146), channel_id=1, source_target_pairs={{0,48},{16,0},{32,16},{48,32},{64,112},{80,64},{96,80},{112,96},{1... | collective-permute-start | bytes 688136 | tf_op jit(solution)/shard_map/ppermute | solution.py:444
  177.0 9.5 %collective-permute-start.21 = (bf16[112,1024]{1,0:T(8,128)(2,1)S(1)}, bf16[112,1024]{1,0:T(8,128)(2,1)S(1)}, u32[]{:S(2)}, u32[]{:S(2)}) collective-permute-start(bf16[112,1024]{1,0:T(8,128)(2,1)S(1)} %get-tuple-element.147), channel_id=1, source_target_pairs={{0,32},{16,48},{32,0},{48,16},{64,96},{80,112},{96,64},{112,80},{1... | collective-permute-start | bytes 688136 | tf_op jit(solution)/shard_map/ppermute | solution.py:444
  177.8 11.0 %collective-permute-start.20 = (bf16[112,1024]{1,0:T(8,128)(2,1)S(1)}, bf16[112,1024]{1,0:T(8,128)(2,1)S(1)}, u32[]{:S(2)}, u32[]{:S(2)}) collective-permute-start(bf16[112,1024]{1,0:T(8,128)(2,1)S(1)} %get-tuple-element.148), channel_id=1, source_target_pairs={{0,16},{16,32},{32,48},{48,0},{64,80},{80,96},{96,112},{112,64},{1... | collective-permute-start | bytes 688136 | tf_op jit(solution)/shard_map/ppermute | solution.py:444
  195.5 10.4 %collective-permute-start.23 = (bf16[34,4096]{1,0:T(8,128)(2,1)S(1)}, bf16[34,4096]{1,0:T(8,128)(2,1)S(1)}, u32[]{:S(2)}, u32[]{:S(2)}) collective-permute-start(bf16[34,4096]{1,0:T(8,128)(2,1)S(1)} %pad_maximum_fusion.1), channel_id=1, source_target_pairs={{0,8},{1,9},{2,10},{3,11},{4,12},{5,13},{6,14},{7,15},{8,0},{9,1},... | collective-permute-start | bytes 835592 | tf_op jit(solution)/shard_map/ppermute | solution.py:595
  203.4 2.6 %copy-start.15 = (f32[4096]{0:T(1024)S(1)}, f32[4096]{0:T(1024)}, u32[]{:S(2)}) copy-start(f32[4096]{0:T(1024)} %param.10) | copy-start | bytes 49156
